TPU v7x, 256 devices: a whole 4x4x8 slice. The times are simulated.
256 devices in a mesh: dp: 16 (over x, z_lo), ctx: 16 (over z_hi, y, core).
Axes of the slice: x: 4, y: 4, z: 8 (z_hi: 2, z_lo: 4; z = z_hi * 4 + z_lo), core: 2. Of those that a mesh axis runs over, the one named last changes fastest.
Arguments:
- query_rows: bfloat16 [16, 2048, 2560], P('dp', 'ctx'), may hold values from -8 to 8
- key_rows: bfloat16 [16, 2048, 512], P('dp', 'ctx'), may hold values from -8 to 8
- value_rows: bfloat16 [16, 2048, 512], P('dp', 'ctx'), may hold values from -6 to 6
- out_grad: bfloat16 [16, 2048, 2560], P('dp', 'ctx'), may hold values from -6 to 6
- doc_ids: int32 [16, 2048], P('dp', 'ctx'), may hold values from 0 to 7, never falling along the last dimension, each value on 1 to 1024 neighbouring positions
Outputs:
- query_grad: bfloat16 [16, 2048, 2560], P('dp', 'ctx')
- key_grad: bfloat16 [16, 2048, 512], P('dp', 'ctx')
- value_grad: bfloat16 [16, 2048, 512], P('dp', 'ctx')
- bias_grad: float32 [2560], replicated
Inputs may be any that keep to these rules, and one draw needn't show every extreme that they name: `doc_ids`: each row numbers the 8 documents packed into one sequence in order, never falling; a document holds 1 to 1024 tokens and one holds exactly 1024.
All inputs are finite; a program needn't handle non-finite values.
Results may differ from a plain program's by a relative error of at most 0.03.
Values may be sent and summed in bfloat16 or wider, within the bound.
No kernel may reach another device: no remote copies, remote signals or barrier semaphores. Data moves between devices by JAX's collectives and lax.ppermute only.
A program may use at most 128 MiB of HBM per device.

v0:
```python
import math

import jax
import jax.numpy as jnp
from jax import lax
from jax.sharding import PartitionSpec as P

HD = 128
QH = 20
KVH = 4


floor_score = -1e30


def blockwise(step_fn, carried, slices):
    rows_in = slices[0].shape[0]
    block_rows = math.gcd(rows_in, 512)

    def advance(block_index, current_state):
        offset = block_index * block_rows
        window = tuple(
            (lax.dynamic_slice_in_dim(member, offset, block_rows, 0) for member in slices)
        )
        return step_fn(current_state, window, offset)

    return lax.fori_loop(0, rows_in // block_rows, advance, carried)


def body(query_rows, key_rows, value_rows, out_grad, doc_ids):
    local_rows = query_rows.shape[1]
    seq_rows = lax.axis_size("ctx") * local_rows
    group_size = QH // KVH
    head_cols = KVH * HD
    inv_root = HD ** (-0.5)
    query_heads = query_rows[0].reshape(local_rows, KVH, group_size, HD)
    grad_heads = out_grad[0].reshape(local_rows, KVH, group_size, HD)
    query_docs = doc_ids[0]
    own_index = lax.axis_index("ctx")
    query_places = own_index * local_rows + jnp.arange(local_rows, dtype=jnp.int32)

    def scores_of(key_slice, doc_slice, first_row):
        key_heads = key_slice.reshape(key_slice.shape[0], KVH, HD)
        scores = (
            jnp.einsum("ikgd,jkd->kgij", query_heads, key_heads, preferred_element_type=jnp.float32)
            * inv_root
        )
        key_places = first_row + jnp.arange(key_slice.shape[0], dtype=jnp.int32)
        allowed = (query_docs[:, None] == doc_slice[None, :]) & (
            key_places[None, :] <= query_places[:, None]
        )
        return (scores, allowed)

    def forward_step(carried, window, first_row):
        running_max, weight_sum, weighted = carried
        key_slice, value_slice, doc_slice = window
        scores, allowed = scores_of(key_slice, doc_slice, first_row)
        new_max = jnp.maximum(
            running_max, jnp.max(jnp.where(allowed, scores, floor_score), axis=-1)
        )
        factor = jnp.exp(running_max - new_max)
        weights = jnp.where(allowed, jnp.exp(scores - new_max[..., None]), 0.0)
        value_heads = value_slice.reshape(value_slice.shape[0], KVH, HD)
        weight_sum = weight_sum * factor + jnp.sum(weights, axis=-1)
        weighted = weighted * factor[..., None] + jnp.einsum(
            "kgij,jkd->kgid",
            weights.astype(jnp.bfloat16),
            value_heads,
            preferred_element_type=jnp.float32,
        )
        return (new_max, weight_sum, weighted)

    initial = (
        jnp.full((KVH, group_size, local_rows), floor_score, jnp.float32),
        jnp.zeros((KVH, group_size, local_rows), jnp.float32),
        jnp.zeros((KVH, group_size, local_rows, HD), jnp.float32),
    )
    pieces = (
        lax.all_gather(key_rows, "ctx", axis=1, tiled=True),
        lax.all_gather(value_rows, "ctx", axis=1, tiled=True),
        lax.all_gather(doc_ids, "ctx", axis=1, tiled=True),
    )
    forward = blockwise(forward_step, initial, (pieces[0][0], pieces[1][0], pieces[2][0]))
    running_max, weight_sum, weighted = forward
    log_norm = running_max + jnp.log(weight_sum)
    attended = (weighted / weight_sum[..., None]).astype(jnp.bfloat16)
    row_dots = jnp.einsum(
        "kgid,ikgd->kgi", attended, grad_heads, preferred_element_type=jnp.float32
    )

    def backward_step(carried, window, first_row):
        query_acc, key_acc = carried
        key_slice, value_slice, doc_slice = window
        slice_rows = key_slice.shape[0]
        scores, allowed = scores_of(key_slice, doc_slice, first_row)
        softmax = jnp.where(allowed, jnp.exp(scores - log_norm[..., None]), 0.0)
        key_heads = key_slice.reshape(slice_rows, KVH, HD)
        value_heads = value_slice.reshape(slice_rows, KVH, HD)
        value_part = jnp.einsum(
            "kgij,ikgd->jkd",
            softmax.astype(jnp.bfloat16),
            grad_heads,
            preferred_element_type=jnp.float32,
        )
        prob_grad = jnp.einsum(
            "ikgd,jkd->kgij", grad_heads, value_heads, preferred_element_type=jnp.float32
        )
        score_grad = (softmax * (prob_grad - row_dots[..., None])).astype(jnp.bfloat16)
        query_acc = (
            query_acc
            + jnp.einsum(
                "kgij,jkd->ikgd", score_grad, key_heads, preferred_element_type=jnp.float32
            )
            * inv_root
        )
        key_part = (
            jnp.einsum(
                "kgij,ikgd->jkd", score_grad, query_heads, preferred_element_type=jnp.float32
            )
            * inv_root
        )
        update = jnp.concatenate(
            [key_part.reshape(slice_rows, head_cols), value_part.reshape(slice_rows, head_cols)],
            axis=1,
        )
        current = lax.dynamic_slice_in_dim(key_acc, first_row, slice_rows, 0)
        key_acc = lax.dynamic_update_slice_in_dim(key_acc, current + update, first_row, 0)
        return (query_acc, key_acc)

    starting = (
        jnp.zeros((local_rows, KVH, group_size, HD), jnp.float32),
        jnp.zeros((seq_rows, 2 * head_cols), jnp.float32),
    )
    pieces = (
        lax.all_gather(key_rows, "ctx", axis=1, tiled=True),
        lax.all_gather(value_rows, "ctx", axis=1, tiled=True),
        lax.all_gather(doc_ids, "ctx", axis=1, tiled=True),
    )
    gradients = blockwise(backward_step, starting, (pieces[0][0], pieces[1][0], pieces[2][0]))
    query_acc, key_acc = gradients
    owned_rows = lax.psum_scatter(
        key_acc.astype(jnp.bfloat16), "ctx", scatter_dimension=0, tiled=True
    ).astype(jnp.float32)
    query_flat = query_acc.reshape(local_rows, QH * HD)
    bias_total = lax.psum(jnp.sum(query_flat, axis=0), ("dp", "ctx"))
    query_out = query_flat.astype(jnp.bfloat16)[None]
    key_out = owned_rows[:, :head_cols].astype(jnp.bfloat16)[None]
    value_out = owned_rows[:, head_cols:].astype(jnp.bfloat16)[None]
    return (query_out, key_out, value_out, bias_total)


def solution(mesh):
    in_specs = (
        P("dp", "ctx", None),
        P("dp", "ctx", None),
        P("dp", "ctx", None),
        P("dp", "ctx", None),
        P("dp", "ctx"),
    )
    out_specs = (P("dp", "ctx", None), P("dp", "ctx", None), P("dp", "ctx", None), P())
    return jax.shard_map(body, mesh=mesh, in_specs=in_specs, out_specs=out_specs, check_vma=False)
```

profile of v0, /device:TPU:6, one launch (start us, length us, event | category | flops | bytes accessed | tf_op | source)
XLA Modules:
  0.0 404.8 jit_solution(6876155699614866819)
XLA Ops:
  12.5 2.2 copy.35
  14.7 33.2 %all_gather.13 = s32[1,2048]{1,0:T(1,128)S(1)} all-gather(s32[1,128]{1,0:T(1,128)S(1)} %copy-done.8), channel_id=1, replica_groups=mesh['dp'=16,'ctx'=16] {'ctx'}, dimensions={1}, use_global_device_ids=true | all-gather | bytes 8704 | tf_op jit(solution)/shard_map/all_gather | solution.py:137
  47.9 29.3 %all-gather.3.cloned.1.call-done = bf16[1,2048,512]{1,2,0:T(8,128)(2,1)} async-done(((bf16[1,128,512]{1,2,0:T(8,128)(2,1)}), bf16[1,2048,512]{1,2,0:T(8,128)(2,1)}) %all-gather.3.cloned.1.call-update) | async-done | bytes 2097168 | tf_op jit(solution)/shard_map/all_gather | solution.py:135
  77.2 61.9 %all-gather.5.cloned.1.call-done = bf16[1,2048,512]{1,2,0:T(8,128)(2,1)} async-done(((bf16[1,128,512]{1,2,0:T(8,128)(2,1)}), bf16[1,2048,512]{1,2,0:T(8,128)(2,1)}) %all-gather.5.cloned.1.call-update) | async-done | bytes 2097168 | tf_op jit(solution)/shard_map/all_gather | solution.py:136
  139.0 44.0 %while.34 = (s32[]{:T(128)}, f32[4,5,128]{2,1,0:T(8,128)S(1)}, f32[4,5,128]{2,1,0:T(8,128)S(1)}, f32[4,5,128,128]{3,2,1,0:T(8,128)S(1)}, s32[1,128]{1,0:T(1,128)...) while((s32[]{:T(128)}, f32[4,5,128]{2,1,0:T(8,128)S(1)}, ...), condition=%wide.region_3.4_spmd.clone, body=%wide.region_0.3_spmd.clone.sunk | while | flops 686699648 | bytes 43560688 | solution.py:27
  140.6 3.3 fusion.79
  144.0 3.7 fusion.80
  148.0 2.0 fusion.82
  151.6 3.3 fusion.79
  155.0 3.7 fusion.80
  159.0 2.0 fusion.82
  162.6 3.3 fusion.79
  166.0 3.7 fusion.80
  170.0 2.0 fusion.82
  173.7 3.3 fusion.79
  177.0 3.7 fusion.80
  181.1 2.0 fusion.82
  185.2 4.3 %broadcast_in_dim.92.clone = f32[2048,1024]{1,0:T(8,128)} broadcast(f32[]{:T(128)} %constant.106.clone.1), dimensions={} | broadcast | bytes 8388612 | tf_op jit(solution)/shard_map/broadcast_in_dim | solution.py:132
  189.5 100.4 %while.35 = (s32[]{:T(128)}, f32[128,4,5,128]{0,3,2,1:T(8,128)}, f32[2048,1024]{1,0:T(8,128)}, bf16[2048,512]{0,1:T(8,128)(2,1)}, s32[1,128]{1,0:T(1,128)S(1)}, ...) while((s32[]{:T(128)}, f32[128,4,5,128]{0,3,2,1:T(8,128)}, ...), condition=%wide.region_5.6_spmd.clone, body=%wide.region_4.5_spmd.clone.sunk | while | flops 1693319808 | bytes 97757072 | solution.py:27
  196.0 3.2 constant_dynamic-slice_fusion.10
  199.2 3.0 copy.71
  202.1 3.6 fusion.96
  205.8 2.2 fusion.97
  208.5 1.9 copy.72
  210.3 3.2 constant_dynamic-update-slice_fusion.2
  218.4 3.0 fusion.95
  221.4 3.2 constant_dynamic-slice_fusion.10
  224.6 3.0 copy.71
  227.6 3.6 fusion.96
  231.2 2.2 fusion.97
  233.9 1.9 copy.72
  235.8 3.2 constant_dynamic-update-slice_fusion.2
  243.8 3.0 fusion.95
  246.8 3.2 constant_dynamic-slice_fusion.10
  250.0 3.0 copy.71
  253.0 3.6 fusion.96
  256.6 2.2 fusion.97
  261.2 3.2 constant_dynamic-update-slice_fusion.2
  269.2 3.0 fusion.95
  272.2 3.2 constant_dynamic-slice_fusion.10
  275.4 3.0 copy.71
  278.4 3.6 fusion.96
  282.1 2.2 fusion.97
  284.7 1.9 copy.72
  286.6 3.3 constant_dynamic-update-slice_fusion.2
  289.9 6.0 %convert_element_type.46 = bf16[2048,1024]{1,0:T(8,128)(2,1)} convert(f32[2048,1024]{1,0:T(8,128)} %get-tuple-element.379) | non-fusion elementwise | flops 2097152 | bytes 12582912 | tf_op jit(solution)/shard_map/convert_element_type | solution.py:142
  298.8 89.4 %psum.7 = f32[2560]{0:T(1024)} all-reduce(f32[2560]{0:T(1024)S(1)} %reduce_sum.25), channel_id=1, replica_groups=mesh['dp'=16,'ctx'=16] {'dp','ctx'}, use_global_device_ids=true, to_apply=%region_8.9 | all-reduce | flops 2560 | bytes 20480 | tf_op jit(solution)/shard_map/psum | solution.py:145
  388.2 8.4 %reduce-scatter.2.cloned.1.call-done = bf16[128,1024]{1,0:T(8,128)(2,1)} async-done(((bf16[2048,1024]{1,0:T(8,128)(2,1)}), bf16[128,1024]{1,0:T(8,128)(2,1)}) %reduce-scatter.2.cloned.1.call-update) | async-done | bytes 262160 | tf_op jit(solution)/shard_map/reduce_scatter | solution.py:141
  (148 shorter events, 43.9 us)
Async XLA Ops:
  7.2 7.5 %copy-start.8 = (s32[1,128]{1,0:T(1,128)S(1)}, s32[1,128]{1,0:T(1,128)}, u32[]{:S(2)}) copy-start(s32[1,128]{1,0:T(1,128)} %param.13) | copy-start | bytes 1540
  7.2 70.0 %all-gather.3.cloned.1.call-start = ((), (), s32[]{:S(2)}) async-start(), calls=%async_computation.1 | async-start | bytes 2228224 | tf_op jit(solution)/shard_map/all_gather | solution.py:135
  8.9 130.1 %all-gather.5.cloned.1.call-start = ((), (), s32[]{:S(2)}) async-start(), calls=%async_computation.2 | async-start | bytes 2228224 | tf_op jit(solution)/shard_map/all_gather | solution.py:136
  10.7 386.0 %reduce-scatter.2.cloned.1.call-start = ((), (), s32[]{:S(2)}) async-start(), calls=%async_computation.3 | async-start | bytes 4456448 | tf_op jit(solution)/shard_map/reduce_scatter | solution.py:141
  144.0 4.0 copy-start
  155.0 4.0 copy-start
  166.0 4.0 copy-start
  177.0 4.0 copy-start
  189.5 2.4 copy-start.3
  191.0 1.2 copy-start.6
  191.9 2.4 copy-start.2
  199.2 3.0 copy-start.7
  205.8 2.2 copy-start.1
  210.3 3.3 copy-start.4
  213.6 2.4 copy-start.3
  215.1 1.2 copy-start.6
  216.0 2.4 copy-start.2
  224.6 3.0 copy-start.7
  231.2 2.2 copy-start.1
  235.8 3.2 copy-start.4
  239.0 2.4 copy-start.3
  240.5 1.2 copy-start.6
  241.4 2.4 copy-start.2
  250.0 3.0 copy-start.7
  256.6 2.2 copy-start.1
  261.2 3.2 copy-start.4
  264.4 2.4 copy-start.3
  265.9 1.2 copy-start.6
  266.8 2.4 copy-start.2
  275.4 3.0 copy-start.7
  282.1 2.2 copy-start.1
  286.6 3.3 copy-start.4
  295.9 1.3 copy-start.5
Sparse Core Ops, SparseCore 0:
  11.1 65.9 all-gather.2
  80.3 58.6 all-gather.4
  296.0 100.5 reduce-scatter.1
where the time goes:
time: 406 us; the launch traced here: 405 us
  blocking collectives  123 us (30%)
  waiting for transfers between devices  99.6 us (25%)
  local copies, waits for them, and re-layouts  75.2 us (19%)
  matrix products  66 us (16%)
  other arithmetic  26.7 us (7%)
  between operations  13.8 us (3%)
    psum x1, blocking collectives, body(): bias_total = lax.psum(jnp.sum(query_flat, axis=0), ('dp', 'ctx'))  89.4 us
    all_gather x1, waiting for transfers between devices, body(): lax.all_gather(value_rows, 'ctx', axis=1, tiled=True)  61.9 us
    all_gather x1, blocking collectives, body(): lax.all_gather(doc_ids, 'ctx', axis=1, tiled=True)  33.2 us
    all_gather x1, waiting for transfers between devices, body(): lax.all_gather(key_rows, 'ctx', axis=1, tiled=True)  29.3 us
    dynamic_slice x8, local copies, waits for them, and re-layouts, backward_step(): current = lax.dynamic_slice_in_dim(key_acc, first_row, slice_rows, 0)  24.6 us
    dynamic_update_slice x8, local copies, waits for them, and re-layouts, backward_step(): lax.dynamic_update_slice_in_dim(key_acc, current + update, first_row, 0)  20.4 us
    dot_general x8, matrix products, scores_of(): jnp.einsum('ikgd,jkd->kgij', query_heads, key_heads, preferred_element_ty...  16.9 us
    reduce_sum x4, other arithmetic, forward_step(): weight_sum = weight_sum * factor + jnp.sum(weights, axis=-1)  14.8 us
  transfers between devices with their start and end apart: 3, of which 3 were waited for; matrix products, arithmetic and copies ran while one was open for 2% of the time, Pallas kernels for 0%

commit v1 on v0

v1 whole, which is shorter than its diff:
```python
import math

import jax
import jax.numpy as jnp
from jax import lax
from jax.experimental import pallas as pl
from jax.experimental.pallas import tpu as pltpu
from jax.sharding import PartitionSpec as P

HD = 128
QH = 20
KVH = 4
GROUP = QH // KVH
ROWS = 128
PAIR = 2 * ROWS
HALF_Q = QH // 2 * HD
HALF_KV = KVH // 2 * HD
LINE = ROWS + 16
WINDOW = 5
INV_ROOT = HD ** (-0.5)
LOG2E = math.log2(math.e)
MASKED = -1e30


def place():
    index = lax.axis_index("ctx")
    return index // 8, (index // 2) % 4, index % 2


def pairs(target):
    out = []
    for z in range(2):
        for y in range(4):
            for c in range(2):
                to = target(z, y, c)
                if to is not None:
                    out.append((z * 8 + y * 2 + c, to[0] * 8 + to[1] * 2 + to[2]))
    return out


SWAP = pairs(lambda z, y, c: (z, y, 1 - c))
UP = pairs(lambda z, y, c: (1, y, c) if z == 0 else None)
DOWN = pairs(lambda z, y, c: (0, y, c) if z == 1 else None)
DOWN_CROSS = pairs(lambda z, y, c: (0, y, 1 - c) if z == 1 else None)


def near_pairs(k):
    return pairs(lambda z, y, c: (z, y + k, c) if y + k < 4 else None)


def far_pairs(k):
    return pairs(lambda z, y, c: (1, y - k, c) if z == 1 and y >= k else None)


def back_pairs(p):
    return pairs(
        lambda z, y, c: (z, (y + p) % 4, c) if z == 1 or y + p >= 4 else None
    )


def pack_kernel(q_ref, g_ref, k_ref, v_ref, ids_ref, send_ref, keep_ref, qg_ref):
    _, _, core = place()
    ids = jnp.broadcast_to(ids_ref[...].astype(jnp.float32), (16, ROWS)).astype(jnp.bfloat16)
    for ref, side in ((keep_ref, core), (send_ref, 1 - core)):
        columns = pl.ds(pl.multiple_of(side * HALF_KV, HALF_KV), HALF_KV)
        ref[0:ROWS, 0:HALF_KV] = k_ref[0, :, columns]
        ref[0:ROWS, HALF_KV:] = v_ref[0, :, columns]
        ref[ROWS:, 0:ROWS] = ids
        ref[ROWS:, ROWS:] = jnp.zeros((16, 2 * HALF_KV - ROWS), jnp.bfloat16)
    other = pl.ds(pl.multiple_of((1 - core) * HALF_Q, HALF_Q), HALF_Q)
    qg_ref[:, 0:HALF_Q] = q_ref[0, :, other]
    qg_ref[:, HALF_Q:] = g_ref[0, :, other]


def dot_nt(a, b):
    return lax.dot_general(a, b, (((1,), (1,)), ((), ())), preferred_element_type=jnp.float32)


def dot_nn(a, b):
    return jnp.dot(a, b, preferred_element_type=jnp.float32)


def attention_kernel(
    q_ref, g_ref, qg_ref, own, up, n1, n2, n3, f1, f2, f3,
    dq_keep, dq_send, bias_ref, d0, d1, d2, d3, d4,
    qs, gs, kv, kt, mask, top, s_ref, dp_ref, dk_acc, dv_acc,
):
    z, y, core = place()
    mine = pl.ds(pl.multiple_of(core * HALF_Q, HALF_Q), HALF_Q)
    qs[0:ROWS, :] = q_ref[0, :, mine]
    qs[ROWS:, :] = qg_ref[:, 0:HALF_Q]
    gs[0:ROWS, :] = g_ref[0, :, mine]
    gs[ROWS:, :] = qg_ref[:, HALF_Q:]

    own_ids = jnp.concatenate(
        [own[ROWS : ROWS + 8, 0:ROWS], own[LINE + ROWS : LINE + ROWS + 8, 0:ROWS]], axis=1
    ).astype(jnp.float32)
    first_doc = jnp.min(own_ids)
    q_ids = own_ids[0:1, :]

    def fill(p, ref):
        kv[p, 0:ROWS, :] = ref[0:ROWS, :]
        kv[p, ROWS:, :] = ref[LINE : LINE + ROWS, :]
        a = ref[ROWS : ROWS + 8, 0:ROWS].astype(jnp.float32)
        b = ref[LINE + ROWS : LINE + ROWS + 8, 0:ROWS].astype(jnp.float32)
        top[p] = jnp.maximum(jnp.max(a), jnp.max(b))
        for part, ids in enumerate((a, b)):
            column = jnp.broadcast_to(ids[0:1, :], (ROWS, ROWS)).T
            same = jnp.concatenate([column, column], axis=1) == q_ids
            rows = slice(part * ROWS, (part + 1) * ROWS)
            if p == WINDOW - 1:
                key_at = lax.broadcasted_iota(jnp.int32, (ROWS, PAIR), 0) + ROWS * (
                    core if part == 0 else 1 - core
                )
                lane = lax.broadcasted_iota(jnp.int32, (ROWS, PAIR), 1)
                own_at = lane + ROWS * core
                query_at = jnp.where(lane < ROWS, own_at, own_at - 2 * ROWS * core)
                same = same & (key_at <= query_at)
            mask[p, rows, :] = jnp.where(same, 0.0, MASKED)
        for head in range(2):
            block = kv[p, :, head * HD : (head + 1) * HD].astype(jnp.float32)
            kt[head, p] = block.T.astype(jnp.bfloat16)

    for p in range(WINDOW):
        top[p] = -1.0
    fill(WINDOW - 1, own)

    @pl.when(z == 1)
    def _():
        fill(0, up)

    for p, far, near in ((1, f1, n3), (2, f2, n2), (3, f3, n1)):

        @pl.when((y + p < 4) & (z == 1))
        def _():
            fill(p, far)

        @pl.when(y + p >= 4)
        def _():
            fill(p, near)

    count = jnp.int32(1)
    for p in range(WINDOW - 1):
        count = count + (top[p] >= first_doc).astype(jnp.int32)

    outs = (d0, d1, d2, d3, d4)

    def run(amount):
        blocks = range(WINDOW - amount, WINDOW)
        for p in range(WINDOW - amount):
            outs[p][...] = jnp.zeros(outs[p].shape, jnp.bfloat16)

        def kv_head(kh, _):
            key_columns = pl.ds(pl.multiple_of(kh * HD, HD), HD)
            value_columns = pl.ds(pl.multiple_of(HALF_KV + kh * HD, HD), HD)
            for p in blocks:
                dk_acc[p] = jnp.zeros((PAIR, HD), jnp.float32)
                dv_acc[p] = jnp.zeros((PAIR, HD), jnp.float32)

            def one(g, _):
                columns = pl.ds(pl.multiple_of((kh * GROUP + g) * HD, HD), HD)
                query, grad = qs[:, columns], gs[:, columns]
                peak = jnp.full((1, PAIR), MASKED, jnp.float32)
                for p in blocks:
                    scores = dot_nt(kv[p, :, key_columns], query) * (INV_ROOT * LOG2E) + mask[p]
                    s_ref[p] = scores
                    peak = jnp.maximum(peak, jnp.max(scores, axis=0, keepdims=True))
                    dp_ref[p] = dot_nt(kv[p, :, value_columns], grad)
                total = jnp.zeros((1, PAIR), jnp.float32)
                dots = jnp.zeros((1, PAIR), jnp.float32)
                for p in blocks:
                    weights = jnp.exp2(s_ref[p] - peak)
                    s_ref[p] = weights
                    total = total + jnp.sum(weights, axis=0, keepdims=True)
                    dots = dots + jnp.sum(weights * dp_ref[p], axis=0, keepdims=True)
                inverse = 1.0 / total
                dots = dots * inverse
                dq = jnp.zeros((HD, PAIR), jnp.float32)
                for p in blocks:
                    softmax = s_ref[p] * inverse
                    score_grad = (softmax * (dp_ref[p] - dots)).astype(jnp.bfloat16)
                    dv_acc[p] += dot_nn(softmax.astype(jnp.bfloat16), grad)
                    dk_acc[p] += dot_nn(score_grad, query)
                    dq = dq + dot_nn(kt[kh, p], score_grad)
                dq = dq.T * INV_ROOT
                bias_ref[0:1, columns] = jnp.sum(dq, axis=0, keepdims=True)
                dq_keep[:, columns] = dq[0:ROWS].astype(jnp.bfloat16)
                dq_send[:, columns] = dq[ROWS:].astype(jnp.bfloat16)
                return 0

            lax.fori_loop(0, GROUP, one, 0)
            for p in blocks:
                outs[p][:, key_columns] = (dk_acc[p] * INV_ROOT).astype(jnp.bfloat16)
                outs[p][:, value_columns] = dv_acc[p].astype(jnp.bfloat16)
            return 0

        lax.fori_loop(0, 2, kv_head, 0)

    for amount in range(1, WINDOW + 1):

        @pl.when(count == amount)
        def _():
            run(amount)


def move(array, table):
    return lax.ppermute(array, "ctx", table)


def body(query_rows, key_rows, value_rows, out_grad, doc_ids):
    z, y, core = place()
    bf16, f32 = jnp.bfloat16, jnp.float32
    shape = jax.ShapeDtypeStruct
    line = shape((LINE, 2 * HALF_KV), bf16)
    send, keep, qg = pl.pallas_call(
        pack_kernel, out_shape=(line, line, shape((ROWS, 2 * HALF_Q), bf16)), name="pack"
    )(query_rows, out_grad, key_rows, value_rows, doc_ids)
    own = jnp.concatenate([keep, move(send, SWAP)], axis=0)
    up = move(own, UP)
    near = [move(own, near_pairs(k)) for k in (1, 2, 3)]
    qg = move(qg, SWAP)
    far = [move(up, far_pairs(k)) for k in (1, 2, 3)]

    block = shape((PAIR, 2 * HALF_KV), bf16)
    outs = pl.pallas_call(
        attention_kernel,
        out_shape=(
            shape((ROWS, HALF_Q), bf16),
            shape((ROWS, HALF_Q), bf16),
            shape((1, HALF_Q), f32),
            *[block] * WINDOW,
        ),
        scratch_shapes=[
            pltpu.VMEM((PAIR, HALF_Q), bf16),
            pltpu.VMEM((PAIR, HALF_Q), bf16),
            pltpu.VMEM((WINDOW, PAIR, 2 * HALF_KV), bf16),
            pltpu.VMEM((2, WINDOW, HD, PAIR), bf16),
            pltpu.VMEM((WINDOW, PAIR, PAIR), f32),
            pltpu.SMEM((WINDOW,), f32),
            pltpu.VMEM((WINDOW, PAIR, PAIR), f32),
            pltpu.VMEM((WINDOW, PAIR, PAIR), f32),
            pltpu.VMEM((WINDOW, PAIR, HD), f32),
            pltpu.VMEM((WINDOW, PAIR, HD), f32),
        ],
        compiler_params=pltpu.CompilerParams(vmem_limit_bytes=40 * 1024 * 1024),
        name="attention",
    )(query_rows, out_grad, qg, own, up, *near, *far)
    dq_keep, dq_send, bias = outs[:3]
    parts = outs[3:]

    back = [move(parts[p], back_pairs(p)).astype(f32) for p in (1, 2, 3)]
    far_sum, near_sum = parts[0].astype(f32), parts[4].astype(f32)
    for p, got in zip((1, 2, 3), back):
        far_sum = far_sum + jnp.where(y >= p, got, 0.0)
        near_sum = near_sum + jnp.where(y >= p, 0.0, got)
    far_sum = far_sum.astype(bf16)
    same = move(far_sum[:ROWS], DOWN).astype(f32)
    cross = move(far_sum[ROWS:], DOWN_CROSS).astype(f32)
    swapped = move(near_sum[ROWS:].astype(bf16), SWAP).astype(f32)
    mine = (near_sum[:ROWS] + same).astype(bf16)
    theirs = (swapped + cross).astype(bf16)

    def join(a, b):
        return jnp.where(
            core == 0, jnp.concatenate([a, b], axis=1), jnp.concatenate([b, a], axis=1)
        )[None]

    key_out = join(mine[:, :HALF_KV], theirs[:, :HALF_KV])
    value_out = join(mine[:, HALF_KV:], theirs[:, HALF_KV:])
    query_out = join(dq_keep, move(dq_send, SWAP))

    bias = bias[0]
    for axis, first in (("ctx", 1), ("dp", 0)):
        size = lax.axis_size(axis)
        step = 1 << first
        while step < size:
            bias = bias + lax.ppermute(bias, axis, [(i, i ^ step) for i in range(size)])
            step *= 2
    other = move(bias, SWAP)
    bias_out = jnp.where(
        core == 0, jnp.concatenate([bias, other]), jnp.concatenate([other, bias])
    )
    return (query_out, key_out, value_out, bias_out)


def solution(mesh):
    in_specs = (
        P("dp", "ctx", None),
        P("dp", "ctx", None),
        P("dp", "ctx", None),
        P("dp", "ctx", None),
        P("dp", "ctx"),
    )
    out_specs = (P("dp", "ctx", None), P("dp", "ctx", None), P("dp", "ctx", None), P())
    return jax.shard_map(body, mesh=mesh, in_specs=in_specs, out_specs=out_specs, check_vma=False)
```

time: 406 us -> 134 us (0.33)
  the two profiles are of different devices: /device:TPU:6 before, /device:TPU:65 now
where the time goes in v1:
time: 134 us; the launch traced here: 133 us
  starting transfers between devices  76.9 us (57%)
  waiting for transfers between devices  42.6 us (32%)
  Pallas kernels  9.18 us (7%)
  other arithmetic  2.84 us (2%)
    ppermute x7, starting transfers between devices, body(): bias = bias + lax.ppermute(bias, axis, [(i, i ^ step) for i in range(size)])  43.2 us
    ppermute x17, starting transfers between devices, move(): return lax.ppermute(array, 'ctx', table)  33.7 us
    ppermute x17, waiting for transfers between devices, move(): return lax.ppermute(array, 'ctx', table)  24.7 us
    ppermute x7, waiting for transfers between devices, body(): bias = bias + lax.ppermute(bias, axis, [(i, i ^ step) for i in range(size)])  17.9 us
    pallas_call x1, Pallas kernels, body(): pl.pallas_call(attention_kernel, out_shape=(shape((ROWS, HALF_Q), bf16),...  6.74 us
  transfers between devices with their start and end apart: 24, of which 14 were waited for; matrix products, arithmetic and copies ran while one was open for 2% of the time, Pallas kernels for 0%

profile of v1, /device:TPU:65, one launch (start us, length us, event | category | flops | bytes accessed | tf_op | source)
XLA Modules:
  0.0 133.4 jit_solution(7851227978226752162)
XLA Ops:
  0.7 2.4 %pack.1 = (bf16[144,512]{1,0:T(8,128)(2,1)}, bf16[144,512]{1,0:T(8,128)(2,1)}, bf16[128,2560]{1,0:T(8,128)(2,1)}) custom-call(bf16[1,128,2560]{2,1,0:T(8,128)(2,1)} %q_ref.3, bf16[1,128,2560]{2,1,0:T(8,128)(2,1)} %g_ref.3, bf16[1,128,512]{2,1,0:T(8,128)(2,1)} %k_ref.1, bf16[1,128,512]{2,1,0:T(8,128)(2,1)} %v_ref.1, s32[1,128]{1,0:T(1,128)} %ids_ref.1), custom_call_target="tpu_custom_call" | custom-call | tf_op jit(solution)/shard_map/pack/pallas_call | solution.py:215
  3.1 0.7 collective-permute-start.1
  3.8 0.9 constant_dynamic-update-slice_fusion.1
  4.7 0.3 collective-permute-done.1
  5.0 7.0 %collective-permute-start.2 = (bf16[288,512]{1,0:T(8,128)(2,1)S(1)}, bf16[288,512]{1,0:T(8,128)(2,1)S(1)}, u32[]{:S(2)}, u32[]{:S(2)}) collective-permute-start(bf16[288,512]{1,0:T(8,128)(2,1)S(1)} %constant_dynamic-update-slice_fusion.own), channel_id=1, source_target_pairs={{0,8},{1,9},{2,10},{3,11},{4,12},{5,13},{6,14},{7,15},{16,24},{17,... | collective-permute-start | bytes 884744 | tf_op jit(solution)/shard_map/ppermute | solution.py:207
  12.0 3.2 %collective-permute-start.3 = (bf16[288,512]{1,0:T(8,128)(2,1)S(1)}, bf16[288,512]{1,0:T(8,128)(2,1)S(1)}, u32[]{:S(2)}, u32[]{:S(2)}) collective-permute-start(bf16[288,512]{1,0:T(8,128)(2,1)S(1)} %constant_dynamic-update-slice_fusion.own), channel_id=1, source_target_pairs={{0,2},{1,3},{2,4},{3,5},{4,6},{5,7},{8,10},{9,11},{10,12},{11,13},... | collective-permute-start | bytes 884744 | tf_op jit(solution)/shard_map/ppermute | solution.py:207
  15.3 4.5 %collective-permute-start.4 = (bf16[288,512]{1,0:T(8,128)(2,1)S(1)}, bf16[288,512]{1,0:T(8,128)(2,1)S(1)}, u32[]{:S(2)}, u32[]{:S(2)}) collective-permute-start(bf16[288,512]{1,0:T(8,128)(2,1)S(1)} %constant_dynamic-update-slice_fusion.own), channel_id=1, source_target_pairs={{0,4},{1,5},{2,6},{3,7},{8,12},{9,13},{10,14},{11,15},{16,20},{17,... | collective-permute-start | bytes 884744 | tf_op jit(solution)/shard_map/ppermute | solution.py:207
  19.8 1.3 collective-permute-start.5
  21.1 3.2 %collective-permute-done.2.up = bf16[288,512]{1,0:T(8,128)(2,1)S(1)} collective-permute-done((bf16[288,512]{1,0:T(8,128)(2,1)S(1)}, bf16[288,512]{1,0:T(8,128)(2,1)S(1)}, u32[]{:S(2)}, u32[]{:S(2)}) %collective-permute-start.2) | collective-permute-done | bytes 294944 | tf_op jit(solution)/shard_map/ppermute | solution.py:207
  24.4 0.7 collective-permute-start.6
  25.0 0.7 collective-permute-start.7
  25.7 1.6 %collective-permute-done.4.n2 = bf16[288,512]{1,0:T(8,128)(2,1)S(1)} collective-permute-done((bf16[288,512]{1,0:T(8,128)(2,1)S(1)}, bf16[288,512]{1,0:T(8,128)(2,1)S(1)}, u32[]{:S(2)}, u32[]{:S(2)}) %collective-permute-start.4) | collective-permute-done | bytes 294944 | tf_op jit(solution)/shard_map/ppermute | solution.py:207
  27.3 0.7 collective-permute-start.8
  28.0 3.3 %collective-permute-done.5.n3 = bf16[288,512]{1,0:T(8,128)(2,1)S(1)} collective-permute-done((bf16[288,512]{1,0:T(8,128)(2,1)S(1)}, bf16[288,512]{1,0:T(8,128)(2,1)S(1)}, u32[]{:S(2)}, u32[]{:S(2)}) %collective-permute-start.5) | collective-permute-done | bytes 294944 | tf_op jit(solution)/shard_map/ppermute | solution.py:207
  31.3 0.0 collective-permute-done.7.f2
  31.3 0.0 collective-permute-done.8.f3
  31.4 6.7 %attention.1 = (bf16[128,1280]{1,0:T(8,128)(2,1)S(1)}, bf16[128,1280]{1,0:T(8,128)(2,1)S(1)}, f32[1,1280]{1,0:T(1,128)S(1)}, bf16[256,512]{1,0:T(8,128)(2,1)S(1)...) custom-call(bf16[1,128,2560]{2,1,0:T(8,128)(2,1)S(1)} %copy-done, ...), custom_call_target="tpu_custom_call" | custom-call | tf_op jit(solution)/shard_map/attention/pallas_call | solution.py:225
  38.1 1.3 collective-permute-start.10
  39.4 1.3 collective-permute-start.11
  40.7 1.3 collective-permute-start.12
  42.0 2.2 %collective-permute-start.16 = (f32[1280]{0:T(1024)S(1)}, f32[1280]{0:T(1024)S(1)}, u32[]{:S(2)}, u32[]{:S(2)}) collective-permute-start(f32[1280]{0:T(1024)S(1)} %reduce), channel_id=1, source_target_pairs={{0,2},{1,3},{2,0},{3,1},{4,6},{5,7},{6,4},{7,5},{8,10},{9,11},{10,... | collective-permute-start | bytes 15368 | tf_op jit(solution)/shard_map/ppermute | solution.py:277
  44.2 6.0 %collective-permute-done.16 = f32[1280]{0:T(1024)S(1)} collective-permute-done((f32[1280]{0:T(1024)S(1)}, f32[1280]{0:T(1024)S(1)}, u32[]{:S(2)}, u32[]{:S(2)}) %collective-permute-start.16) | collective-permute-done | bytes 5152 | tf_op jit(solution)/shard_map/ppermute | solution.py:277
  50.2 14.0 %collective-permute-start.17 = (f32[1280]{0:T(1024)S(1)}, f32[1280]{0:T(1024)S(1)}, u32[]{:S(2)}, u32[]{:S(2)}) collective-permute-start(f32[1280]{0:T(1024)S(1)} %add.63), channel_id=1, source_target_pairs={{0,4},{1,5},{2,6},{3,7},{4,0},{5,1},{6,2},{7,3},{8,12},{9,13},{10,... | collective-permute-start | bytes 15368 | tf_op jit(solution)/shard_map/ppermute | solution.py:277
  64.2 1.0 collective-permute-done.17
  65.2 24.1 %collective-permute-start.18 = (f32[1280]{0:T(1024)S(1)}, f32[1280]{0:T(1024)S(1)}, u32[]{:S(2)}, u32[]{:S(2)}) collective-permute-start(f32[1280]{0:T(1024)S(1)} %add.64), channel_id=1, source_target_pairs={{0,8},{1,9},{2,10},{3,11},{4,12},{5,13},{6,14},{7,15},{8,0},{9,1},... | collective-permute-start | bytes 15368 | tf_op jit(solution)/shard_map/ppermute | solution.py:277
  89.4 1.0 collective-permute-done.18
  90.4 2.8 %collective-permute-done.19 = f32[1280]{0:T(1024)S(1)} collective-permute-done((f32[1280]{0:T(1024)S(1)}, f32[1280]{0:T(1024)S(1)}, u32[]{:S(2)}, u32[]{:S(2)}) %collective-permute-start.19) | collective-permute-done | bytes 5152 | tf_op jit(solution)/shard_map/ppermute | solution.py:277
  93.2 0.1 collective-permute-start.20
  93.3 3.3 %collective-permute-done.20 = f32[1280]{0:T(1024)S(1)} collective-permute-done((f32[1280]{0:T(1024)S(1)}, f32[1280]{0:T(1024)S(1)}, u32[]{:S(2)}, u32[]{:S(2)}) %collective-permute-start.20) | collective-permute-done | bytes 5152 | tf_op jit(solution)/shard_map/ppermute | solution.py:277
  96.6 0.0 collective-permute-start.21
  96.6 2.5 %collective-permute-done.21 = f32[1280]{0:T(1024)S(1)} collective-permute-done((f32[1280]{0:T(1024)S(1)}, f32[1280]{0:T(1024)S(1)}, u32[]{:S(2)}, u32[]{:S(2)}) %collective-permute-start.21) | collective-permute-done | bytes 5152 | tf_op jit(solution)/shard_map/ppermute | solution.py:277
  99.1 2.7 %collective-permute-start.22 = (f32[1280]{0:T(1024)S(1)}, f32[1280]{0:T(1024)S(1)}, u32[]{:S(2)}, u32[]{:S(2)}) collective-permute-start(f32[1280]{0:T(1024)S(1)} %add.68), channel_id=1, source_target_pairs={{0,128},{16,144},{32,160},{48,176},{64,192},{80,208},{96,224},{112... | collective-permute-start | bytes 15368 | tf_op jit(solution)/shard_map/ppermute | solution.py:277
  101.9 1.3 collective-permute-done.22
  103.1 8.0 %collective-permute-start.23 = (f32[1280]{0:T(1024)S(1)}, f32[1280]{0:T(1024)S(1)}, u32[]{:S(2)}, u32[]{:S(2)}) collective-permute-start(f32[1280]{0:T(1024)S(1)} %add.69), channel_id=1, source_target_pairs={{0,1},{1,0},{2,3},{3,2},{4,5},{5,4},{6,7},{7,6},{8,9},{9,8},{10,11... | collective-permute-start | bytes 15368 | tf_op jit(solution)/shard_map/ppermute | solution.py:207
  111.2 0.0 collective-permute-start.9
  111.2 0.8 collective-permute-done.23
  112.0 0.6 maximum_select_fusion.3
  112.6 0.0 collective-permute-done.12
  112.6 0.3 fusion.2
  113.0 1.3 collective-permute-start.13
  114.3 1.3 collective-permute-start.15
  115.6 0.4 collective-permute-start.14
  116.0 0.0 collective-permute-done.9
  116.0 1.0 maximum_select_fusion
  117.0 12.7 %collective-permute-done.13 = bf16[128,512]{1,0:T(8,128)(2,1)S(1)} collective-permute-done((bf16[128,512]{1,0:T(8,128)(2,1)S(1)}, bf16[128,512]{1,0:T(8,128)(2,1)S(1)}, u32[]{:S(2)}, u32[]{:S(2)}) %collective-permute-start.13) | collective-permute-done | bytes 131104 | tf_op jit(solution)/shard_map/ppermute | solution.py:207
  129.8 2.8 %collective-permute-done.15 = bf16[128,512]{1,0:T(8,128)(2,1)S(1)} collective-permute-done((bf16[128,512]{1,0:T(8,128)(2,1)S(1)}, bf16[128,512]{1,0:T(8,128)(2,1)S(1)}, u32[]{:S(2)}, u32[]{:S(2)}) %collective-permute-start.15) | collective-permute-done | bytes 131104 | tf_op jit(solution)/shard_map/ppermute | solution.py:207
  132.5 0.0 collective-permute-done.14
  132.6 0.8 maximum_select_fusion.1
  (26 shorter events, 0.2 us)
Async XLA Ops:
  0.6 30.7 %copy-start = (bf16[1,128,2560]{2,1,0:T(8,128)(2,1)S(1)}, bf16[1,128,2560]{2,1,0:T(8,128)(2,1)}, u32[]{:S(2)}) copy-start(bf16[1,128,2560]{2,1,0:T(8,128)(2,1)} %q_ref.3) | copy-start | bytes 1966084
  0.6 30.7 %copy-start.1 = (bf16[1,128,2560]{2,1,0:T(8,128)(2,1)S(1)}, bf16[1,128,2560]{2,1,0:T(8,128)(2,1)}, u32[]{:S(2)}) copy-start(bf16[1,128,2560]{2,1,0:T(8,128)(2,1)} %g_ref.3) | copy-start | bytes 1966084
  3.1 1.9 %collective-permute-start.1 = (bf16[144,512]{1,0:T(8,128)(2,1)}, bf16[144,512]{1,0:T(8,128)(2,1)S(1)}, u32[]{:S(2)}, u32[]{:S(2)}) collective-permute-start(bf16[144,512]{1,0:T(8,128)(2,1)} %get-tuple-element.17), channel_id=1, source_target_pairs={{0,1},{1,0},{2,3},{3,2},{4,5},{5,4},{6,7},{7,6},{8,9},{9,8},{10,11... | collective-permute-start | bytes 442376 | tf_op jit(solution)/shard_map/ppermute | solution.py:207
  3.8 27.5 %collective-permute-start = (bf16[128,2560]{1,0:T(8,128)(2,1)}, bf16[128,2560]{1,0:T(8,128)(2,1)S(1)}, u32[]{:S(2)}, u32[]{:S(2)}) collective-permute-start(bf16[128,2560]{1,0:T(8,128)(2,1)} %get-tuple-element.15), channel_id=1, source_target_pairs={{0,1},{1,0},{2,3},{3,2},{4,5},{5,4},{6,7},{7,6},{8,9},{9,8},{10,11... | collective-permute-start | bytes 1966088 | tf_op jit(solution)/shard_map/ppermute | solution.py:207
  5.0 19.4 %collective-permute-start.2 = (bf16[288,512]{1,0:T(8,128)(2,1)S(1)}, bf16[288,512]{1,0:T(8,128)(2,1)S(1)}, u32[]{:S(2)}, u32[]{:S(2)}) collective-permute-start(bf16[288,512]{1,0:T(8,128)(2,1)S(1)} %constant_dynamic-update-slice_fusion.own), channel_id=1, source_target_pairs={{0,8},{1,9},{2,10},{3,11},{4,12},{5,13},{6,14},{7,15},{16,24},{17,... | collective-permute-start | bytes 884744 | tf_op jit(solution)/shard_map/ppermute | solution.py:207
  12.0 13.0 %collective-permute-start.3 = (bf16[288,512]{1,0:T(8,128)(2,1)S(1)}, bf16[288,512]{1,0:T(8,128)(2,1)S(1)}, u32[]{:S(2)}, u32[]{:S(2)}) collective-permute-start(bf16[288,512]{1,0:T(8,128)(2,1)S(1)} %constant_dynamic-update-slice_fusion.own), channel_id=1, source_target_pairs={{0,2},{1,3},{2,4},{3,5},{4,6},{5,7},{8,10},{9,11},{10,12},{11,13},... | collective-permute-start | bytes 884744 | tf_op jit(solution)/shard_map/ppermute | solution.py:207
  15.3 12.0 %collective-permute-start.4 = (bf16[288,512]{1,0:T(8,128)(2,1)S(1)}, bf16[288,512]{1,0:T(8,128)(2,1)S(1)}, u32[]{:S(2)}, u32[]{:S(2)}) collective-permute-start(bf16[288,512]{1,0:T(8,128)(2,1)S(1)} %constant_dynamic-update-slice_fusion.own), channel_id=1, source_target_pairs={{0,4},{1,5},{2,6},{3,7},{8,12},{9,13},{10,14},{11,15},{16,20},{17,... | collective-permute-start | bytes 884744 | tf_op jit(solution)/shard_map/ppermute | solution.py:207
  19.8 11.5 %collective-permute-start.5 = (bf16[288,512]{1,0:T(8,128)(2,1)S(1)}, bf16[288,512]{1,0:T(8,128)(2,1)S(1)}, u32[]{:S(2)}, u32[]{:S(2)}) collective-permute-start(bf16[288,512]{1,0:T(8,128)(2,1)S(1)} %constant_dynamic-update-slice_fusion.own), channel_id=1, source_target_pairs={{0,6},{1,7},{8,14},{9,15},{16,22},{17,23},{24,30},{25,31},{32,38},... | collective-permute-start | bytes 884744 | tf_op jit(solution)/shard_map/ppermute | solution.py:207
  24.4 7.0 %collective-permute-start.6 = (bf16[288,512]{1,0:T(8,128)(2,1)S(1)}, bf16[288,512]{1,0:T(8,128)(2,1)S(1)}, u32[]{:S(2)}, u32[]{:S(2)}) collective-permute-start(bf16[288,512]{1,0:T(8,128)(2,1)S(1)} %collective-permute-done.2.up), channel_id=1, source_target_pairs={{10,8},{11,9},{12,10},{13,11},{14,12},{15,13},{26,24},{27,25},{28,... | collective-permute-start | bytes 884744 | tf_op jit(solution)/shard_map/ppermute | solution.py:207
  25.0 6.3 %collective-permute-start.7 = (bf16[288,512]{1,0:T(8,128)(2,1)S(1)}, bf16[288,512]{1,0:T(8,128)(2,1)S(1)}, u32[]{:S(2)}, u32[]{:S(2)}) collective-permute-start(bf16[288,512]{1,0:T(8,128)(2,1)S(1)} %collective-permute-done.2.up), channel_id=1, source_target_pairs={{12,8},{13,9},{14,10},{15,11},{28,24},{29,25},{30,26},{31,27},{44,... | collective-permute-start | bytes 884744 | tf_op jit(solution)/shard_map/ppermute | solution.py:207
  27.3 4.0 %collective-permute-start.8 = (bf16[288,512]{1,0:T(8,128)(2,1)S(1)}, bf16[288,512]{1,0:T(8,128)(2,1)S(1)}, u32[]{:S(2)}, u32[]{:S(2)}) collective-permute-start(bf16[288,512]{1,0:T(8,128)(2,1)S(1)} %collective-permute-done.2.up), channel_id=1, source_target_pairs={{14,8},{15,9},{30,24},{31,25},{46,40},{47,41},{62,56},{63,57},{78,... | collective-permute-start | bytes 884744 | tf_op jit(solution)/shard_map/ppermute | solution.py:207
  38.1 74.5 %collective-permute-start.10 = (bf16[256,512]{1,0:T(8,128)(2,1)S(1)}, bf16[256,512]{1,0:T(8,128)(2,1)S(1)}, u32[]{:S(2)}, u32[]{:S(2)}) collective-permute-start(bf16[256,512]{1,0:T(8,128)(2,1)S(1)} %get-tuple-element.21), channel_id=1, source_target_pairs={{6,0},{7,1},{8,10},{9,11},{10,12},{11,13},{12,14},{13,15},{14,8},{... | collective-permute-start | bytes 786440 | tf_op jit(solution)/shard_map/ppermute | solution.py:207
  39.4 73.2 %collective-permute-start.11 = (bf16[256,512]{1,0:T(8,128)(2,1)S(1)}, bf16[256,512]{1,0:T(8,128)(2,1)S(1)}, u32[]{:S(2)}, u32[]{:S(2)}) collective-permute-start(bf16[256,512]{1,0:T(8,128)(2,1)S(1)} %get-tuple-element.22), channel_id=1, source_target_pairs={{4,0},{5,1},{6,2},{7,3},{8,12},{9,13},{10,14},{11,15},{12,8},{13,9... | collective-permute-start | bytes 786440 | tf_op jit(solution)/shard_map/ppermute | solution.py:207
  40.7 71.9 %collective-permute-start.12 = (bf16[256,512]{1,0:T(8,128)(2,1)S(1)}, bf16[256,512]{1,0:T(8,128)(2,1)S(1)}, u32[]{:S(2)}, u32[]{:S(2)}) collective-permute-start(bf16[256,512]{1,0:T(8,128)(2,1)S(1)} %get-tuple-element.23), channel_id=1, source_target_pairs={{2,0},{3,1},{4,2},{5,3},{6,4},{7,5},{8,14},{9,15},{10,8},{11,9},{1... | collective-permute-start | bytes 786440 | tf_op jit(solution)/shard_map/ppermute | solution.py:207
  42.0 8.1 %collective-permute-start.16 = (f32[1280]{0:T(1024)S(1)}, f32[1280]{0:T(1024)S(1)}, u32[]{:S(2)}, u32[]{:S(2)}) collective-permute-start(f32[1280]{0:T(1024)S(1)} %reduce), channel_id=1, source_target_pairs={{0,2},{1,3},{2,0},{3,1},{4,6},{5,7},{6,4},{7,5},{8,10},{9,11},{10,... | collective-permute-start | bytes 15368 | tf_op jit(solution)/shard_map/ppermute | solution.py:277
  50.2 15.1 %collective-permute-start.17 = (f32[1280]{0:T(1024)S(1)}, f32[1280]{0:T(1024)S(1)}, u32[]{:S(2)}, u32[]{:S(2)}) collective-permute-start(f32[1280]{0:T(1024)S(1)} %add.63), channel_id=1, source_target_pairs={{0,4},{1,5},{2,6},{3,7},{4,0},{5,1},{6,2},{7,3},{8,12},{9,13},{10,... | collective-permute-start | bytes 15368 | tf_op jit(solution)/shard_map/ppermute | solution.py:277
  65.2 25.2 %collective-permute-start.18 = (f32[1280]{0:T(1024)S(1)}, f32[1280]{0:T(1024)S(1)}, u32[]{:S(2)}, u32[]{:S(2)}) collective-permute-start(f32[1280]{0:T(1024)S(1)} %add.64), channel_id=1, source_target_pairs={{0,8},{1,9},{2,10},{3,11},{4,12},{5,13},{6,14},{7,15},{8,0},{9,1},... | collective-permute-start | bytes 15368 | tf_op jit(solution)/shard_map/ppermute | solution.py:277
  90.4 2.8 %collective-permute-start.19 = (f32[1280]{0:T(1024)S(1)}, f32[1280]{0:T(1024)S(1)}, u32[]{:S(2)}, u32[]{:S(2)}) collective-permute-start(f32[1280]{0:T(1024)S(1)} %add.65), channel_id=1, source_target_pairs={{0,16},{16,0},{32,48},{48,32},{64,80},{80,64},{96,112},{112,96},{1... | collective-permute-start | bytes 15368 | tf_op jit(solution)/shard_map/ppermute | solution.py:277
  93.2 3.4 %collective-permute-start.20 = (f32[1280]{0:T(1024)S(1)}, f32[1280]{0:T(1024)S(1)}, u32[]{:S(2)}, u32[]{:S(2)}) collective-permute-start(f32[1280]{0:T(1024)S(1)} %add.66), channel_id=1, source_target_pairs={{0,32},{16,48},{32,0},{48,16},{64,96},{80,112},{96,64},{112,80},{1... | collective-permute-start | bytes 15368 | tf_op jit(solution)/shard_map/ppermute | solution.py:277
  96.6 2.5 %collective-permute-start.21 = (f32[1280]{0:T(1024)S(1)}, f32[1280]{0:T(1024)S(1)}, u32[]{:S(2)}, u32[]{:S(2)}) collective-permute-start(f32[1280]{0:T(1024)S(1)} %add.67), channel_id=1, source_target_pairs={{0,64},{16,80},{32,96},{48,112},{64,0},{80,16},{96,32},{112,48},{1... | collective-permute-start | bytes 15368 | tf_op jit(solution)/shard_map/ppermute | solution.py:277
  99.1 4.0 %collective-permute-start.22 = (f32[1280]{0:T(1024)S(1)}, f32[1280]{0:T(1024)S(1)}, u32[]{:S(2)}, u32[]{:S(2)}) collective-permute-start(f32[1280]{0:T(1024)S(1)} %add.68), channel_id=1, source_target_pairs={{0,128},{16,144},{32,160},{48,176},{64,192},{80,208},{96,224},{112... | collective-permute-start | bytes 15368 | tf_op jit(solution)/shard_map/ppermute | solution.py:277
  103.1 8.9 %collective-permute-start.23 = (f32[1280]{0:T(1024)S(1)}, f32[1280]{0:T(1024)S(1)}, u32[]{:S(2)}, u32[]{:S(2)}) collective-permute-start(f32[1280]{0:T(1024)S(1)} %add.69), channel_id=1, source_target_pairs={{0,1},{1,0},{2,3},{3,2},{4,5},{5,4},{6,7},{7,6},{8,9},{9,8},{10,11... | collective-permute-start | bytes 15368 | tf_op jit(solution)/shard_map/ppermute | solution.py:207
  111.2 4.8 %collective-permute-start.9 = (bf16[128,1280]{1,0:T(8,128)(2,1)S(1)}, bf16[128,1280]{1,0:T(8,128)(2,1)S(1)}, u32[]{:S(2)}, u32[]{:S(2)}) collective-permute-start(bf16[128,1280]{1,0:T(8,128)(2,1)S(1)} %get-tuple-element.19), channel_id=1, source_target_pairs={{0,1},{1,0},{2,3},{3,2},{4,5},{5,4},{6,7},{7,6},{8,9},{9,8},{10,11... | collective-permute-start | bytes 983048 | tf_op jit(solution)/shard_map/ppermute | solution.py:207
  113.0 16.7 %collective-permute-start.13 = (bf16[128,512]{1,0:T(8,128)(2,1)S(1)}, bf16[128,512]{1,0:T(8,128)(2,1)S(1)}, u32[]{:S(2)}, u32[]{:S(2)}) collective-permute-start(bf16[128,512]{1,0:T(8,128)(2,1)S(1)} %get-tuple-element.28), channel_id=1, source_target_pairs={{8,0},{9,1},{10,2},{11,3},{12,4},{13,5},{14,6},{15,7},{24,16},{25,... | collective-permute-start | bytes 393224 | tf_op jit(solution)/shard_map/ppermute | solution.py:207
  114.3 18.2 %collective-permute-start.15 = (bf16[128,512]{1,0:T(8,128)(2,1)S(1)}, bf16[128,512]{1,0:T(8,128)(2,1)S(1)}, u32[]{:S(2)}, u32[]{:S(2)}) collective-permute-start(bf16[128,512]{1,0:T(8,128)(2,1)S(1)} %get-tuple-element.29), channel_id=1, source_target_pairs={{8,1},{9,0},{10,3},{11,2},{12,5},{13,4},{14,7},{15,6},{24,17},{25,... | collective-permute-start | bytes 393224 | tf_op jit(solution)/shard_map/ppermute | solution.py:207
  115.6 16.9 %collective-permute-start.14 = (bf16[128,512]{1,0:T(8,128)(2,1)S(1)}, bf16[128,512]{1,0:T(8,128)(2,1)S(1)}, u32[]{:S(2)}, u32[]{:S(2)}) collective-permute-start(bf16[128,512]{1,0:T(8,128)(2,1)S(1)} %slice.49), channel_id=1, source_target_pairs={{0,1},{1,0},{2,3},{3,2},{4,5},{5,4},{6,7},{7,6},{8,9},{9,8},{10,11... | collective-permute-start | bytes 393224 | tf_op jit(solution)/shard_map/ppermute | solution.py:207

commit v2 on v0

v2 whole, which is shorter than its diff:
```python
import math

import jax
import jax.numpy as jnp
from jax import lax
from jax.experimental import pallas as pl
from jax.experimental.pallas import tpu as pltpu
from jax.sharding import PartitionSpec as P

HD = 128
QH = 20
KVH = 4
GROUP = QH // KVH
ROWS = 128
CHIPS = 4
GCOLS = GROUP * HD
LANES = GROUP * ROWS
LINE = ROWS + 16
BUNDLE = CHIPS * ROWS + 16
CHUNKS = 16
BLOCKS = 5
INV_ROOT = HD ** (-0.5)
LOG2E = math.log2(math.e)
MASKED = -1e30
bf16, f32 = jnp.bfloat16, jnp.float32


def place():
    index = lax.axis_index("ctx")
    return index // 8, (index // 2) % 4, index % 2


def pairs(target):
    out = []
    for z in range(2):
        for y in range(4):
            for c in range(2):
                to = target(z, y, c)
                if to is not None:
                    out.append((z * 8 + y * 2 + c, to[0] * 8 + to[1] * 2 + to[2]))
    return out


SWAP = pairs(lambda z, y, c: (z, y, 1 - c))
UP = pairs(lambda z, y, c: (1, y, c) if z == 0 else None)
DOWN = pairs(lambda z, y, c: (0, y, c) if z == 1 else None)


def shift(k):
    return pairs(lambda z, y, c: (z, (y + k) % CHIPS, c))


def head_of(y, k, width):
    return pl.ds(pl.multiple_of(lax.rem(y + k, CHIPS) * width, width), width)


def pack_kv_kernel(k_ref, v_ref, ids_ref, *outs):
    _, y, _ = place()
    ids = jnp.broadcast_to(ids_ref[...].astype(f32), (16, ROWS)).astype(bf16)
    for k, out in enumerate(outs):
        out[0:ROWS, 0:HD] = k_ref[0, :, head_of(y, k, HD)]
        out[0:ROWS, HD:] = v_ref[0, :, head_of(y, k, HD)]
        out[ROWS:, 0:HD] = ids
        out[ROWS:, HD:] = ids


def bundle_kernel(l0, l1, l2, l3, out):
    lines = (l0, l1, l2, l3)
    for k, line in enumerate(lines):
        out[k * ROWS : (k + 1) * ROWS, :] = line[0:ROWS, :]
    ids = [line[ROWS:, 0:HD].astype(f32)[0:8] for line in lines]
    first = jnp.concatenate([ids[0], ids[1]], axis=1)
    second = jnp.concatenate([ids[2], ids[3]], axis=1)
    out[CHIPS * ROWS :, :] = jnp.concatenate([first, second], axis=0).astype(bf16)


def pack_qg_kernel(q_ref, g_ref, after_ref, *outs):
    _, y, _ = place()
    for k, out in enumerate(outs):
        out[:, 0:GCOLS] = q_ref[0, :, head_of(y, k + 1, GCOLS)]
        out[:, GCOLS:] = g_ref[0, :, head_of(y, k + 1, GCOLS)]


def dot_nt(a, b):
    return lax.dot_general(a, b, (((1,), (1,)), ((), ())), preferred_element_type=f32)


def dot_nn(a, b):
    return jnp.dot(a, b, preferred_element_type=f32)


def ids_of(ref):
    rows = ref[CHIPS * ROWS :, :].astype(f32)
    return [rows[8 * (k // 2) : 8 * (k // 2) + 1, (k % 2) * ROWS : (k % 2 + 1) * ROWS] for k in range(4)]


def attention_kernel(
    q_ref, g_ref, g1, g2, g3, near_own, near_sib, far_own, far_sib,
    dq0, dq1, dq2, dq3, bias_ref, sib_ref, far_ref, near_ref,
    qs, gs, kv, kt, s_ref, dp_ref, peaks, dk_acc, dv_acc, dq_acc, starts, lows,
):
    z, y, core = place()

    for k, ref in enumerate((None, g1, g2, g3)):
        for h in range(GROUP):
            rows = slice(h * ROWS, (h + 1) * ROWS)
            if k == 0:
                columns = pl.ds(pl.multiple_of(y * GCOLS + h * HD, HD), HD)
                qs[k, rows, :] = q_ref[0, :, columns]
                gs[k, rows, :] = g_ref[0, :, columns]
            else:
                qs[k, rows, :] = ref[:, h * HD : (h + 1) * HD]
                gs[k, rows, :] = ref[:, GCOLS + h * HD : GCOLS + (h + 1) * HD]

    kv[0] = jnp.zeros((ROWS, 2 * HD), bf16)
    kt[0] = jnp.zeros((HD, ROWS), bf16)

    sources = ((far_own, 0, core), (far_sib, 0, 1 - core), (near_own, 1, core), (near_sib, 1, 1 - core))
    for ref, half, parity in sources:
        for k in range(CHIPS):
            at = 1 + half * 8 + 2 * lax.rem(y - k + CHIPS, CHIPS) + parity
            chunk = ref[k * ROWS : (k + 1) * ROWS, :]
            kv[at] = chunk
            kt[at] = chunk[:, 0:HD].astype(f32).T.astype(bf16)
    dk_acc[...] = jnp.zeros(dk_acc.shape, f32)
    dv_acc[...] = jnp.zeros(dv_acc.shape, f32)

    far_ids = [jnp.where(z == 1, row, -1.0) for ref in (far_own, far_sib) for row in ids_of(ref)]
    own_ids = ids_of(near_own)
    all_ids = jnp.concatenate(far_ids + own_ids + ids_of(near_sib), axis=0)
    begin = [jnp.sum((all_ids < d).astype(f32), keepdims=True).reshape(1, 1) for d in range(8)]
    for k in range(CHIPS):
        start = jnp.zeros((1, ROWS), f32)
        for d in range(8):
            start = start + jnp.where(own_ids[k] == d, begin[d], 0.0)
        starts[k] = jnp.broadcast_to(start, (8, ROWS)).astype(jnp.int32)
        lows[k] = jnp.min(start).astype(jnp.int32)

    def query_chunk(k, total_bias):
        place_in_half = 2 * lax.rem(y - k + CHIPS, CHIPS) + core
        here = 8 + place_in_half
        low = lows[k] // ROWS
        amount = (here - low + 2) // 2
        query, grad = qs[k], gs[k]
        start = starts[k][0:1, :]
        query_at = here * ROWS + lax.broadcasted_iota(jnp.int32, (1, ROWS), 1)

        def first(b, carried):
            peak, total, dots = carried
            base = here - 2 * b
            keys = kv[pl.ds(base, 2), :, 0:HD].reshape(2 * ROWS, HD)
            values = kv[pl.ds(base, 2), :, HD:].reshape(2 * ROWS, HD)
            key_at = (base - 1) * ROWS + lax.broadcasted_iota(jnp.int32, (2 * ROWS, ROWS), 0)
            allowed = (key_at >= start) & (key_at <= query_at)
            bias = jnp.where(allowed, 0.0, MASKED)
            bias = jnp.concatenate([bias] * GROUP, axis=1)
            scores = dot_nt(keys, query) * (INV_ROOT * LOG2E) + bias
            peak_now = jnp.maximum(peak, jnp.max(scores, axis=0, keepdims=True))
            weights = jnp.exp2(scores - peak_now)
            s_ref[b] = weights
            grads = dot_nt(values, grad)
            dp_ref[b] = grads
            peaks[b] = jnp.broadcast_to(peak_now, (8, LANES))
            fade = jnp.exp2(peak - peak_now)
            total = total * fade + jnp.sum(weights.reshape(-1, 8, LANES), axis=0)
            dots = dots * fade + jnp.sum((weights * grads).reshape(-1, 8, LANES), axis=0)
            return peak_now, total, dots

        nothing = jnp.zeros((8, LANES), f32)
        peak, total, dots = lax.fori_loop(
            0, amount, first, (jnp.full((1, LANES), MASKED, f32), nothing, nothing)
        )
        inverse = 1.0 / jnp.sum(total, axis=0, keepdims=True)
        dots = jnp.sum(dots, axis=0, keepdims=True) * inverse
        dq_acc[...] = jnp.zeros(dq_acc.shape, f32)

        def third(b, _):
            base = here - 2 * b
            softmax = s_ref[b] * (jnp.exp2(peaks[b][0:1] - peak) * inverse)
            score_grad = (softmax * (dp_ref[b] - dots)).astype(bf16)
            dv = dot_nn(softmax.astype(bf16), grad)
            dk = dot_nn(score_grad, query)
            dv_acc[pl.ds(base, 2)] += dv.reshape(2, ROWS, HD)
            dk_acc[pl.ds(base, 2)] += dk.reshape(2, ROWS, HD)
            dq_acc[...] += dot_nn(kt[base], score_grad[0:ROWS]) + dot_nn(
                kt[base + 1], score_grad[ROWS:]
            )
            return 0

        lax.fori_loop(0, amount, third, 0)
        bias_rows = []
        for h in range(GROUP):
            dq = dq_acc[:, h * ROWS : (h + 1) * ROWS].T * INV_ROOT
            bias_rows.append(jnp.sum(dq, axis=0, keepdims=True))
            for j, out in enumerate((dq0, dq1, dq2, dq3)):

                @pl.when(k == j)
                def _():
                    out[:, h * HD : (h + 1) * HD] = dq.astype(bf16)

        return total_bias + jnp.concatenate(bias_rows, axis=1)

    bias_ref[...] = lax.fori_loop(0, CHIPS, query_chunk, jnp.zeros((1, GCOLS), f32))

    half_rows = CHIPS * ROWS
    outputs = ((far_ref, 0, 0, core), (sib_ref, 0, 0, 1 - core), (near_ref, 0, 1, core), (sib_ref, half_rows, 1, 1 - core))
    for ref, offset, half, parity in outputs:
        for k in range(CHIPS):
            at = 1 + half * 8 + 2 * lax.rem(y - k + CHIPS, CHIPS) + parity
            rows = slice(offset + k * ROWS, offset + (k + 1) * ROWS)
            ref[rows, 0:HD] = (dk_acc[at] * INV_ROOT).astype(ref.dtype)
            ref[rows, HD:] = dv_acc[at].astype(ref.dtype)


def place_q_kernel(c0, c1, c2, c3, out):
    _, y, _ = place()
    for k, ref in enumerate((c0, c1, c2, c3)):
        out[0, :, head_of(y, k, GCOLS)] = ref[...]


def place_kernel(c0, c1, c2, c3, b0, b1, b2, b3, key_out, value_out, bias_out):
    _, y, _ = place()
    for k, ref in enumerate((c0, c1, c2, c3)):
        key_out[0, :, head_of(y, k, HD)] = ref[:, 0:HD]
        value_out[0, :, head_of(y, k, HD)] = ref[:, HD:]
    rows = [ref[...] for ref in (b0, b1, b2, b3)]
    for j in range(CHIPS):
        row = rows[j]
        for near in range(1, CHIPS):
            row = jnp.where(y == near, rows[(j - near) % CHIPS], row)
        bias_out[j * GCOLS : (j + 1) * GCOLS] = row


def move(array, table):
    return lax.ppermute(array, "ctx", table)


def meet(partner_x, partner_z):
    out = []
    for x in range(4):
        for z in range(8):
            px, pz = partner_x[x], partner_z[z]
            for rest in range(8):
                a = (x * 4 + z % 4) * 16 + z // 4 * 8 + rest
                b = (px * 4 + pz % 4) * 16 + pz // 4 * 8 + rest
                out.append((a, b))
    return out


STAY_X, STAY_Z = range(4), range(8)
MEETINGS = [
    meet((1, 0, 3, 2), STAY_Z),
    meet((3, 2, 1, 0), STAY_Z),
    meet(STAY_X, (1, 0, 3, 2, 5, 4, 7, 6)),
    meet(STAY_X, (7, 2, 1, 4, 3, 6, 5, 0)),
    meet(STAY_X, (3, 6, 5, 0, 7, 2, 1, 4)),
]


def body(query_rows, key_rows, value_rows, out_grad, doc_ids):
    _, y, _ = place()
    shape = jax.ShapeDtypeStruct
    vmem, anywhere = pl.BlockSpec(memory_space=pltpu.VMEM), pl.BlockSpec(memory_space=pl.ANY)

    lines = pl.pallas_call(
        pack_kv_kernel, out_shape=[shape((LINE, 2 * HD), bf16)] * CHIPS, name="pack_kv"
    )(key_rows, value_rows, doc_ids)
    lines = [lines[0]] + [move(lines[k], shift(k)) for k in (1, 2, 3)]
    near = pl.pallas_call(bundle_kernel, out_shape=shape((BUNDLE, 2 * HD), bf16), name="bundle")(
        *lines
    )
    far = move(near, UP)
    near_sib = move(near, SWAP)
    qg = pl.pallas_call(
        pack_qg_kernel,
        out_shape=[shape((ROWS, 2 * GCOLS), bf16)] * 3,
        in_specs=[vmem, vmem, anywhere],
        name="pack_qg",
    )(query_rows, out_grad, near)
    qg = [move(qg[k - 1], shift(k)) for k in (1, 2, 3)]
    far_sib = move(far, SWAP)

    half = shape((CHIPS * ROWS, 2 * HD), f32)
    outs = pl.pallas_call(
        attention_kernel,
        out_shape=(
            *[shape((ROWS, GCOLS), bf16)] * CHIPS,
            shape((1, GCOLS), f32),
            shape((2 * CHIPS * ROWS, 2 * HD), bf16),
            half,
            half,
        ),
        scratch_shapes=[
            pltpu.VMEM((CHIPS, LANES, HD), bf16),
            pltpu.VMEM((CHIPS, LANES, HD), bf16),
            pltpu.VMEM((CHUNKS + 1, ROWS, 2 * HD), bf16),
            pltpu.VMEM((CHUNKS + 1, HD, ROWS), bf16),
            pltpu.VMEM((BLOCKS, 2 * ROWS, LANES), f32),
            pltpu.VMEM((BLOCKS, 2 * ROWS, LANES), f32),
            pltpu.VMEM((BLOCKS, 8, LANES), f32),
            pltpu.VMEM((CHUNKS + 1, ROWS, HD), f32),
            pltpu.VMEM((CHUNKS + 1, ROWS, HD), f32),
            pltpu.VMEM((HD, LANES), f32),
            pltpu.VMEM((CHIPS, 8, ROWS), jnp.int32),
            pltpu.SMEM((CHIPS,), jnp.int32),
        ],
        compiler_params=pltpu.CompilerParams(vmem_limit_bytes=32 * 1024 * 1024),
        name="attention",
    )(query_rows, out_grad, *qg, near, near_sib, far, far_sib)
    dq, bias = outs[:CHIPS], outs[CHIPS][0]
    to_sib, far_part, near_part = outs[CHIPS + 1 :]

    sib = move(to_sib, SWAP).astype(f32)
    half_rows = CHIPS * ROWS
    far_sum = (far_part + sib[:half_rows]).astype(bf16)
    down = move(far_sum, DOWN)
    dq = [dq[0]] + [move(dq[k], shift(-k)) for k in (1, 2, 3)]
    kv_grad = (near_part + sib[half_rows:] + down.astype(f32)).astype(bf16)
    kv_grad = [kv_grad[k * ROWS : (k + 1) * ROWS] for k in range(CHIPS)]
    kv_grad = [kv_grad[0]] + [move(kv_grad[k], shift(-k)) for k in (1, 2, 3)]

    query_out = pl.pallas_call(
        place_q_kernel, out_shape=shape(query_rows.shape, bf16), name="place_q"
    )(*dq)

    bias = bias + move(bias, SWAP)
    bias = jnp.where(y < CHIPS, bias, far_sum[0, 0].astype(f32))
    for table in MEETINGS:
        bias = bias + lax.ppermute(bias, ("dp", "ctx"), table)
    heads = [bias] + [move(bias, shift(-k)) for k in (1, 2, 3)]
    key_out, value_out, bias_out = pl.pallas_call(
        place_kernel,
        out_shape=(
            shape(key_rows.shape, bf16),
            shape(value_rows.shape, bf16),
            shape((QH * HD,), f32),
        ),
        name="place",
    )(*kv_grad, *heads)
    return (query_out, key_out, value_out, bias_out)


def solution(mesh):
    in_specs = (
        P("dp", "ctx", None),
        P("dp", "ctx", None),
        P("dp", "ctx", None),
        P("dp", "ctx", None),
        P("dp", "ctx"),
    )
    out_specs = (P("dp", "ctx", None), P("dp", "ctx", None), P("dp", "ctx", None), P())
    return jax.shard_map(body, mesh=mesh, in_specs=in_specs, out_specs=out_specs, check_vma=False)
```

time: 406 us -> 98.8 us (0.24)
  blocking collectives: 123 us -> 0 us
  local copies, waits for them, and re-layouts: 75.2 us -> 2.45 us
  waiting for transfers between devices: 99.6 us -> 33.4 us
  matrix products: 66 us -> 0 us
  starting transfers between devices: 0.12 us -> 40.2 us
  other arithmetic: 26.7 us -> 0.3 us
  Pallas kernels: 0 us -> 20.8 us
  between operations: 13.8 us -> 1.48 us
    all_gather x2 -> x0, waiting for transfers between devices: 91.1 us -> none  [the longest x1 61.9 us: body(): lax.all_gather(value_rows, 'ctx', axis=1, tiled=True)]
    psum x1 -> x0, blocking collectives: 89.4 us -> none  [body(): bias_total = lax.psum(jnp.sum(query_flat, axis=0), ('dp', 'ctx'))]
    dot_general x28 -> x0, matrix products: 66 us -> none  [the longest x8 16.9 us: scores_of(): jnp.einsum('ikgd,jkd->kgij', query_heads, key_heads, preferred_element_ty...]
    ppermute x0 -> x26, starting transfers between devices: none -> 40.2 us  [the longest x21 33.1 us: move(): return lax.ppermute(array, 'ctx', table)]
    dynamic_slice x24 -> x0, local copies, waits for them, and re-layouts: 36.4 us -> none  [the longest x8 24.6 us: backward_step(): current = lax.dynamic_slice_in_dim(key_acc, first_row, slice_rows, 0)]
    ppermute x0 -> x26, waiting for transfers between devices: none -> 33.4 us  [the longest x21 21.4 us: move(): return lax.ppermute(array, 'ctx', table)]
    all_gather x1 -> x0, blocking collectives: 33.2 us -> none  [body(): lax.all_gather(doc_ids, 'ctx', axis=1, tiled=True)]
    pallas_call x0 -> x6, Pallas kernels: none -> 20.8 us  [the longest x1 11.3 us: body(): pl.pallas_call(attention_kernel, out_shape=(*[shape((ROWS, GCOLS), bf16)]...]
  transfers between devices with their start and end apart: 3 -> 26, of which waited for: 3 -> 12; matrix products, arithmetic and copies ran while one was open for 2% -> 1% of each run, Pallas kernels for 0% -> 4%
where the time goes in v2:
time: 98.8 us; the launch traced here: 98.7 us
  starting transfers between devices  40.2 us (41%)
  waiting for transfers between devices  33.4 us (34%)
  Pallas kernels  20.8 us (21%)
  local copies, waits for them, and re-layouts  2.45 us (2%)
  between operations  1.48 us (1%)
    ppermute x21, starting transfers between devices, move(): return lax.ppermute(array, 'ctx', table)  33.1 us
    ppermute x21, waiting for transfers between devices, move(): return lax.ppermute(array, 'ctx', table)  21.4 us
    ppermute x5, waiting for transfers between devices, body(): bias = bias + lax.ppermute(bias, ('dp', 'ctx'), table)  12 us
    pallas_call x1, Pallas kernels, body(): pl.pallas_call(attention_kernel, out_shape=(*[shape((ROWS, GCOLS), bf16)]...  11.3 us
    ppermute x5, starting transfers between devices, body(): bias = bias + lax.ppermute(bias, ('dp', 'ctx'), table)  7.12 us
    pallas_call x1, Pallas kernels, body(): pl.pallas_call(pack_qg_kernel, out_shape=[shape((ROWS, 2 * GCOLS), bf16)]...  2.3 us
    pallas_call x1, Pallas kernels, body(): pl.pallas_call(place_q_kernel, out_shape=shape(query_rows.shape, bf16), n...  2.07 us
  transfers between devices with their start and end apart: 26, of which 12 were waited for; matrix products, arithmetic and copies ran while one was open for 1% of the time, Pallas kernels for 4%

profile of v2, /device:TPU:6, one launch (start us, length us, event | category | flops | bytes accessed | tf_op | source)
XLA Modules:
  0.0 98.7 jit_solution(4206717987716683044)
XLA Ops:
  0.6 1.7 %pack_kv.1 = (bf16[144,256]{1,0:T(8,128)(2,1)}, bf16[144,256]{1,0:T(8,128)(2,1)}, bf16[144,256]{1,0:T(8,128)(2,1)}, bf16[144,256]{1,0:T(8,128)(2,1)}) custom-call(bf16[1,128,512]{2,1,0:T(8,128)(2,1)} %k_ref.1, bf16[1,128,512]{2,1,0:T(8,128)(2,1)} %v_ref.1, s32[1,128]{1,0:T(1,128)} %ids_ref.1), custom_call_target="tpu_custom_call" | custom-call | tf_op jit(solution)/shard_map/pack_kv/pallas_call | solution.py:265
  2.3 1.6 %collective-permute-start = (bf16[144,256]{1,0:T(8,128)(2,1)}, bf16[144,256]{1,0:T(8,128)(2,1)S(1)}, u32[]{:S(2)}, u32[]{:S(2)}) collective-permute-start(bf16[144,256]{1,0:T(8,128)(2,1)} %get-tuple-element.23), channel_id=1, source_target_pairs={{0,2},{1,3},{2,4},{3,5},{4,6},{5,7},{6,0},{7,1},{8,10},{9,11},{10,... | collective-permute-start | bytes 221192 | tf_op jit(solution)/shard_map/ppermute | solution.py:235
  3.9 2.9 %collective-permute-start.1 = (bf16[144,256]{1,0:T(8,128)(2,1)}, bf16[144,256]{1,0:T(8,128)(2,1)S(1)}, u32[]{:S(2)}, u32[]{:S(2)}) collective-permute-start(bf16[144,256]{1,0:T(8,128)(2,1)} %get-tuple-element.24), channel_id=1, source_target_pairs={{0,4},{1,5},{2,6},{3,7},{4,0},{5,1},{6,2},{7,3},{8,12},{9,13},{10,... | collective-permute-start | bytes 221192 | tf_op jit(solution)/shard_map/ppermute | solution.py:235
  6.8 1.3 %collective-permute-start.2 = (bf16[144,256]{1,0:T(8,128)(2,1)}, bf16[144,256]{1,0:T(8,128)(2,1)S(1)}, u32[]{:S(2)}, u32[]{:S(2)}) collective-permute-start(bf16[144,256]{1,0:T(8,128)(2,1)} %get-tuple-element.25), channel_id=1, source_target_pairs={{0,6},{1,7},{2,0},{3,1},{4,2},{5,3},{6,4},{7,5},{8,14},{9,15},{10,... | collective-permute-start | bytes 221192 | tf_op jit(solution)/shard_map/ppermute | solution.py:235
  8.2 2.4 %collective-permute-done.1.l2 = bf16[144,256]{1,0:T(8,128)(2,1)S(1)} collective-permute-done((bf16[144,256]{1,0:T(8,128)(2,1)}, bf16[144,256]{1,0:T(8,128)(2,1)S(1)}, u32[]{:S(2)}, u32[]{:S(2)}) %collective-permute-start.1) | collective-permute-done | bytes 73760 | tf_op jit(solution)/shard_map/ppermute | solution.py:235
  10.6 0.8 collective-permute-done.2.l3
  11.4 0.6 copy-done.9
  12.0 1.7 %bundle.1.after_ref.near_own = bf16[528,256]{1,0:T(8,128)(2,1)} custom-call(bf16[144,256]{1,0:T(8,128)(2,1)} %get-tuple-element.22.l0, bf16[144,256]{1,0:T(8,128)(2,1)} %copy-done.7, bf16[144,256]{1,0:T(8,128)(2,1)} %copy-done.8, bf16[144,256]{1,0:T(8,128)(2,1)} %copy-done.9), custom_call_target="tpu_custom_call" | custom-call | tf_op jit(solution)/shard_map/bundle/pallas_call | solution.py:269
  13.7 9.2 %collective-permute-start.7 = (bf16[528,256]{1,0:T(8,128)(2,1)}, bf16[528,256]{1,0:T(8,128)(2,1)S(1)}, u32[]{:S(2)}, u32[]{:S(2)}) collective-permute-start(bf16[528,256]{1,0:T(8,128)(2,1)} %bundle.1.after_ref.near_own), channel_id=1, source_target_pairs={{0,8},{1,9},{2,10},{3,11},{4,12},{5,13},{6,14},{7,15},{16,24},{17,... | collective-permute-start | bytes 811016 | tf_op jit(solution)/shard_map/ppermute | solution.py:235
  23.0 2.3 %pack_qg.1 = (bf16[128,1280]{1,0:T(8,128)(2,1)}, bf16[128,1280]{1,0:T(8,128)(2,1)}, bf16[128,1280]{1,0:T(8,128)(2,1)}) custom-call(bf16[1,128,2560]{2,1,0:T(8,128)(2,1)} %q_ref.3, bf16[1,128,2560]{2,1,0:T(8,128)(2,1)} %g_ref.3, bf16[528,256]{1,0:T(8,128)(2,1)} %bundle.1.after_ref.near_own), custom_call_target="tpu_custom_call" | custom-call | tf_op jit(solution)/shard_map/pack_qg/pallas_call | solution.py:274
  25.3 0.4 collective-permute-start.3
  25.7 3.6 %collective-permute-start.4 = (bf16[128,1280]{1,0:T(8,128)(2,1)}, bf16[128,1280]{1,0:T(8,128)(2,1)S(1)}, u32[]{:S(2)}, u32[]{:S(2)}) collective-permute-start(bf16[128,1280]{1,0:T(8,128)(2,1)} %get-tuple-element.27), channel_id=1, source_target_pairs={{0,4},{1,5},{2,6},{3,7},{4,0},{5,1},{6,2},{7,3},{8,12},{9,13},{10,... | collective-permute-start | bytes 983048 | tf_op jit(solution)/shard_map/ppermute | solution.py:235
  29.3 0.3 collective-permute-start.5
  29.6 0.5 collective-permute-start.8
  30.2 1.0 %collective-permute-done.6.near_sib = bf16[528,256]{1,0:T(8,128)(2,1)S(1)} collective-permute-done((bf16[528,256]{1,0:T(8,128)(2,1)S(1)}, bf16[528,256]{1,0:T(8,128)(2,1)S(1)}, u32[]{:S(2)}, u32[]{:S(2)}) %collective-permute-start.6) | collective-permute-done | bytes 270368 | tf_op jit(solution)/shard_map/ppermute | solution.py:235
  31.2 5.7 %collective-permute-done.3.g1 = bf16[128,1280]{1,0:T(8,128)(2,1)S(1)} collective-permute-done((bf16[128,1280]{1,0:T(8,128)(2,1)}, bf16[128,1280]{1,0:T(8,128)(2,1)S(1)}, u32[]{:S(2)}, u32[]{:S(2)}) %collective-permute-start.3) | collective-permute-done | bytes 327712 | tf_op jit(solution)/shard_map/ppermute | solution.py:235
  36.9 5.2 %collective-permute-done.4.g2 = bf16[128,1280]{1,0:T(8,128)(2,1)S(1)} collective-permute-done((bf16[128,1280]{1,0:T(8,128)(2,1)}, bf16[128,1280]{1,0:T(8,128)(2,1)S(1)}, u32[]{:S(2)}, u32[]{:S(2)}) %collective-permute-start.4) | collective-permute-done | bytes 327712 | tf_op jit(solution)/shard_map/ppermute | solution.py:235
  42.2 11.3 %attention.1 = (bf16[128,640]{1,0:T(8,128)(2,1)S(1)}, bf16[128,640]{1,0:T(8,128)(2,1)S(1)}, bf16[128,640]{1,0:T(8,128)(2,1)S(1)}, bf16[128,640]{1,0:T(8,128)(2,1...) custom-call(bf16[1,128,2560]{2,1,0:T(8,128)(2,1)S(1)} %copy-done, ...), custom_call_target="tpu_custom_call" | custom-call | tf_op jit(solution)/shard_map/attention/pallas_call | solution.py:284
  53.5 0.1 collective-permute-start.12
  53.6 1.9 %collective-permute-done.12 = bf16[1024,256]{1,0:T(8,128)(2,1)S(1)} collective-permute-done((bf16[1024,256]{1,0:T(8,128)(2,1)S(1)}, bf16[1024,256]{1,0:T(8,128)(2,1)S(1)}, u32[]{:S(2)}, u32[]{:S(2)}) %collective-permute-start.12) | collective-permute-done | bytes 524320 | tf_op jit(solution)/shard_map/ppermute | solution.py:235
  55.5 0.1 convert_element_type.18
  55.6 0.1 fusion
  55.7 1.3 %collective-permute-start.13 = (bf16[512,256]{1,0:T(8,128)(2,1)S(1)}, bf16[512,256]{1,0:T(8,128)(2,1)S(1)}, u32[]{:S(2)}, u32[]{:S(2)}) collective-permute-start(bf16[512,256]{1,0:T(8,128)(2,1)S(1)} %fusion), channel_id=1, source_target_pairs={{8,0},{9,1},{10,2},{11,3},{12,4},{13,5},{14,6},{15,7},{24,16},{25,... | collective-permute-start | bytes 786440 | tf_op jit(solution)/shard_map/ppermute | solution.py:235
  57.0 0.2 collective-permute-start.17
  57.2 0.5 slice.34
  58.4 0.1 collective-permute-start.18
  58.5 3.6 %collective-permute-done.18 = f32[640]{0:T(1024)S(1)} collective-permute-done((f32[640]{0:T(1024)S(1)}, f32[640]{0:T(1024)S(1)}, u32[]{:S(2)}, u32[]{:S(2)}) %collective-permute-start.18) | collective-permute-done | bytes 2592 | tf_op jit(solution)/shard_map/ppermute | solution.py:329
  62.1 4.8 %collective-permute-done.19 = f32[640]{0:T(1024)S(1)} collective-permute-done((f32[640]{0:T(1024)S(1)}, f32[640]{0:T(1024)S(1)}, u32[]{:S(2)}, u32[]{:S(2)}) %collective-permute-start.19) | collective-permute-done | bytes 2592 | tf_op jit(solution)/shard_map/ppermute | solution.py:329
  67.0 3.6 %collective-permute-done.20 = f32[640]{0:T(1024)S(1)} collective-permute-done((f32[640]{0:T(1024)S(1)}, f32[640]{0:T(1024)S(1)}, u32[]{:S(2)}, u32[]{:S(2)}) %collective-permute-start.20) | collective-permute-done | bytes 2592 | tf_op jit(solution)/shard_map/ppermute | solution.py:329
  70.6 5.1 %collective-permute-start.21 = (f32[640]{0:T(1024)S(1)}, f32[640]{0:T(1024)S(1)}, u32[]{:S(2)}, u32[]{:S(2)}) collective-permute-start(f32[640]{0:T(1024)S(1)} %add.39), channel_id=1, source_target_pairs={{0,56},{1,57},{2,58},{3,59},{4,60},{5,61},{6,62},{7,63},{16,32},{1... | collective-permute-start | bytes 7688 | tf_op jit(solution)/shard_map/ppermute | solution.py:329
  75.7 1.6 %collective-permute-start.10 = (bf16[128,640]{1,0:T(8,128)(2,1)S(1)}, bf16[128,640]{1,0:T(8,128)(2,1)S(1)}, u32[]{:S(2)}, u32[]{:S(2)}) collective-permute-start(bf16[128,640]{1,0:T(8,128)(2,1)S(1)} %get-tuple-element.31), channel_id=1, source_target_pairs={{0,4},{1,5},{2,6},{3,7},{4,0},{5,1},{6,2},{7,3},{8,12},{9,13},{10,... | collective-permute-start | bytes 491528 | tf_op jit(solution)/shard_map/ppermute | solution.py:235
  77.3 1.9 %collective-permute-start.11 = (bf16[128,640]{1,0:T(8,128)(2,1)S(1)}, bf16[128,640]{1,0:T(8,128)(2,1)S(1)}, u32[]{:S(2)}, u32[]{:S(2)}) collective-permute-start(bf16[128,640]{1,0:T(8,128)(2,1)S(1)} %get-tuple-element.32), channel_id=1, source_target_pairs={{0,2},{1,3},{2,4},{3,5},{4,6},{5,7},{6,0},{7,1},{8,10},{9,11},{10,... | collective-permute-start | bytes 491528 | tf_op jit(solution)/shard_map/ppermute | solution.py:235
  79.2 1.3 %collective-permute-start.9 = (bf16[128,640]{1,0:T(8,128)(2,1)S(1)}, bf16[128,640]{1,0:T(8,128)(2,1)S(1)}, u32[]{:S(2)}, u32[]{:S(2)}) collective-permute-start(bf16[128,640]{1,0:T(8,128)(2,1)S(1)} %get-tuple-element.30), channel_id=1, source_target_pairs={{0,6},{1,7},{2,0},{3,1},{4,2},{5,3},{6,4},{7,5},{8,14},{9,15},{10,... | collective-permute-start | bytes 491528 | tf_op jit(solution)/shard_map/ppermute | solution.py:235
  80.5 1.9 %collective-permute-start.22 = (f32[640]{0:T(1024)S(1)}, f32[640]{0:T(1024)S(1)}, u32[]{:S(2)}, u32[]{:S(2)}) collective-permute-start(f32[640]{0:T(1024)S(1)} %add.40), channel_id=1, source_target_pairs={{0,48},{1,49},{2,50},{3,51},{4,52},{5,53},{6,54},{7,55},{16,40},{1... | collective-permute-start | bytes 7688 | tf_op jit(solution)/shard_map/ppermute | solution.py:329
  82.4 0.1 fusion.2
  82.6 0.6 fusion.3
  83.2 0.8 collective-permute-start.14
  84.0 1.9 %collective-permute-start.15 = (bf16[128,256]{1,0:T(8,128)(2,1)S(1)}, bf16[128,256]{1,0:T(8,128)(2,1)S(1)}, u32[]{:S(2)}, u32[]{:S(2)}) collective-permute-start(bf16[128,256]{1,0:T(8,128)(2,1)S(1)} %get-tuple-element.41), channel_id=1, source_target_pairs={{0,4},{1,5},{2,6},{3,7},{4,0},{5,1},{6,2},{7,3},{8,12},{9,13},{10,... | collective-permute-start | bytes 196616 | tf_op jit(solution)/shard_map/ppermute | solution.py:235
  85.9 1.8 %collective-permute-start.16 = (bf16[128,256]{1,0:T(8,128)(2,1)S(1)}, bf16[128,256]{1,0:T(8,128)(2,1)S(1)}, u32[]{:S(2)}, u32[]{:S(2)}) collective-permute-start(bf16[128,256]{1,0:T(8,128)(2,1)S(1)} %get-tuple-element.40), channel_id=1, source_target_pairs={{0,2},{1,3},{2,4},{3,5},{4,6},{5,7},{6,0},{7,1},{8,10},{9,11},{10,... | collective-permute-start | bytes 196616 | tf_op jit(solution)/shard_map/ppermute | solution.py:235
  87.8 1.5 %collective-permute-start.23 = (f32[640]{0:T(1024)S(1)}, f32[640]{0:T(1024)S(1)}, u32[]{:S(2)}, u32[]{:S(2)}) collective-permute-start(f32[640]{0:T(1024)S(1)} %add.41.b0), channel_id=1, source_target_pairs={{0,6},{1,7},{2,0},{3,1},{4,2},{5,3},{6,4},{7,5},{8,14},{9,15},{10,... | collective-permute-start | bytes 7688 | tf_op jit(solution)/shard_map/ppermute | solution.py:235
  89.3 0.6 collective-permute-start.24
  89.9 1.5 %collective-permute-done.23.b1 = f32[640]{0:T(1024)S(1)} collective-permute-done((f32[640]{0:T(1024)S(1)}, f32[640]{0:T(1024)S(1)}, u32[]{:S(2)}, u32[]{:S(2)}) %collective-permute-start.23) | collective-permute-done | bytes 2592 | tf_op jit(solution)/shard_map/ppermute | solution.py:235
  91.5 2.1 %place_q.1 = bf16[1,128,2560]{2,1,0:T(8,128)(2,1)} custom-call(bf16[128,640]{1,0:T(8,128)(2,1)} %copy-done.3, bf16[128,640]{1,0:T(8,128)(2,1)} %copy-done.6, bf16[128,640]{1,0:T(8,128)(2,1)} %copy-done.4, bf16[128,640]{1,0:T(8,128)(2,1)} %copy-done.5), custom_call_target="tpu_custom_call" | custom-call | tf_op jit(solution)/shard_map/place_q/pallas_call | solution.py:322
  93.6 0.8 collective-permute-done.24.b2
  94.4 1.9 %collective-permute-done.25.b3 = f32[640]{0:T(1024)S(1)} collective-permute-done((f32[640]{0:T(1024)S(1)}, f32[640]{0:T(1024)S(1)}, u32[]{:S(2)}, u32[]{:S(2)}) %collective-permute-start.25) | collective-permute-done | bytes 2592 | tf_op jit(solution)/shard_map/ppermute | solution.py:235
  96.3 0.5 copy-done.16
  96.9 0.0 copy-done.12
  97.0 1.7 %place.1 = (bf16[1,128,512]{2,1,0:T(8,128)(2,1)}, bf16[1,128,512]{2,1,0:T(8,128)(2,1)}, f32[2560]{0:T(1024)}) custom-call(bf16[128,256]{1,0:T(8,128)(2,1)} %get-tuple-element.43.c0, bf16[128,256]{1,0:T(8,128)(2,1)} %copy-done.10, bf16[128,256]{1,0:T(8,128)(2,1)} %copy-done.11, bf16[128,256]{1,0:T(8,128)(2,1)} %copy-done.12, f32[640]{0:T(1024)} %copy-done.13, ...), custom_call_target="tpu_custom_call" | custom-call | tf_op jit(solution)/shard_map/place/pallas_call | solution.py:331
  (56 shorter events, 0.2 us)
Async XLA Ops:
  2.3 5.8 %collective-permute-start = (bf16[144,256]{1,0:T(8,128)(2,1)}, bf16[144,256]{1,0:T(8,128)(2,1)S(1)}, u32[]{:S(2)}, u32[]{:S(2)}) collective-permute-start(bf16[144,256]{1,0:T(8,128)(2,1)} %get-tuple-element.23), channel_id=1, source_target_pairs={{0,2},{1,3},{2,4},{3,5},{4,6},{5,7},{6,0},{7,1},{8,10},{9,11},{10,... | collective-permute-start | bytes 221192 | tf_op jit(solution)/shard_map/ppermute | solution.py:235
  3.9 6.7 %collective-permute-start.1 = (bf16[144,256]{1,0:T(8,128)(2,1)}, bf16[144,256]{1,0:T(8,128)(2,1)S(1)}, u32[]{:S(2)}, u32[]{:S(2)}) collective-permute-start(bf16[144,256]{1,0:T(8,128)(2,1)} %get-tuple-element.24), channel_id=1, source_target_pairs={{0,4},{1,5},{2,6},{3,7},{4,0},{5,1},{6,2},{7,3},{8,12},{9,13},{10,... | collective-permute-start | bytes 221192 | tf_op jit(solution)/shard_map/ppermute | solution.py:235
  6.8 4.6 %collective-permute-start.2 = (bf16[144,256]{1,0:T(8,128)(2,1)}, bf16[144,256]{1,0:T(8,128)(2,1)S(1)}, u32[]{:S(2)}, u32[]{:S(2)}) collective-permute-start(bf16[144,256]{1,0:T(8,128)(2,1)} %get-tuple-element.25), channel_id=1, source_target_pairs={{0,6},{1,7},{2,0},{3,1},{4,2},{5,3},{6,4},{7,5},{8,14},{9,15},{10,... | collective-permute-start | bytes 221192 | tf_op jit(solution)/shard_map/ppermute | solution.py:235
  8.2 3.2 %copy-start.7 = (bf16[144,256]{1,0:T(8,128)(2,1)}, bf16[144,256]{1,0:T(8,128)(2,1)S(1)}, u32[]{:S(2)}) copy-start(bf16[144,256]{1,0:T(8,128)(2,1)S(1)} %collective-permute-done.l1) | copy-start | bytes 221188
  10.6 0.8 copy-start.8
  11.4 0.6 copy-start.9
  13.7 15.9 %copy-start.2 = (bf16[528,256]{1,0:T(8,128)(2,1)S(1)}, bf16[528,256]{1,0:T(8,128)(2,1)}, u32[]{:S(2)}) copy-start(bf16[528,256]{1,0:T(8,128)(2,1)} %bundle.1.after_ref.near_own) | copy-start | bytes 811012
  13.7 28.4 %copy-start = (bf16[1,128,2560]{2,1,0:T(8,128)(2,1)S(1)}, bf16[1,128,2560]{2,1,0:T(8,128)(2,1)}, u32[]{:S(2)}) copy-start(bf16[1,128,2560]{2,1,0:T(8,128)(2,1)} %q_ref.3) | copy-start | bytes 1966084
  13.7 28.4 %copy-start.1 = (bf16[1,128,2560]{2,1,0:T(8,128)(2,1)S(1)}, bf16[1,128,2560]{2,1,0:T(8,128)(2,1)}, u32[]{:S(2)}) copy-start(bf16[1,128,2560]{2,1,0:T(8,128)(2,1)} %g_ref.3) | copy-start | bytes 1966084
  13.7 15.9 %collective-permute-start.7 = (bf16[528,256]{1,0:T(8,128)(2,1)}, bf16[528,256]{1,0:T(8,128)(2,1)S(1)}, u32[]{:S(2)}, u32[]{:S(2)}) collective-permute-start(bf16[528,256]{1,0:T(8,128)(2,1)} %bundle.1.after_ref.near_own), channel_id=1, source_target_pairs={{0,8},{1,9},{2,10},{3,11},{4,12},{5,13},{6,14},{7,15},{16,24},{17,... | collective-permute-start | bytes 811016 | tf_op jit(solution)/shard_map/ppermute | solution.py:235
  25.3 11.6 %collective-permute-start.3 = (bf16[128,1280]{1,0:T(8,128)(2,1)}, bf16[128,1280]{1,0:T(8,128)(2,1)S(1)}, u32[]{:S(2)}, u32[]{:S(2)}) collective-permute-start(bf16[128,1280]{1,0:T(8,128)(2,1)} %get-tuple-element.26), channel_id=1, source_target_pairs={{0,2},{1,3},{2,4},{3,5},{4,6},{5,7},{6,0},{7,1},{8,10},{9,11},{10,... | collective-permute-start | bytes 983048 | tf_op jit(solution)/shard_map/ppermute | solution.py:235
  25.7 16.4 %collective-permute-start.4 = (bf16[128,1280]{1,0:T(8,128)(2,1)}, bf16[128,1280]{1,0:T(8,128)(2,1)S(1)}, u32[]{:S(2)}, u32[]{:S(2)}) collective-permute-start(bf16[128,1280]{1,0:T(8,128)(2,1)} %get-tuple-element.27), channel_id=1, source_target_pairs={{0,4},{1,5},{2,6},{3,7},{4,0},{5,1},{6,2},{7,3},{8,12},{9,13},{10,... | collective-permute-start | bytes 983048 | tf_op jit(solution)/shard_map/ppermute | solution.py:235
  29.3 12.9 %collective-permute-start.5 = (bf16[128,1280]{1,0:T(8,128)(2,1)}, bf16[128,1280]{1,0:T(8,128)(2,1)S(1)}, u32[]{:S(2)}, u32[]{:S(2)}) collective-permute-start(bf16[128,1280]{1,0:T(8,128)(2,1)} %get-tuple-element.28), channel_id=1, source_target_pairs={{0,6},{1,7},{2,0},{3,1},{4,2},{5,3},{6,4},{7,5},{8,14},{9,15},{10,... | collective-permute-start | bytes 983048 | tf_op jit(solution)/shard_map/ppermute | solution.py:235
  29.6 1.5 %collective-permute-start.6 = (bf16[528,256]{1,0:T(8,128)(2,1)S(1)}, bf16[528,256]{1,0:T(8,128)(2,1)S(1)}, u32[]{:S(2)}, u32[]{:S(2)}) collective-permute-start(bf16[528,256]{1,0:T(8,128)(2,1)S(1)} %copy-done.2), channel_id=1, source_target_pairs={{0,1},{1,0},{2,3},{3,2},{4,5},{5,4},{6,7},{7,6},{8,9},{9,8},{10,11... | collective-permute-start | bytes 811016 | tf_op jit(solution)/shard_map/ppermute | solution.py:235
  29.6 12.5 %collective-permute-start.8 = (bf16[528,256]{1,0:T(8,128)(2,1)S(1)}, bf16[528,256]{1,0:T(8,128)(2,1)S(1)}, u32[]{:S(2)}, u32[]{:S(2)}) collective-permute-start(bf16[528,256]{1,0:T(8,128)(2,1)S(1)} %collective-permute-done.7.far_own), channel_id=1, source_target_pairs={{0,1},{1,0},{2,3},{3,2},{4,5},{5,4},{6,7},{7,6},{8,9},{9,8},{10,11... | collective-permute-start | bytes 811016 | tf_op jit(solution)/shard_map/ppermute | solution.py:235
  53.5 2.1 %copy-start.3 = (bf16[128,640]{1,0:T(8,128)(2,1)}, bf16[128,640]{1,0:T(8,128)(2,1)S(1)}, u32[]{:S(2)}) copy-start(bf16[128,640]{1,0:T(8,128)(2,1)S(1)} %get-tuple-element.29.c0) | copy-start | bytes 491524
  53.5 2.0 %collective-permute-start.12 = (bf16[1024,256]{1,0:T(8,128)(2,1)S(1)}, bf16[1024,256]{1,0:T(8,128)(2,1)S(1)}, u32[]{:S(2)}, u32[]{:S(2)}) collective-permute-start(bf16[1024,256]{1,0:T(8,128)(2,1)S(1)} %get-tuple-element.34), channel_id=1, source_target_pairs={{0,1},{1,0},{2,3},{3,2},{4,5},{5,4},{6,7},{7,6},{8,9},{9,8},{10,11... | collective-permute-start | bytes 1572872 | tf_op jit(solution)/shard_map/ppermute | solution.py:235
  55.7 26.7 %collective-permute-start.13 = (bf16[512,256]{1,0:T(8,128)(2,1)S(1)}, bf16[512,256]{1,0:T(8,128)(2,1)S(1)}, u32[]{:S(2)}, u32[]{:S(2)}) collective-permute-start(bf16[512,256]{1,0:T(8,128)(2,1)S(1)} %fusion), channel_id=1, source_target_pairs={{8,0},{9,1},{10,2},{11,3},{12,4},{13,5},{14,6},{15,7},{24,16},{25,... | collective-permute-start | bytes 786440 | tf_op jit(solution)/shard_map/ppermute | solution.py:235
  57.0 1.4 %collective-permute-start.17 = (f32[640]{0:T(1024)S(1)}, f32[640]{0:T(1024)S(1)}, u32[]{:S(2)}, u32[]{:S(2)}) collective-permute-start(f32[640]{0:T(1024)S(1)} %reduce), channel_id=1, source_target_pairs={{0,1},{1,0},{2,3},{3,2},{4,5},{5,4},{6,7},{7,6},{8,9},{9,8},{10,11... | collective-permute-start | bytes 7688 | tf_op jit(solution)/shard_map/ppermute | solution.py:235
  58.4 3.7 %collective-permute-start.18 = (f32[640]{0:T(1024)S(1)}, f32[640]{0:T(1024)S(1)}, u32[]{:S(2)}, u32[]{:S(2)}) collective-permute-start(f32[640]{0:T(1024)S(1)} %add_select_fusion), channel_id=1, source_target_pairs={{0,64},{1,65},{2,66},{3,67},{4,68},{5,69},{6,70},{7,71},{16,80},{1... | collective-permute-start | bytes 7688 | tf_op jit(solution)/shard_map/ppermute | solution.py:329
  62.1 4.8 %collective-permute-start.19 = (f32[640]{0:T(1024)S(1)}, f32[640]{0:T(1024)S(1)}, u32[]{:S(2)}, u32[]{:S(2)}) collective-permute-start(f32[640]{0:T(1024)S(1)} %add.37), channel_id=1, source_target_pairs={{0,192},{1,193},{2,194},{3,195},{4,196},{5,197},{6,198},{7,199},{1... | collective-permute-start | bytes 7688 | tf_op jit(solution)/shard_map/ppermute | solution.py:329
  67.0 3.6 %collective-permute-start.20 = (f32[640]{0:T(1024)S(1)}, f32[640]{0:T(1024)S(1)}, u32[]{:S(2)}, u32[]{:S(2)}) collective-permute-start(f32[640]{0:T(1024)S(1)} %add.38), channel_id=1, source_target_pairs={{0,16},{1,17},{2,18},{3,19},{4,20},{5,21},{6,22},{7,23},{16,0},{17... | collective-permute-start | bytes 7688 | tf_op jit(solution)/shard_map/ppermute | solution.py:329
  70.6 10.0 %collective-permute-start.21 = (f32[640]{0:T(1024)S(1)}, f32[640]{0:T(1024)S(1)}, u32[]{:S(2)}, u32[]{:S(2)}) collective-permute-start(f32[640]{0:T(1024)S(1)} %add.39), channel_id=1, source_target_pairs={{0,56},{1,57},{2,58},{3,59},{4,60},{5,61},{6,62},{7,63},{16,32},{1... | collective-permute-start | bytes 7688 | tf_op jit(solution)/shard_map/ppermute | solution.py:329
  75.7 8.3 %collective-permute-start.10 = (bf16[128,640]{1,0:T(8,128)(2,1)S(1)}, bf16[128,640]{1,0:T(8,128)(2,1)S(1)}, u32[]{:S(2)}, u32[]{:S(2)}) collective-permute-start(bf16[128,640]{1,0:T(8,128)(2,1)S(1)} %get-tuple-element.31), channel_id=1, source_target_pairs={{0,4},{1,5},{2,6},{3,7},{4,0},{5,1},{6,2},{7,3},{8,12},{9,13},{10,... | collective-permute-start | bytes 491528 | tf_op jit(solution)/shard_map/ppermute | solution.py:235
  77.3 10.5 %collective-permute-start.11 = (bf16[128,640]{1,0:T(8,128)(2,1)S(1)}, bf16[128,640]{1,0:T(8,128)(2,1)S(1)}, u32[]{:S(2)}, u32[]{:S(2)}) collective-permute-start(bf16[128,640]{1,0:T(8,128)(2,1)S(1)} %get-tuple-element.32), channel_id=1, source_target_pairs={{0,2},{1,3},{2,4},{3,5},{4,6},{5,7},{6,0},{7,1},{8,10},{9,11},{10,... | collective-permute-start | bytes 491528 | tf_op jit(solution)/shard_map/ppermute | solution.py:235
  79.2 10.1 %collective-permute-start.9 = (bf16[128,640]{1,0:T(8,128)(2,1)S(1)}, bf16[128,640]{1,0:T(8,128)(2,1)S(1)}, u32[]{:S(2)}, u32[]{:S(2)}) collective-permute-start(bf16[128,640]{1,0:T(8,128)(2,1)S(1)} %get-tuple-element.30), channel_id=1, source_target_pairs={{0,6},{1,7},{2,0},{3,1},{4,2},{5,3},{6,4},{7,5},{8,14},{9,15},{10,... | collective-permute-start | bytes 491528 | tf_op jit(solution)/shard_map/ppermute | solution.py:235
  80.5 5.4 %collective-permute-start.22 = (f32[640]{0:T(1024)S(1)}, f32[640]{0:T(1024)S(1)}, u32[]{:S(2)}, u32[]{:S(2)}) collective-permute-start(f32[640]{0:T(1024)S(1)} %add.40), channel_id=1, source_target_pairs={{0,48},{1,49},{2,50},{3,51},{4,52},{5,53},{6,54},{7,55},{16,40},{1... | collective-permute-start | bytes 7688 | tf_op jit(solution)/shard_map/ppermute | solution.py:329
  83.2 13.1 %collective-permute-start.14 = (bf16[128,256]{1,0:T(8,128)(2,1)S(1)}, bf16[128,256]{1,0:T(8,128)(2,1)S(1)}, u32[]{:S(2)}, u32[]{:S(2)}) collective-permute-start(bf16[128,256]{1,0:T(8,128)(2,1)S(1)} %get-tuple-element.42), channel_id=1, source_target_pairs={{0,6},{1,7},{2,0},{3,1},{4,2},{5,3},{6,4},{7,5},{8,14},{9,15},{10,... | collective-permute-start | bytes 196616 | tf_op jit(solution)/shard_map/ppermute | solution.py:235
  84.0 7.5 %copy-start.4 = (bf16[128,640]{1,0:T(8,128)(2,1)}, bf16[128,640]{1,0:T(8,128)(2,1)S(1)}, u32[]{:S(2)}) copy-start(bf16[128,640]{1,0:T(8,128)(2,1)S(1)} %collective-permute-done.10.c2) | copy-start | bytes 491524
  84.0 12.3 %collective-permute-start.15 = (bf16[128,256]{1,0:T(8,128)(2,1)S(1)}, bf16[128,256]{1,0:T(8,128)(2,1)S(1)}, u32[]{:S(2)}, u32[]{:S(2)}) collective-permute-start(bf16[128,256]{1,0:T(8,128)(2,1)S(1)} %get-tuple-element.41), channel_id=1, source_target_pairs={{0,4},{1,5},{2,6},{3,7},{4,0},{5,1},{6,2},{7,3},{8,12},{9,13},{10,... | collective-permute-start | bytes 196616 | tf_op jit(solution)/shard_map/ppermute | solution.py:235
  85.9 10.4 %collective-permute-start.16 = (bf16[128,256]{1,0:T(8,128)(2,1)S(1)}, bf16[128,256]{1,0:T(8,128)(2,1)S(1)}, u32[]{:S(2)}, u32[]{:S(2)}) collective-permute-start(bf16[128,256]{1,0:T(8,128)(2,1)S(1)} %get-tuple-element.40), channel_id=1, source_target_pairs={{0,2},{1,3},{2,4},{3,5},{4,6},{5,7},{6,0},{7,1},{8,10},{9,11},{10,... | collective-permute-start | bytes 196616 | tf_op jit(solution)/shard_map/ppermute | solution.py:235
  87.8 5.8 %copy-start.13 = (f32[640]{0:T(1024)}, f32[640]{0:T(1024)S(1)}, u32[]{:S(2)}) copy-start(f32[640]{0:T(1024)S(1)} %add.41.b0) | copy-start | bytes 7684
  87.8 3.7 %copy-start.5 = (bf16[128,640]{1,0:T(8,128)(2,1)}, bf16[128,640]{1,0:T(8,128)(2,1)S(1)}, u32[]{:S(2)}) copy-start(bf16[128,640]{1,0:T(8,128)(2,1)S(1)} %collective-permute-done.11.c3) | copy-start | bytes 491524
  87.8 3.7 %collective-permute-start.23 = (f32[640]{0:T(1024)S(1)}, f32[640]{0:T(1024)S(1)}, u32[]{:S(2)}, u32[]{:S(2)}) collective-permute-start(f32[640]{0:T(1024)S(1)} %add.41.b0), channel_id=1, source_target_pairs={{0,6},{1,7},{2,0},{3,1},{4,2},{5,3},{6,4},{7,5},{8,14},{9,15},{10,... | collective-permute-start | bytes 7688 | tf_op jit(solution)/shard_map/ppermute | solution.py:235
  89.3 2.2 %copy-start.6 = (bf16[128,640]{1,0:T(8,128)(2,1)}, bf16[128,640]{1,0:T(8,128)(2,1)S(1)}, u32[]{:S(2)}) copy-start(bf16[128,640]{1,0:T(8,128)(2,1)S(1)} %collective-permute-done.9.c1) | copy-start | bytes 491524
  89.3 5.1 %collective-permute-start.24 = (f32[640]{0:T(1024)S(1)}, f32[640]{0:T(1024)S(1)}, u32[]{:S(2)}, u32[]{:S(2)}) collective-permute-start(f32[640]{0:T(1024)S(1)} %add.41.b0), channel_id=1, source_target_pairs={{0,4},{1,5},{2,6},{3,7},{4,0},{5,1},{6,2},{7,3},{8,12},{9,13},{10,... | collective-permute-start | bytes 7688 | tf_op jit(solution)/shard_map/ppermute | solution.py:235
  91.5 2.1 %copy-start.14 = (f32[640]{0:T(1024)}, f32[640]{0:T(1024)S(1)}, u32[]{:S(2)}) copy-start(f32[640]{0:T(1024)S(1)} %collective-permute-done.23.b1) | copy-start | bytes 7684
  91.5 4.8 %collective-permute-start.25 = (f32[640]{0:T(1024)S(1)}, f32[640]{0:T(1024)S(1)}, u32[]{:S(2)}, u32[]{:S(2)}) collective-permute-start(f32[640]{0:T(1024)S(1)} %add.41.b0), channel_id=1, source_target_pairs={{0,2},{1,3},{2,4},{3,5},{4,6},{5,7},{6,0},{7,1},{8,10},{9,11},{10,... | collective-permute-start | bytes 7688 | tf_op jit(solution)/shard_map/ppermute | solution.py:235
  94.4 1.9 %copy-start.15 = (f32[640]{0:T(1024)}, f32[640]{0:T(1024)S(1)}, u32[]{:S(2)}) copy-start(f32[640]{0:T(1024)S(1)} %collective-permute-done.24.b2) | copy-start | bytes 7684
  96.3 0.6 copy-start.16
  96.3 0.6 copy-start.10
  96.3 0.6 copy-start.11
  96.3 0.7 copy-start.12

commit v3 on v2

--- a/solution.py
+++ b/solution.py
@@ -42,8 +42,7 @@
 
 
 SWAP = pairs(lambda z, y, c: (z, y, 1 - c))
-UP = pairs(lambda z, y, c: (1, y, c) if z == 0 else None)
-DOWN = pairs(lambda z, y, c: (0, y, c) if z == 1 else None)
+ACROSS = pairs(lambda z, y, c: (1 - z, y, c))
 
 
 def shift(k):
@@ -64,7 +63,7 @@
         out[ROWS:, HD:] = ids
 
 
-def bundle_kernel(l0, l1, l2, l3, out):
+def bundle_kernel(l0, l1, l2, l3, after_ref, out):
     lines = (l0, l1, l2, l3)
     for k, line in enumerate(lines):
         out[k * ROWS : (k + 1) * ROWS, :] = line[0:ROWS, :]
@@ -97,7 +96,7 @@
 def attention_kernel(
     q_ref, g_ref, g1, g2, g3, near_own, near_sib, far_own, far_sib,
     dq0, dq1, dq2, dq3, bias_ref, sib_ref, far_ref, near_ref,
-    qs, gs, kv, kt, s_ref, dp_ref, peaks, dk_acc, dv_acc, dq_acc, starts, lows,
+    qs, gs, kv, s_ref, dp_ref, peaks, dk_acc, dv_acc, dq_acc, starts, lows,
 ):
     z, y, core = place()
 
@@ -113,7 +112,6 @@
                 gs[k, rows, :] = ref[:, GCOLS + h * HD : GCOLS + (h + 1) * HD]
 
     kv[0] = jnp.zeros((ROWS, 2 * HD), bf16)
-    kt[0] = jnp.zeros((HD, ROWS), bf16)
 
     sources = ((far_own, 0, core), (far_sib, 0, 1 - core), (near_own, 1, core), (near_sib, 1, 1 - core))
     for ref, half, parity in sources:
@@ -121,7 +119,6 @@
             at = 1 + half * 8 + 2 * lax.rem(y - k + CHIPS, CHIPS) + parity
             chunk = ref[k * ROWS : (k + 1) * ROWS, :]
             kv[at] = chunk
-            kt[at] = chunk[:, 0:HD].astype(f32).T.astype(bf16)
     dk_acc[...] = jnp.zeros(dk_acc.shape, f32)
     dv_acc[...] = jnp.zeros(dv_acc.shape, f32)
 
@@ -182,15 +179,14 @@
             dk = dot_nn(score_grad, query)
             dv_acc[pl.ds(base, 2)] += dv.reshape(2, ROWS, HD)
             dk_acc[pl.ds(base, 2)] += dk.reshape(2, ROWS, HD)
-            dq_acc[...] += dot_nn(kt[base], score_grad[0:ROWS]) + dot_nn(
-                kt[base + 1], score_grad[ROWS:]
-            )
+            keys = kv[pl.ds(base, 2), :, 0:HD].reshape(2 * ROWS, HD)
+            dq_acc[...] += lax.dot_general(score_grad, keys, (((0,), (0,)), ((), ())), preferred_element_type=f32)
             return 0
 
         lax.fori_loop(0, amount, third, 0)
         bias_rows = []
         for h in range(GROUP):
-            dq = dq_acc[:, h * ROWS : (h + 1) * ROWS].T * INV_ROOT
+            dq = dq_acc[h * ROWS : (h + 1) * ROWS] * INV_ROOT
             bias_rows.append(jnp.sum(dq, axis=0, keepdims=True))
             for j, out in enumerate((dq0, dq1, dq2, dq3)):
 
@@ -265,18 +261,21 @@
     lines = pl.pallas_call(
         pack_kv_kernel, out_shape=[shape((LINE, 2 * HD), bf16)] * CHIPS, name="pack_kv"
     )(key_rows, value_rows, doc_ids)
-    lines = [lines[0]] + [move(lines[k], shift(k)) for k in (1, 2, 3)]
-    near = pl.pallas_call(bundle_kernel, out_shape=shape((BUNDLE, 2 * HD), bf16), name="bundle")(
-        *lines
-    )
-    far = move(near, UP)
-    near_sib = move(near, SWAP)
     qg = pl.pallas_call(
         pack_qg_kernel,
         out_shape=[shape((ROWS, 2 * GCOLS), bf16)] * 3,
         in_specs=[vmem, vmem, anywhere],
         name="pack_qg",
-    )(query_rows, out_grad, near)
+    )(query_rows, out_grad, lines[0])
+    lines = [lines[0]] + [move(lines[k], shift(k)) for k in (1, 2, 3)]
+    near = pl.pallas_call(
+        bundle_kernel,
+        out_shape=shape((BUNDLE, 2 * HD), bf16),
+        in_specs=[vmem] * 4 + [anywhere],
+        name="bundle",
+    )(*lines, qg[0])
+    far = move(near, ACROSS)
+    near_sib = move(near, SWAP)
     qg = [move(qg[k - 1], shift(k)) for k in (1, 2, 3)]
     far_sib = move(far, SWAP)
 
@@ -294,17 +293,16 @@
             pltpu.VMEM((CHIPS, LANES, HD), bf16),
             pltpu.VMEM((CHIPS, LANES, HD), bf16),
             pltpu.VMEM((CHUNKS + 1, ROWS, 2 * HD), bf16),
-            pltpu.VMEM((CHUNKS + 1, HD, ROWS), bf16),
             pltpu.VMEM((BLOCKS, 2 * ROWS, LANES), f32),
             pltpu.VMEM((BLOCKS, 2 * ROWS, LANES), f32),
             pltpu.VMEM((BLOCKS, 8, LANES), f32),
             pltpu.VMEM((CHUNKS + 1, ROWS, HD), f32),
             pltpu.VMEM((CHUNKS + 1, ROWS, HD), f32),
-            pltpu.VMEM((HD, LANES), f32),
+            pltpu.VMEM((LANES, HD), f32),
             pltpu.VMEM((CHIPS, 8, ROWS), jnp.int32),
             pltpu.SMEM((CHIPS,), jnp.int32),
         ],
-        compiler_params=pltpu.CompilerParams(vmem_limit_bytes=32 * 1024 * 1024),
+        compiler_params=pltpu.CompilerParams(vmem_limit_bytes=24 * 1024 * 1024),
         name="attention",
     )(query_rows, out_grad, *qg, near, near_sib, far, far_sib)
     dq, bias = outs[:CHIPS], outs[CHIPS][0]
@@ -313,7 +311,7 @@
     sib = move(to_sib, SWAP).astype(f32)
     half_rows = CHIPS * ROWS
     far_sum = (far_part + sib[:half_rows]).astype(bf16)
-    down = move(far_sum, DOWN)
+    down = move(far_sum, ACROSS)
     dq = [dq[0]] + [move(dq[k], shift(-k)) for k in (1, 2, 3)]
     kv_grad = (near_part + sib[half_rows:] + down.astype(f32)).astype(bf16)
     kv_grad = [kv_grad[k * ROWS : (k + 1) * ROWS] for k in range(CHIPS)]

time: 98.8 us -> 92.6 us (0.937); the launches traced: 98.7 us -> 90.9 us
  waiting for transfers between devices: 33.4 us -> 26.3 us
  Pallas kernels: 20.8 us -> 16.8 us
  starting transfers between devices: 40.2 us -> 42.5 us
    ppermute x21, waiting for transfers between devices: 21.4 us -> 17.1 us  [move(): return lax.ppermute(array, 'ctx', table)]
    ppermute x21, starting transfers between devices: 33.1 us -> 37.3 us  [move(): return lax.ppermute(array, 'ctx', table)]
    pallas_call x1, Pallas kernels: 11.3 us -> 7.26 us  [body(): pl.pallas_call(attention_kernel, out_shape=(*[shape((ROWS, GCOLS), bf16)]...]
    ppermute x5, waiting for transfers between devices: 12 us -> 9.28 us  [body(): bias = bias + lax.ppermute(bias, ('dp', 'ctx'), table)]
    ppermute x5, starting transfers between devices: 7.12 us -> 5.25 us  [body(): bias = bias + lax.ppermute(bias, ('dp', 'ctx'), table)]
  transfers between devices with their start and end apart: 26 -> 26, of which waited for: 12 -> 10; matrix products, arithmetic and copies ran while one was open for 1% -> 1% of each run, Pallas kernels for 4% -> 5%
where the time goes in v3:
time: 92.6 us; the launch traced here: 90.9 us
  starting transfers between devices  42.5 us (46%)
  waiting for transfers between devices  26.3 us (28%)
  Pallas kernels  16.8 us (18%)
  local copies, waits for them, and re-layouts  3.4 us (4%)
  between operations  1.51 us (2%)
    ppermute x21, starting transfers between devices, move(): return lax.ppermute(array, 'ctx', table)  37.3 us
    ppermute x21, waiting for transfers between devices, move(): return lax.ppermute(array, 'ctx', table)  17.1 us
    ppermute x5, waiting for transfers between devices, body(): bias = bias + lax.ppermute(bias, ('dp', 'ctx'), table)  9.28 us
    pallas_call x1, Pallas kernels, body(): pl.pallas_call(attention_kernel, out_shape=(*[shape((ROWS, GCOLS), bf16)]...  7.26 us
    ppermute x5, starting transfers between devices, body(): bias = bias + lax.ppermute(bias, ('dp', 'ctx'), table)  5.25 us
    pallas_call x1, Pallas kernels, body(): pl.pallas_call(pack_qg_kernel, out_shape=[shape((ROWS, 2 * GCOLS), bf16)]...  2.36 us
    unnamed x34, local copies, waits for them, and re-layouts  2.25 us
    pallas_call x1, Pallas kernels, body(): pl.pallas_call(place_q_kernel, out_shape=shape(query_rows.shape, bf16), n...  2.07 us
  transfers between devices with their start and end apart: 26, of which 10 were waited for; matrix products, arithmetic and copies ran while one was open for 1% of the time, Pallas kernels for 5%

profile of v3, /device:TPU:6, one launch (start us, length us, event | category | flops | bytes accessed | tf_op | source)
XLA Modules:
  0.0 90.9 jit_solution(5227147762758277053)
XLA Ops:
  0.6 1.7 %pack_kv.1 = (bf16[144,256]{1,0:T(8,128)(2,1)}, bf16[144,256]{1,0:T(8,128)(2,1)}, bf16[144,256]{1,0:T(8,128)(2,1)}, bf16[144,256]{1,0:T(8,128)(2,1)}) custom-call(bf16[1,128,512]{2,1,0:T(8,128)(2,1)} %k_ref.1, bf16[1,128,512]{2,1,0:T(8,128)(2,1)} %v_ref.1, s32[1,128]{1,0:T(1,128)} %ids_ref.1), custom_call_target="tpu_custom_call" | custom-call | tf_op jit(solution)/shard_map/pack_kv/pallas_call | solution.py:261
  2.4 1.6 %collective-permute-start.3 = (bf16[144,256]{1,0:T(8,128)(2,1)}, bf16[144,256]{1,0:T(8,128)(2,1)S(1)}, u32[]{:S(2)}, u32[]{:S(2)}) collective-permute-start(bf16[144,256]{1,0:T(8,128)(2,1)} %get-tuple-element.26), channel_id=1, source_target_pairs={{0,2},{1,3},{2,4},{3,5},{4,6},{5,7},{6,0},{7,1},{8,10},{9,11},{10,... | collective-permute-start | bytes 221192 | tf_op jit(solution)/shard_map/ppermute | solution.py:231
  3.9 2.9 %collective-permute-start.4 = (bf16[144,256]{1,0:T(8,128)(2,1)}, bf16[144,256]{1,0:T(8,128)(2,1)S(1)}, u32[]{:S(2)}, u32[]{:S(2)}) collective-permute-start(bf16[144,256]{1,0:T(8,128)(2,1)} %get-tuple-element.27), channel_id=1, source_target_pairs={{0,4},{1,5},{2,6},{3,7},{4,0},{5,1},{6,2},{7,3},{8,12},{9,13},{10,... | collective-permute-start | bytes 221192 | tf_op jit(solution)/shard_map/ppermute | solution.py:231
  6.8 1.3 %collective-permute-start.5 = (bf16[144,256]{1,0:T(8,128)(2,1)}, bf16[144,256]{1,0:T(8,128)(2,1)S(1)}, u32[]{:S(2)}, u32[]{:S(2)}) collective-permute-start(bf16[144,256]{1,0:T(8,128)(2,1)} %get-tuple-element.28), channel_id=1, source_target_pairs={{0,6},{1,7},{2,0},{3,1},{4,2},{5,3},{6,4},{7,5},{8,14},{9,15},{10,... | collective-permute-start | bytes 221192 | tf_op jit(solution)/shard_map/ppermute | solution.py:231
  8.2 2.4 %pack_qg.1 = (bf16[128,1280]{1,0:T(8,128)(2,1)}, bf16[128,1280]{1,0:T(8,128)(2,1)}, bf16[128,1280]{1,0:T(8,128)(2,1)}) custom-call(bf16[1,128,2560]{2,1,0:T(8,128)(2,1)} %q_ref.3, bf16[1,128,2560]{2,1,0:T(8,128)(2,1)} %g_ref.3, bf16[144,256]{1,0:T(8,128)(2,1)} %get-tuple-element.22.after_ref.l0), custom_call_target="tpu_custom_call" | custom-call | tf_op jit(solution)/shard_map/pack_qg/pallas_call | solution.py:264
  10.6 0.0 collective-permute-done.4.l2
  10.6 0.8 collective-permute-done.5.l3
  11.4 0.6 copy-done.9
  12.0 1.7 %bundle.1.near_own = bf16[528,256]{1,0:T(8,128)(2,1)} custom-call(bf16[144,256]{1,0:T(8,128)(2,1)} %get-tuple-element.22.after_ref.l0, bf16[144,256]{1,0:T(8,128)(2,1)} %copy-done.7, bf16[144,256]{1,0:T(8,128)(2,1)} %copy-done.8, bf16[144,256]{1,0:T(8,128)(2,1)} %copy-done.9, bf16[128,1280]{1,0:T(8,128)(2,1)} %get-tuple-element.23.after_ref), custom_call_target="tpu_custom_call" | custom-call | tf_op jit(solution)/shard_map/bundle/pallas_call | solution.py:271
  13.7 7.2 %collective-permute-start.7 = (bf16[528,256]{1,0:T(8,128)(2,1)}, bf16[528,256]{1,0:T(8,128)(2,1)S(1)}, u32[]{:S(2)}, u32[]{:S(2)}) collective-permute-start(bf16[528,256]{1,0:T(8,128)(2,1)} %bundle.1.near_own), channel_id=1, source_target_pairs={{0,8},{1,9},{2,10},{3,11},{4,12},{5,13},{6,14},{7,15},{8,0},{9,1},... | collective-permute-start | bytes 811016 | tf_op jit(solution)/shard_map/ppermute | solution.py:231
  20.9 0.4 collective-permute-start
  21.4 3.6 %collective-permute-start.1 = (bf16[128,1280]{1,0:T(8,128)(2,1)}, bf16[128,1280]{1,0:T(8,128)(2,1)S(1)}, u32[]{:S(2)}, u32[]{:S(2)}) collective-permute-start(bf16[128,1280]{1,0:T(8,128)(2,1)} %get-tuple-element.24), channel_id=1, source_target_pairs={{0,4},{1,5},{2,6},{3,7},{4,0},{5,1},{6,2},{7,3},{8,12},{9,13},{10,... | collective-permute-start | bytes 983048 | tf_op jit(solution)/shard_map/ppermute | solution.py:231
  25.0 0.3 collective-permute-start.2
  25.3 2.1 %collective-permute-done.7.far_own = bf16[528,256]{1,0:T(8,128)(2,1)S(1)} collective-permute-done((bf16[528,256]{1,0:T(8,128)(2,1)}, bf16[528,256]{1,0:T(8,128)(2,1)S(1)}, u32[]{:S(2)}, u32[]{:S(2)}) %collective-permute-start.7) | collective-permute-done | bytes 270368 | tf_op jit(solution)/shard_map/ppermute | solution.py:231
  27.4 5.2 %collective-permute-done.g1 = bf16[128,1280]{1,0:T(8,128)(2,1)S(1)} collective-permute-done((bf16[128,1280]{1,0:T(8,128)(2,1)}, bf16[128,1280]{1,0:T(8,128)(2,1)S(1)}, u32[]{:S(2)}, u32[]{:S(2)}) %collective-permute-start) | collective-permute-done | bytes 327712 | tf_op jit(solution)/shard_map/ppermute | solution.py:231
  32.6 5.2 %collective-permute-done.1.g2 = bf16[128,1280]{1,0:T(8,128)(2,1)S(1)} collective-permute-done((bf16[128,1280]{1,0:T(8,128)(2,1)}, bf16[128,1280]{1,0:T(8,128)(2,1)S(1)}, u32[]{:S(2)}, u32[]{:S(2)}) %collective-permute-start.1) | collective-permute-done | bytes 327712 | tf_op jit(solution)/shard_map/ppermute | solution.py:231
  37.9 0.9 %copy-done.2 = bf16[528,256]{1,0:T(8,128)(2,1)S(1)} copy-done((bf16[528,256]{1,0:T(8,128)(2,1)S(1)}, bf16[528,256]{1,0:T(8,128)(2,1)}, u32[]{:S(2)}) %copy-start.2) | copy-done | bytes 270360
  38.8 7.3 %attention.1 = (bf16[128,640]{1,0:T(8,128)(2,1)S(1)}, bf16[128,640]{1,0:T(8,128)(2,1)S(1)}, bf16[128,640]{1,0:T(8,128)(2,1)S(1)}, bf16[128,640]{1,0:T(8,128)(2,1...) custom-call(bf16[1,128,2560]{2,1,0:T(8,128)(2,1)S(1)} %copy-done, ...), custom_call_target="tpu_custom_call" | custom-call | tf_op jit(solution)/shard_map/attention/pallas_call | solution.py:283
  46.1 0.1 collective-permute-start.12
  46.2 1.9 %collective-permute-done.12 = bf16[1024,256]{1,0:T(8,128)(2,1)S(1)} collective-permute-done((bf16[1024,256]{1,0:T(8,128)(2,1)S(1)}, bf16[1024,256]{1,0:T(8,128)(2,1)S(1)}, u32[]{:S(2)}, u32[]{:S(2)}) %collective-permute-start.12) | collective-permute-done | bytes 524320 | tf_op jit(solution)/shard_map/ppermute | solution.py:231
  48.1 0.1 convert_element_type.18
  48.2 0.1 fusion
  48.2 5.6 %collective-permute-start.13 = (bf16[512,256]{1,0:T(8,128)(2,1)S(1)}, bf16[512,256]{1,0:T(8,128)(2,1)S(1)}, u32[]{:S(2)}, u32[]{:S(2)}) collective-permute-start(bf16[512,256]{1,0:T(8,128)(2,1)S(1)} %fusion), channel_id=1, source_target_pairs={{0,8},{1,9},{2,10},{3,11},{4,12},{5,13},{6,14},{7,15},{8,0},{9,1},... | collective-permute-start | bytes 786440 | tf_op jit(solution)/shard_map/ppermute | solution.py:231
  53.9 0.1 collective-permute-start.17
  54.0 0.5 slice.34
  55.2 0.9 collective-permute-start.18
  56.1 2.8 %collective-permute-done.18 = f32[640]{0:T(1024)S(1)} collective-permute-done((f32[640]{0:T(1024)S(1)}, f32[640]{0:T(1024)S(1)}, u32[]{:S(2)}, u32[]{:S(2)}) %collective-permute-start.18) | collective-permute-done | bytes 2592 | tf_op jit(solution)/shard_map/ppermute | solution.py:327
  58.9 4.8 %collective-permute-done.19 = f32[640]{0:T(1024)S(1)} collective-permute-done((f32[640]{0:T(1024)S(1)}, f32[640]{0:T(1024)S(1)}, u32[]{:S(2)}, u32[]{:S(2)}) %collective-permute-start.19) | collective-permute-done | bytes 2592 | tf_op jit(solution)/shard_map/ppermute | solution.py:327
  63.8 2.5 %collective-permute-start.20 = (f32[640]{0:T(1024)S(1)}, f32[640]{0:T(1024)S(1)}, u32[]{:S(2)}, u32[]{:S(2)}) collective-permute-start(f32[640]{0:T(1024)S(1)} %add.38), channel_id=1, source_target_pairs={{0,16},{1,17},{2,18},{3,19},{4,20},{5,21},{6,22},{7,23},{16,0},{17... | collective-permute-start | bytes 7688 | tf_op jit(solution)/shard_map/ppermute | solution.py:327
  66.2 1.7 %collective-permute-done.20 = f32[640]{0:T(1024)S(1)} collective-permute-done((f32[640]{0:T(1024)S(1)}, f32[640]{0:T(1024)S(1)}, u32[]{:S(2)}, u32[]{:S(2)}) %collective-permute-start.20) | collective-permute-done | bytes 2592 | tf_op jit(solution)/shard_map/ppermute | solution.py:327
  67.9 1.6 %collective-permute-start.10 = (bf16[128,640]{1,0:T(8,128)(2,1)S(1)}, bf16[128,640]{1,0:T(8,128)(2,1)S(1)}, u32[]{:S(2)}, u32[]{:S(2)}) collective-permute-start(bf16[128,640]{1,0:T(8,128)(2,1)S(1)} %get-tuple-element.31), channel_id=1, source_target_pairs={{0,4},{1,5},{2,6},{3,7},{4,0},{5,1},{6,2},{7,3},{8,12},{9,13},{10,... | collective-permute-start | bytes 491528 | tf_op jit(solution)/shard_map/ppermute | solution.py:231
  69.5 1.9 %collective-permute-start.11 = (bf16[128,640]{1,0:T(8,128)(2,1)S(1)}, bf16[128,640]{1,0:T(8,128)(2,1)S(1)}, u32[]{:S(2)}, u32[]{:S(2)}) collective-permute-start(bf16[128,640]{1,0:T(8,128)(2,1)S(1)} %get-tuple-element.32), channel_id=1, source_target_pairs={{0,2},{1,3},{2,4},{3,5},{4,6},{5,7},{6,0},{7,1},{8,10},{9,11},{10,... | collective-permute-start | bytes 491528 | tf_op jit(solution)/shard_map/ppermute | solution.py:231
  71.4 1.3 %collective-permute-start.9 = (bf16[128,640]{1,0:T(8,128)(2,1)S(1)}, bf16[128,640]{1,0:T(8,128)(2,1)S(1)}, u32[]{:S(2)}, u32[]{:S(2)}) collective-permute-start(bf16[128,640]{1,0:T(8,128)(2,1)S(1)} %get-tuple-element.30), channel_id=1, source_target_pairs={{0,6},{1,7},{2,0},{3,1},{4,2},{5,3},{6,4},{7,5},{8,14},{9,15},{10,... | collective-permute-start | bytes 491528 | tf_op jit(solution)/shard_map/ppermute | solution.py:231
  72.7 1.9 %collective-permute-start.22 = (f32[640]{0:T(1024)S(1)}, f32[640]{0:T(1024)S(1)}, u32[]{:S(2)}, u32[]{:S(2)}) collective-permute-start(f32[640]{0:T(1024)S(1)} %add.40), channel_id=1, source_target_pairs={{0,48},{1,49},{2,50},{3,51},{4,52},{5,53},{6,54},{7,55},{16,40},{1... | collective-permute-start | bytes 7688 | tf_op jit(solution)/shard_map/ppermute | solution.py:327
  74.6 0.1 fusion.2
  74.7 0.6 fusion.3
  75.4 2.3 %collective-permute-start.14 = (bf16[128,256]{1,0:T(8,128)(2,1)S(1)}, bf16[128,256]{1,0:T(8,128)(2,1)S(1)}, u32[]{:S(2)}, u32[]{:S(2)}) collective-permute-start(bf16[128,256]{1,0:T(8,128)(2,1)S(1)} %get-tuple-element.42), channel_id=1, source_target_pairs={{0,6},{1,7},{2,0},{3,1},{4,2},{5,3},{6,4},{7,5},{8,14},{9,15},{10,... | collective-permute-start | bytes 196616 | tf_op jit(solution)/shard_map/ppermute | solution.py:231
  77.7 0.5 collective-permute-start.15
  78.2 1.8 %collective-permute-start.16 = (bf16[128,256]{1,0:T(8,128)(2,1)S(1)}, bf16[128,256]{1,0:T(8,128)(2,1)S(1)}, u32[]{:S(2)}, u32[]{:S(2)}) collective-permute-start(bf16[128,256]{1,0:T(8,128)(2,1)S(1)} %get-tuple-element.40), channel_id=1, source_target_pairs={{0,2},{1,3},{2,4},{3,5},{4,6},{5,7},{6,0},{7,1},{8,10},{9,11},{10,... | collective-permute-start | bytes 196616 | tf_op jit(solution)/shard_map/ppermute | solution.py:231
  80.0 1.5 %collective-permute-start.23 = (f32[640]{0:T(1024)S(1)}, f32[640]{0:T(1024)S(1)}, u32[]{:S(2)}, u32[]{:S(2)}) collective-permute-start(f32[640]{0:T(1024)S(1)} %add.41.b0), channel_id=1, source_target_pairs={{0,6},{1,7},{2,0},{3,1},{4,2},{5,3},{6,4},{7,5},{8,14},{9,15},{10,... | collective-permute-start | bytes 7688 | tf_op jit(solution)/shard_map/ppermute | solution.py:231
  81.5 1.9 %collective-permute-start.24 = (f32[640]{0:T(1024)S(1)}, f32[640]{0:T(1024)S(1)}, u32[]{:S(2)}, u32[]{:S(2)}) collective-permute-start(f32[640]{0:T(1024)S(1)} %add.41.b0), channel_id=1, source_target_pairs={{0,4},{1,5},{2,6},{3,7},{4,0},{5,1},{6,2},{7,3},{8,12},{9,13},{10,... | collective-permute-start | bytes 7688 | tf_op jit(solution)/shard_map/ppermute | solution.py:231
  83.4 0.3 collective-permute-done.23.b1
  83.7 1.2 %collective-permute-start.25 = (f32[640]{0:T(1024)S(1)}, f32[640]{0:T(1024)S(1)}, u32[]{:S(2)}, u32[]{:S(2)}) collective-permute-start(f32[640]{0:T(1024)S(1)} %add.41.b0), channel_id=1, source_target_pairs={{0,2},{1,3},{2,4},{3,5},{4,6},{5,7},{6,0},{7,1},{8,10},{9,11},{10,... | collective-permute-start | bytes 7688 | tf_op jit(solution)/shard_map/ppermute | solution.py:231
  84.9 2.1 %place_q.1 = bf16[1,128,2560]{2,1,0:T(8,128)(2,1)} custom-call(bf16[128,640]{1,0:T(8,128)(2,1)} %copy-done.3, bf16[128,640]{1,0:T(8,128)(2,1)} %copy-done.6, bf16[128,640]{1,0:T(8,128)(2,1)} %copy-done.4, bf16[128,640]{1,0:T(8,128)(2,1)} %copy-done.5), custom_call_target="tpu_custom_call" | custom-call | tf_op jit(solution)/shard_map/place_q/pallas_call | solution.py:320
  87.0 1.5 %collective-permute-done.25.b3 = f32[640]{0:T(1024)S(1)} collective-permute-done((f32[640]{0:T(1024)S(1)}, f32[640]{0:T(1024)S(1)}, u32[]{:S(2)}, u32[]{:S(2)}) %collective-permute-start.25) | collective-permute-done | bytes 2592 | tf_op jit(solution)/shard_map/ppermute | solution.py:231
  88.6 0.5 copy-done.16
  89.2 0.0 copy-done.12
  89.2 1.7 %place.1 = (bf16[1,128,512]{2,1,0:T(8,128)(2,1)}, bf16[1,128,512]{2,1,0:T(8,128)(2,1)}, f32[2560]{0:T(1024)}) custom-call(bf16[128,256]{1,0:T(8,128)(2,1)} %get-tuple-element.43.c0, bf16[128,256]{1,0:T(8,128)(2,1)} %copy-done.10, bf16[128,256]{1,0:T(8,128)(2,1)} %copy-done.11, bf16[128,256]{1,0:T(8,128)(2,1)} %copy-done.12, f32[640]{0:T(1024)} %copy-done.13, ...), custom_call_target="tpu_custom_call" | custom-call | tf_op jit(solution)/shard_map/place/pallas_call | solution.py:329
  (56 shorter events, 0.2 us)
Async XLA Ops:
  2.4 8.2 %collective-permute-start.3 = (bf16[144,256]{1,0:T(8,128)(2,1)}, bf16[144,256]{1,0:T(8,128)(2,1)S(1)}, u32[]{:S(2)}, u32[]{:S(2)}) collective-permute-start(bf16[144,256]{1,0:T(8,128)(2,1)} %get-tuple-element.26), channel_id=1, source_target_pairs={{0,2},{1,3},{2,4},{3,5},{4,6},{5,7},{6,0},{7,1},{8,10},{9,11},{10,... | collective-permute-start | bytes 221192 | tf_op jit(solution)/shard_map/ppermute | solution.py:231
  3.9 6.7 %collective-permute-start.4 = (bf16[144,256]{1,0:T(8,128)(2,1)}, bf16[144,256]{1,0:T(8,128)(2,1)S(1)}, u32[]{:S(2)}, u32[]{:S(2)}) collective-permute-start(bf16[144,256]{1,0:T(8,128)(2,1)} %get-tuple-element.27), channel_id=1, source_target_pairs={{0,4},{1,5},{2,6},{3,7},{4,0},{5,1},{6,2},{7,3},{8,12},{9,13},{10,... | collective-permute-start | bytes 221192 | tf_op jit(solution)/shard_map/ppermute | solution.py:231
  6.8 4.6 %collective-permute-start.5 = (bf16[144,256]{1,0:T(8,128)(2,1)}, bf16[144,256]{1,0:T(8,128)(2,1)S(1)}, u32[]{:S(2)}, u32[]{:S(2)}) collective-permute-start(bf16[144,256]{1,0:T(8,128)(2,1)} %get-tuple-element.28), channel_id=1, source_target_pairs={{0,6},{1,7},{2,0},{3,1},{4,2},{5,3},{6,4},{7,5},{8,14},{9,15},{10,... | collective-permute-start | bytes 221192 | tf_op jit(solution)/shard_map/ppermute | solution.py:231
  8.2 29.7 %copy-start.1 = (bf16[1,128,2560]{2,1,0:T(8,128)(2,1)S(1)}, bf16[1,128,2560]{2,1,0:T(8,128)(2,1)}, u32[]{:S(2)}) copy-start(bf16[1,128,2560]{2,1,0:T(8,128)(2,1)} %g_ref.3) | copy-start | bytes 1966084
  10.5 27.3 %copy-start = (bf16[1,128,2560]{2,1,0:T(8,128)(2,1)S(1)}, bf16[1,128,2560]{2,1,0:T(8,128)(2,1)}, u32[]{:S(2)}) copy-start(bf16[1,128,2560]{2,1,0:T(8,128)(2,1)} %q_ref.3) | copy-start | bytes 1966084
  10.5 0.9 copy-start.7
  10.6 0.8 copy-start.8
  11.4 0.6 copy-start.9
  13.7 13.7 %collective-permute-start.7 = (bf16[528,256]{1,0:T(8,128)(2,1)}, bf16[528,256]{1,0:T(8,128)(2,1)S(1)}, u32[]{:S(2)}, u32[]{:S(2)}) collective-permute-start(bf16[528,256]{1,0:T(8,128)(2,1)} %bundle.1.near_own), channel_id=1, source_target_pairs={{0,8},{1,9},{2,10},{3,11},{4,12},{5,13},{6,14},{7,15},{8,0},{9,1},... | collective-permute-start | bytes 811016 | tf_op jit(solution)/shard_map/ppermute | solution.py:231
  20.9 11.6 %collective-permute-start = (bf16[128,1280]{1,0:T(8,128)(2,1)}, bf16[128,1280]{1,0:T(8,128)(2,1)S(1)}, u32[]{:S(2)}, u32[]{:S(2)}) collective-permute-start(bf16[128,1280]{1,0:T(8,128)(2,1)} %get-tuple-element.23.after_ref), channel_id=1, source_target_pairs={{0,2},{1,3},{2,4},{3,5},{4,6},{5,7},{6,0},{7,1},{8,10},{9,11},{10,... | collective-permute-start | bytes 983048 | tf_op jit(solution)/shard_map/ppermute | solution.py:231
  21.4 16.4 %collective-permute-start.1 = (bf16[128,1280]{1,0:T(8,128)(2,1)}, bf16[128,1280]{1,0:T(8,128)(2,1)S(1)}, u32[]{:S(2)}, u32[]{:S(2)}) collective-permute-start(bf16[128,1280]{1,0:T(8,128)(2,1)} %get-tuple-element.24), channel_id=1, source_target_pairs={{0,4},{1,5},{2,6},{3,7},{4,0},{5,1},{6,2},{7,3},{8,12},{9,13},{10,... | collective-permute-start | bytes 983048 | tf_op jit(solution)/shard_map/ppermute | solution.py:231
  25.0 12.9 %collective-permute-start.2 = (bf16[128,1280]{1,0:T(8,128)(2,1)}, bf16[128,1280]{1,0:T(8,128)(2,1)S(1)}, u32[]{:S(2)}, u32[]{:S(2)}) collective-permute-start(bf16[128,1280]{1,0:T(8,128)(2,1)} %get-tuple-element.25), channel_id=1, source_target_pairs={{0,6},{1,7},{2,0},{3,1},{4,2},{5,3},{6,4},{7,5},{8,14},{9,15},{10,... | collective-permute-start | bytes 983048 | tf_op jit(solution)/shard_map/ppermute | solution.py:231
  25.3 12.5 %collective-permute-start.6 = (bf16[528,256]{1,0:T(8,128)(2,1)}, bf16[528,256]{1,0:T(8,128)(2,1)S(1)}, u32[]{:S(2)}, u32[]{:S(2)}) collective-permute-start(bf16[528,256]{1,0:T(8,128)(2,1)} %bundle.1.near_own), channel_id=1, source_target_pairs={{0,1},{1,0},{2,3},{3,2},{4,5},{5,4},{6,7},{7,6},{8,9},{9,8},{10,11... | collective-permute-start | bytes 811016 | tf_op jit(solution)/shard_map/ppermute | solution.py:231
  27.4 10.4 %collective-permute-start.8 = (bf16[528,256]{1,0:T(8,128)(2,1)S(1)}, bf16[528,256]{1,0:T(8,128)(2,1)S(1)}, u32[]{:S(2)}, u32[]{:S(2)}) collective-permute-start(bf16[528,256]{1,0:T(8,128)(2,1)S(1)} %collective-permute-done.7.far_own), channel_id=1, source_target_pairs={{0,1},{1,0},{2,3},{3,2},{4,5},{5,4},{6,7},{7,6},{8,9},{9,8},{10,11... | collective-permute-start | bytes 811016 | tf_op jit(solution)/shard_map/ppermute | solution.py:231
  37.8 1.0 %copy-start.2 = (bf16[528,256]{1,0:T(8,128)(2,1)S(1)}, bf16[528,256]{1,0:T(8,128)(2,1)}, u32[]{:S(2)}) copy-start(bf16[528,256]{1,0:T(8,128)(2,1)} %bundle.1.near_own) | copy-start | bytes 811012
  46.1 2.1 %copy-start.3 = (bf16[128,640]{1,0:T(8,128)(2,1)}, bf16[128,640]{1,0:T(8,128)(2,1)S(1)}, u32[]{:S(2)}) copy-start(bf16[128,640]{1,0:T(8,128)(2,1)S(1)} %get-tuple-element.29.c0) | copy-start | bytes 491524
  46.1 2.0 %collective-permute-start.12 = (bf16[1024,256]{1,0:T(8,128)(2,1)S(1)}, bf16[1024,256]{1,0:T(8,128)(2,1)S(1)}, u32[]{:S(2)}, u32[]{:S(2)}) collective-permute-start(bf16[1024,256]{1,0:T(8,128)(2,1)S(1)} %get-tuple-element.34), channel_id=1, source_target_pairs={{0,1},{1,0},{2,3},{3,2},{4,5},{5,4},{6,7},{7,6},{8,9},{9,8},{10,11... | collective-permute-start | bytes 1572872 | tf_op jit(solution)/shard_map/ppermute | solution.py:231
  48.2 26.4 %collective-permute-start.13 = (bf16[512,256]{1,0:T(8,128)(2,1)S(1)}, bf16[512,256]{1,0:T(8,128)(2,1)S(1)}, u32[]{:S(2)}, u32[]{:S(2)}) collective-permute-start(bf16[512,256]{1,0:T(8,128)(2,1)S(1)} %fusion), channel_id=1, source_target_pairs={{0,8},{1,9},{2,10},{3,11},{4,12},{5,13},{6,14},{7,15},{8,0},{9,1},... | collective-permute-start | bytes 786440 | tf_op jit(solution)/shard_map/ppermute | solution.py:231
  53.9 1.3 %collective-permute-start.17 = (f32[640]{0:T(1024)S(1)}, f32[640]{0:T(1024)S(1)}, u32[]{:S(2)}, u32[]{:S(2)}) collective-permute-start(f32[640]{0:T(1024)S(1)} %reduce), channel_id=1, source_target_pairs={{0,1},{1,0},{2,3},{3,2},{4,5},{5,4},{6,7},{7,6},{8,9},{9,8},{10,11... | collective-permute-start | bytes 7688 | tf_op jit(solution)/shard_map/ppermute | solution.py:231
  55.2 3.7 %collective-permute-start.18 = (f32[640]{0:T(1024)S(1)}, f32[640]{0:T(1024)S(1)}, u32[]{:S(2)}, u32[]{:S(2)}) collective-permute-start(f32[640]{0:T(1024)S(1)} %add_select_fusion), channel_id=1, source_target_pairs={{0,64},{1,65},{2,66},{3,67},{4,68},{5,69},{6,70},{7,71},{16,80},{1... | collective-permute-start | bytes 7688 | tf_op jit(solution)/shard_map/ppermute | solution.py:327
  58.9 4.8 %collective-permute-start.19 = (f32[640]{0:T(1024)S(1)}, f32[640]{0:T(1024)S(1)}, u32[]{:S(2)}, u32[]{:S(2)}) collective-permute-start(f32[640]{0:T(1024)S(1)} %add.37), channel_id=1, source_target_pairs={{0,192},{1,193},{2,194},{3,195},{4,196},{5,197},{6,198},{7,199},{1... | collective-permute-start | bytes 7688 | tf_op jit(solution)/shard_map/ppermute | solution.py:327
  63.8 4.1 %collective-permute-start.20 = (f32[640]{0:T(1024)S(1)}, f32[640]{0:T(1024)S(1)}, u32[]{:S(2)}, u32[]{:S(2)}) collective-permute-start(f32[640]{0:T(1024)S(1)} %add.38), channel_id=1, source_target_pairs={{0,16},{1,17},{2,18},{3,19},{4,20},{5,21},{6,22},{7,23},{16,0},{17... | collective-permute-start | bytes 7688 | tf_op jit(solution)/shard_map/ppermute | solution.py:327
  67.9 4.8 %collective-permute-start.21 = (f32[640]{0:T(1024)S(1)}, f32[640]{0:T(1024)S(1)}, u32[]{:S(2)}, u32[]{:S(2)}) collective-permute-start(f32[640]{0:T(1024)S(1)} %add.39), channel_id=1, source_target_pairs={{0,56},{1,57},{2,58},{3,59},{4,60},{5,61},{6,62},{7,63},{16,32},{1... | collective-permute-start | bytes 7688 | tf_op jit(solution)/shard_map/ppermute | solution.py:327
  67.9 9.8 %collective-permute-start.10 = (bf16[128,640]{1,0:T(8,128)(2,1)S(1)}, bf16[128,640]{1,0:T(8,128)(2,1)S(1)}, u32[]{:S(2)}, u32[]{:S(2)}) collective-permute-start(bf16[128,640]{1,0:T(8,128)(2,1)S(1)} %get-tuple-element.31), channel_id=1, source_target_pairs={{0,4},{1,5},{2,6},{3,7},{4,0},{5,1},{6,2},{7,3},{8,12},{9,13},{10,... | collective-permute-start | bytes 491528 | tf_op jit(solution)/shard_map/ppermute | solution.py:231
  69.5 10.5 %collective-permute-start.11 = (bf16[128,640]{1,0:T(8,128)(2,1)S(1)}, bf16[128,640]{1,0:T(8,128)(2,1)S(1)}, u32[]{:S(2)}, u32[]{:S(2)}) collective-permute-start(bf16[128,640]{1,0:T(8,128)(2,1)S(1)} %get-tuple-element.32), channel_id=1, source_target_pairs={{0,2},{1,3},{2,4},{3,5},{4,6},{5,7},{6,0},{7,1},{8,10},{9,11},{10,... | collective-permute-start | bytes 491528 | tf_op jit(solution)/shard_map/ppermute | solution.py:231
  71.4 10.1 %collective-permute-start.9 = (bf16[128,640]{1,0:T(8,128)(2,1)S(1)}, bf16[128,640]{1,0:T(8,128)(2,1)S(1)}, u32[]{:S(2)}, u32[]{:S(2)}) collective-permute-start(bf16[128,640]{1,0:T(8,128)(2,1)S(1)} %get-tuple-element.30), channel_id=1, source_target_pairs={{0,6},{1,7},{2,0},{3,1},{4,2},{5,3},{6,4},{7,5},{8,14},{9,15},{10,... | collective-permute-start | bytes 491528 | tf_op jit(solution)/shard_map/ppermute | solution.py:231
  72.7 5.4 %collective-permute-start.22 = (f32[640]{0:T(1024)S(1)}, f32[640]{0:T(1024)S(1)}, u32[]{:S(2)}, u32[]{:S(2)}) collective-permute-start(f32[640]{0:T(1024)S(1)} %add.40), channel_id=1, source_target_pairs={{0,48},{1,49},{2,50},{3,51},{4,52},{5,53},{6,54},{7,55},{16,40},{1... | collective-permute-start | bytes 7688 | tf_op jit(solution)/shard_map/ppermute | solution.py:327
  75.4 13.2 %collective-permute-start.14 = (bf16[128,256]{1,0:T(8,128)(2,1)S(1)}, bf16[128,256]{1,0:T(8,128)(2,1)S(1)}, u32[]{:S(2)}, u32[]{:S(2)}) collective-permute-start(bf16[128,256]{1,0:T(8,128)(2,1)S(1)} %get-tuple-element.42), channel_id=1, source_target_pairs={{0,6},{1,7},{2,0},{3,1},{4,2},{5,3},{6,4},{7,5},{8,14},{9,15},{10,... | collective-permute-start | bytes 196616 | tf_op jit(solution)/shard_map/ppermute | solution.py:231
  77.7 7.2 %copy-start.4 = (bf16[128,640]{1,0:T(8,128)(2,1)}, bf16[128,640]{1,0:T(8,128)(2,1)S(1)}, u32[]{:S(2)}) copy-start(bf16[128,640]{1,0:T(8,128)(2,1)S(1)} %collective-permute-done.10.c2) | copy-start | bytes 491524
  77.7 10.8 %collective-permute-start.15 = (bf16[128,256]{1,0:T(8,128)(2,1)S(1)}, bf16[128,256]{1,0:T(8,128)(2,1)S(1)}, u32[]{:S(2)}, u32[]{:S(2)}) collective-permute-start(bf16[128,256]{1,0:T(8,128)(2,1)S(1)} %get-tuple-element.41), channel_id=1, source_target_pairs={{0,4},{1,5},{2,6},{3,7},{4,0},{5,1},{6,2},{7,3},{8,12},{9,13},{10,... | collective-permute-start | bytes 196616 | tf_op jit(solution)/shard_map/ppermute | solution.py:231
  78.2 10.4 %collective-permute-start.16 = (bf16[128,256]{1,0:T(8,128)(2,1)S(1)}, bf16[128,256]{1,0:T(8,128)(2,1)S(1)}, u32[]{:S(2)}, u32[]{:S(2)}) collective-permute-start(bf16[128,256]{1,0:T(8,128)(2,1)S(1)} %get-tuple-element.40), channel_id=1, source_target_pairs={{0,2},{1,3},{2,4},{3,5},{4,6},{5,7},{6,0},{7,1},{8,10},{9,11},{10,... | collective-permute-start | bytes 196616 | tf_op jit(solution)/shard_map/ppermute | solution.py:231
  80.0 7.0 %copy-start.13 = (f32[640]{0:T(1024)}, f32[640]{0:T(1024)S(1)}, u32[]{:S(2)}) copy-start(f32[640]{0:T(1024)S(1)} %add.41.b0) | copy-start | bytes 7684
  80.0 4.9 %copy-start.5 = (bf16[128,640]{1,0:T(8,128)(2,1)}, bf16[128,640]{1,0:T(8,128)(2,1)S(1)}, u32[]{:S(2)}) copy-start(bf16[128,640]{1,0:T(8,128)(2,1)S(1)} %collective-permute-done.11.c3) | copy-start | bytes 491524
  80.0 3.7 %collective-permute-start.23 = (f32[640]{0:T(1024)S(1)}, f32[640]{0:T(1024)S(1)}, u32[]{:S(2)}, u32[]{:S(2)}) collective-permute-start(f32[640]{0:T(1024)S(1)} %add.41.b0), channel_id=1, source_target_pairs={{0,6},{1,7},{2,0},{3,1},{4,2},{5,3},{6,4},{7,5},{8,14},{9,15},{10,... | collective-permute-start | bytes 7688 | tf_op jit(solution)/shard_map/ppermute | solution.py:231
  81.5 3.4 %copy-start.6 = (bf16[128,640]{1,0:T(8,128)(2,1)}, bf16[128,640]{1,0:T(8,128)(2,1)S(1)}, u32[]{:S(2)}) copy-start(bf16[128,640]{1,0:T(8,128)(2,1)S(1)} %collective-permute-done.9.c1) | copy-start | bytes 491524
  81.5 5.5 %collective-permute-start.24 = (f32[640]{0:T(1024)S(1)}, f32[640]{0:T(1024)S(1)}, u32[]{:S(2)}, u32[]{:S(2)}) collective-permute-start(f32[640]{0:T(1024)S(1)} %add.41.b0), channel_id=1, source_target_pairs={{0,4},{1,5},{2,6},{3,7},{4,0},{5,1},{6,2},{7,3},{8,12},{9,13},{10,... | collective-permute-start | bytes 7688 | tf_op jit(solution)/shard_map/ppermute | solution.py:231
  83.7 3.3 %copy-start.14 = (f32[640]{0:T(1024)}, f32[640]{0:T(1024)S(1)}, u32[]{:S(2)}) copy-start(f32[640]{0:T(1024)S(1)} %collective-permute-done.23.b1) | copy-start | bytes 7684
  83.7 4.8 %collective-permute-start.25 = (f32[640]{0:T(1024)S(1)}, f32[640]{0:T(1024)S(1)}, u32[]{:S(2)}, u32[]{:S(2)}) collective-permute-start(f32[640]{0:T(1024)S(1)} %add.41.b0), channel_id=1, source_target_pairs={{0,2},{1,3},{2,4},{3,5},{4,6},{5,7},{6,0},{7,1},{8,10},{9,11},{10,... | collective-permute-start | bytes 7688 | tf_op jit(solution)/shard_map/ppermute | solution.py:231
  87.0 1.5 %copy-start.15 = (f32[640]{0:T(1024)}, f32[640]{0:T(1024)S(1)}, u32[]{:S(2)}) copy-start(f32[640]{0:T(1024)S(1)} %collective-permute-done.24.b2) | copy-start | bytes 7684
  88.5 0.6 copy-start.16
  88.5 0.6 copy-start.10
  88.5 0.6 copy-start.11
  88.5 0.7 copy-start.12

commit v4 on v3

--- a/solution.py
+++ b/solution.py
@@ -76,8 +76,8 @@
 def pack_qg_kernel(q_ref, g_ref, after_ref, *outs):
     _, y, _ = place()
     for k, out in enumerate(outs):
-        out[:, 0:GCOLS] = q_ref[0, :, head_of(y, k + 1, GCOLS)]
-        out[:, GCOLS:] = g_ref[0, :, head_of(y, k + 1, GCOLS)]
+        out[:, 0:GCOLS] = q_ref[0, :, head_of(y, k, GCOLS)]
+        out[:, GCOLS:] = g_ref[0, :, head_of(y, k, GCOLS)]
 
 
 def dot_nt(a, b):
@@ -94,22 +94,17 @@
 
 
 def attention_kernel(
-    q_ref, g_ref, g1, g2, g3, near_own, near_sib, far_own, far_sib,
+    g0, g1, g2, g3, near_own, near_sib, far_own, far_sib,
     dq0, dq1, dq2, dq3, bias_ref, sib_ref, far_ref, near_ref,
     qs, gs, kv, s_ref, dp_ref, peaks, dk_acc, dv_acc, dq_acc, starts, lows,
 ):
     z, y, core = place()
 
-    for k, ref in enumerate((None, g1, g2, g3)):
+    for k, ref in enumerate((g0, g1, g2, g3)):
         for h in range(GROUP):
             rows = slice(h * ROWS, (h + 1) * ROWS)
-            if k == 0:
-                columns = pl.ds(pl.multiple_of(y * GCOLS + h * HD, HD), HD)
-                qs[k, rows, :] = q_ref[0, :, columns]
-                gs[k, rows, :] = g_ref[0, :, columns]
-            else:
-                qs[k, rows, :] = ref[:, h * HD : (h + 1) * HD]
-                gs[k, rows, :] = ref[:, GCOLS + h * HD : GCOLS + (h + 1) * HD]
+            qs[k, rows, :] = ref[:, h * HD : (h + 1) * HD]
+            gs[k, rows, :] = ref[:, GCOLS + h * HD : GCOLS + (h + 1) * HD]
 
     kv[0] = jnp.zeros((ROWS, 2 * HD), bf16)
 
@@ -137,26 +132,27 @@
         place_in_half = 2 * lax.rem(y - k + CHIPS, CHIPS) + core
         here = 8 + place_in_half
         low = lows[k] // ROWS
-        amount = (here - low + 2) // 2
+        count = here - low + 1
+        full, odd = count // 2, lax.rem(count, 2) == 1
         query, grad = qs[k], gs[k]
         start = starts[k][0:1, :]
         query_at = here * ROWS + lax.broadcasted_iota(jnp.int32, (1, ROWS), 1)
 
-        def first(b, carried):
+        def first(b, base, chunks, carried):
             peak, total, dots = carried
-            base = here - 2 * b
-            keys = kv[pl.ds(base, 2), :, 0:HD].reshape(2 * ROWS, HD)
-            values = kv[pl.ds(base, 2), :, HD:].reshape(2 * ROWS, HD)
-            key_at = (base - 1) * ROWS + lax.broadcasted_iota(jnp.int32, (2 * ROWS, ROWS), 0)
+            size = chunks * ROWS
+            keys = kv[pl.ds(base, chunks), :, 0:HD].reshape(size, HD)
+            values = kv[pl.ds(base, chunks), :, HD:].reshape(size, HD)
+            key_at = (base - 1) * ROWS + lax.broadcasted_iota(jnp.int32, (size, ROWS), 0)
             allowed = (key_at >= start) & (key_at <= query_at)
             bias = jnp.where(allowed, 0.0, MASKED)
             bias = jnp.concatenate([bias] * GROUP, axis=1)
             scores = dot_nt(keys, query) * (INV_ROOT * LOG2E) + bias
             peak_now = jnp.maximum(peak, jnp.max(scores, axis=0, keepdims=True))
             weights = jnp.exp2(scores - peak_now)
-            s_ref[b] = weights
+            s_ref[b, 0:size] = weights
             grads = dot_nt(values, grad)
-            dp_ref[b] = grads
+            dp_ref[b, 0:size] = grads
             peaks[b] = jnp.broadcast_to(peak_now, (8, LANES))
             fade = jnp.exp2(peak - peak_now)
             total = total * fade + jnp.sum(weights.reshape(-1, 8, LANES), axis=0)
@@ -164,26 +160,40 @@
             return peak_now, total, dots
 
         nothing = jnp.zeros((8, LANES), f32)
-        peak, total, dots = lax.fori_loop(
-            0, amount, first, (jnp.full((1, LANES), MASKED, f32), nothing, nothing)
+        carried = lax.fori_loop(
+            0,
+            full,
+            lambda b, carried: first(b, here - 2 * b, 2, carried),
+            (jnp.full((1, LANES), MASKED, f32), nothing, nothing),
+        )
+        peak, total, dots = lax.cond(
+            odd, lambda c: first(full, low + 1, 1, c), lambda c: c, carried
         )
         inverse = 1.0 / jnp.sum(total, axis=0, keepdims=True)
         dots = jnp.sum(dots, axis=0, keepdims=True) * inverse
         dq_acc[...] = jnp.zeros(dq_acc.shape, f32)
 
-        def third(b, _):
-            base = here - 2 * b
-            softmax = s_ref[b] * (jnp.exp2(peaks[b][0:1] - peak) * inverse)
-            score_grad = (softmax * (dp_ref[b] - dots)).astype(bf16)
+        def third(b, base, chunks):
+            size = chunks * ROWS
+            softmax = s_ref[b, 0:size] * (jnp.exp2(peaks[b][0:1] - peak) * inverse)
+            score_grad = (softmax * (dp_ref[b, 0:size] - dots)).astype(bf16)
             dv = dot_nn(softmax.astype(bf16), grad)
             dk = dot_nn(score_grad, query)
-            dv_acc[pl.ds(base, 2)] += dv.reshape(2, ROWS, HD)
-            dk_acc[pl.ds(base, 2)] += dk.reshape(2, ROWS, HD)
-            keys = kv[pl.ds(base, 2), :, 0:HD].reshape(2 * ROWS, HD)
-            dq_acc[...] += lax.dot_general(score_grad, keys, (((0,), (0,)), ((), ())), preferred_element_type=f32)
-            return 0
-
-        lax.fori_loop(0, amount, third, 0)
+            dv_acc[pl.ds(base, chunks)] += dv.reshape(chunks, ROWS, HD)
+            dk_acc[pl.ds(base, chunks)] += dk.reshape(chunks, ROWS, HD)
+            keys = kv[pl.ds(base, chunks), :, 0:HD].reshape(size, HD)
+            dq_acc[...] += lax.dot_general(
+                score_grad, keys, (((0,), (0,)), ((), ())), preferred_element_type=f32
+            )
+
+        @pl.loop(0, full)
+        def _(b):
+            third(b, here - 2 * b, 2)
+
+        @pl.when(odd)
+        def _():
+            third(full, low + 1, 1)
+
         bias_rows = []
         for h in range(GROUP):
             dq = dq_acc[h * ROWS : (h + 1) * ROWS] * INV_ROOT
@@ -194,9 +204,16 @@
                 def _():
                     out[:, h * HD : (h + 1) * HD] = dq.astype(bf16)
 
-        return total_bias + jnp.concatenate(bias_rows, axis=1)
-
-    bias_ref[...] = lax.fori_loop(0, CHIPS, query_chunk, jnp.zeros((1, GCOLS), f32))
+        bias_rows.append(jnp.zeros((8 - GROUP, HD), f32))
+        return total_bias + jnp.concatenate(bias_rows, axis=0)
+
+    bias = lax.fori_loop(0, CHIPS, query_chunk, jnp.zeros((8, HD), f32))
+    bias_ref[...] = bias
+    high = bias.astype(bf16).astype(f32)
+    middle = (bias - high).astype(bf16).astype(f32)
+    low_part = bias - high - middle
+    terms = jnp.concatenate([high, middle], axis=1), jnp.concatenate([low_part, low_part * 0], axis=1)
+    sib_ref[2 * CHIPS * ROWS :, :] = jnp.concatenate(terms, axis=0).astype(bf16)
 
     half_rows = CHIPS * ROWS
     outputs = ((far_ref, 0, 0, core), (sib_ref, 0, 0, 1 - core), (near_ref, 0, 1, core), (sib_ref, half_rows, 1, 1 - core))
@@ -224,7 +241,9 @@
         row = rows[j]
         for near in range(1, CHIPS):
             row = jnp.where(y == near, rows[(j - near) % CHIPS], row)
-        bias_out[j * GCOLS : (j + 1) * GCOLS] = row
+        for h in range(GROUP):
+            at = j * GCOLS + h * HD
+            bias_out[at : at + HD] = row[h]
 
 
 def move(array, table):
@@ -263,7 +282,7 @@
     )(key_rows, value_rows, doc_ids)
     qg = pl.pallas_call(
         pack_qg_kernel,
-        out_shape=[shape((ROWS, 2 * GCOLS), bf16)] * 3,
+        out_shape=[shape((ROWS, 2 * GCOLS), bf16)] * CHIPS,
         in_specs=[vmem, vmem, anywhere],
         name="pack_qg",
     )(query_rows, out_grad, lines[0])
@@ -276,7 +295,7 @@
     )(*lines, qg[0])
     far = move(near, ACROSS)
     near_sib = move(near, SWAP)
-    qg = [move(qg[k - 1], shift(k)) for k in (1, 2, 3)]
+    qg = [qg[0]] + [move(qg[k], shift(k)) for k in (1, 2, 3)]
     far_sib = move(far, SWAP)
 
     half = shape((CHIPS * ROWS, 2 * HD), f32)
@@ -284,8 +303,8 @@
         attention_kernel,
         out_shape=(
             *[shape((ROWS, GCOLS), bf16)] * CHIPS,
-            shape((1, GCOLS), f32),
-            shape((2 * CHIPS * ROWS, 2 * HD), bf16),
+            shape((8, HD), f32),
+            shape((2 * CHIPS * ROWS + 16, 2 * HD), bf16),
             half,
             half,
         ),
@@ -302,18 +321,18 @@
             pltpu.VMEM((CHIPS, 8, ROWS), jnp.int32),
             pltpu.SMEM((CHIPS,), jnp.int32),
         ],
-        compiler_params=pltpu.CompilerParams(vmem_limit_bytes=24 * 1024 * 1024),
+        compiler_params=pltpu.CompilerParams(vmem_limit_bytes=36 * 1024 * 1024),
         name="attention",
-    )(query_rows, out_grad, *qg, near, near_sib, far, far_sib)
-    dq, bias = outs[:CHIPS], outs[CHIPS][0]
+    )(*qg, near, near_sib, far, far_sib)
+    dq, bias = outs[:CHIPS], outs[CHIPS]
     to_sib, far_part, near_part = outs[CHIPS + 1 :]
 
-    sib = move(to_sib, SWAP).astype(f32)
+    sib = move(to_sib, SWAP)
     half_rows = CHIPS * ROWS
-    far_sum = (far_part + sib[:half_rows]).astype(bf16)
+    far_sum = (far_part + sib[:half_rows].astype(f32)).astype(bf16)
     down = move(far_sum, ACROSS)
     dq = [dq[0]] + [move(dq[k], shift(-k)) for k in (1, 2, 3)]
-    kv_grad = (near_part + sib[half_rows:] + down.astype(f32)).astype(bf16)
+    kv_grad = (near_part + sib[half_rows : 2 * half_rows].astype(f32) + down.astype(f32)).astype(bf16)
     kv_grad = [kv_grad[k * ROWS : (k + 1) * ROWS] for k in range(CHIPS)]
     kv_grad = [kv_grad[0]] + [move(kv_grad[k], shift(-k)) for k in (1, 2, 3)]
 
@@ -321,8 +340,8 @@
         place_q_kernel, out_shape=shape(query_rows.shape, bf16), name="place_q"
     )(*dq)
 
-    bias = bias + move(bias, SWAP)
-    bias = jnp.where(y < CHIPS, bias, far_sum[0, 0].astype(f32))
+    terms = sib[2 * half_rows :].astype(f32)
+    bias = bias + ((terms[0:8, 0:HD] + terms[0:8, HD:]) + terms[8:, 0:HD])
     for table in MEETINGS:
         bias = bias + lax.ppermute(bias, ("dp", "ctx"), table)
     heads = [bias] + [move(bias, shift(-k)) for k in (1, 2, 3)]

time: 92.6 us -> 91.8 us (level)
  starting transfers between devices: 42.5 us -> 45.3 us
  Pallas kernels: 16.8 us -> 15.3 us
    ppermute x5, starting transfers between devices: 5.25 us -> 8.34 us  [body(): bias = bias + lax.ppermute(bias, ('dp', 'ctx'), table)]
    pallas_call x1, Pallas kernels: 7.26 us -> 5.6 us  [body(): pl.pallas_call(attention_kernel, out_shape=(*[shape((ROWS, GCOLS), bf16)]...]
    ppermute x21 -> x20, waiting for transfers between devices: 17.1 us -> 18.3 us  [move(): return lax.ppermute(array, 'ctx', table)]
    ppermute x5, waiting for transfers between devices: 9.28 us -> 8.11 us  [body(): bias = bias + lax.ppermute(bias, ('dp', 'ctx'), table)]
    ppermute x21 -> x20, starting transfers between devices: 37.3 us -> 36.9 us  [move(): return lax.ppermute(array, 'ctx', table)]
  transfers between devices with their start and end apart: 26 -> 25, of which waited for: 10 -> 12; matrix products, arithmetic and copies ran while one was open for 1% -> 1% of each run, Pallas kernels for 5% -> 5%
where the time goes in v4:
time: 91.8 us; the launch traced here: 90.8 us
  starting transfers between devices  45.3 us (49%)
  waiting for transfers between devices  26.4 us (29%)
  Pallas kernels  15.3 us (17%)
  local copies, waits for them, and re-layouts  2.89 us (3%)
    ppermute x20, starting transfers between devices, move(): return lax.ppermute(array, 'ctx', table)  36.9 us
    ppermute x20, waiting for transfers between devices, move(): return lax.ppermute(array, 'ctx', table)  18.3 us
    ppermute x5, starting transfers between devices, body(): bias = bias + lax.ppermute(bias, ('dp', 'ctx'), table)  8.34 us
    ppermute x5, waiting for transfers between devices, body(): bias = bias + lax.ppermute(bias, ('dp', 'ctx'), table)  8.11 us
    pallas_call x1, Pallas kernels, body(): pl.pallas_call(attention_kernel, out_shape=(*[shape((ROWS, GCOLS), bf16)]...  5.6 us
    pallas_call x1, Pallas kernels, body(): pl.pallas_call(pack_qg_kernel, out_shape=[shape((ROWS, 2 * GCOLS), bf16)]...  2.44 us
    unnamed x34, local copies, waits for them, and re-layouts  2.25 us
    pallas_call x1, Pallas kernels, body(): pl.pallas_call(place_q_kernel, out_shape=shape(query_rows.shape, bf16), n...  2.07 us
  transfers between devices with their start and end apart: 25, of which 12 were waited for; matrix products, arithmetic and copies ran while one was open for 1% of the time, Pallas kernels for 5%

profile of v4, /device:TPU:6, one launch (start us, length us, event | category | flops | bytes accessed | tf_op | source)
XLA Modules:
  0.0 90.8 jit_solution(5170521117680946946)
XLA Ops:
  0.6 1.7 %pack_kv.1 = (bf16[144,256]{1,0:T(8,128)(2,1)}, bf16[144,256]{1,0:T(8,128)(2,1)}, bf16[144,256]{1,0:T(8,128)(2,1)}, bf16[144,256]{1,0:T(8,128)(2,1)}) custom-call(bf16[1,128,512]{2,1,0:T(8,128)(2,1)} %k_ref.1, bf16[1,128,512]{2,1,0:T(8,128)(2,1)} %v_ref.1, s32[1,128]{1,0:T(1,128)} %ids_ref.1), custom_call_target="tpu_custom_call" | custom-call | tf_op jit(solution)/shard_map/pack_kv/pallas_call | solution.py:280
  2.4 1.6 %collective-permute-start.3 = (bf16[144,256]{1,0:T(8,128)(2,1)}, bf16[144,256]{1,0:T(8,128)(2,1)S(1)}, u32[]{:S(2)}, u32[]{:S(2)}) collective-permute-start(bf16[144,256]{1,0:T(8,128)(2,1)} %get-tuple-element.28), channel_id=1, source_target_pairs={{0,2},{1,3},{2,4},{3,5},{4,6},{5,7},{6,0},{7,1},{8,10},{9,11},{10,... | collective-permute-start | bytes 221192 | tf_op jit(solution)/shard_map/ppermute | solution.py:250
  3.9 2.9 %collective-permute-start.4 = (bf16[144,256]{1,0:T(8,128)(2,1)}, bf16[144,256]{1,0:T(8,128)(2,1)S(1)}, u32[]{:S(2)}, u32[]{:S(2)}) collective-permute-start(bf16[144,256]{1,0:T(8,128)(2,1)} %get-tuple-element.29), channel_id=1, source_target_pairs={{0,4},{1,5},{2,6},{3,7},{4,0},{5,1},{6,2},{7,3},{8,12},{9,13},{10,... | collective-permute-start | bytes 221192 | tf_op jit(solution)/shard_map/ppermute | solution.py:250
  6.8 1.3 %collective-permute-start.5 = (bf16[144,256]{1,0:T(8,128)(2,1)}, bf16[144,256]{1,0:T(8,128)(2,1)S(1)}, u32[]{:S(2)}, u32[]{:S(2)}) collective-permute-start(bf16[144,256]{1,0:T(8,128)(2,1)} %get-tuple-element.30), channel_id=1, source_target_pairs={{0,6},{1,7},{2,0},{3,1},{4,2},{5,3},{6,4},{7,5},{8,14},{9,15},{10,... | collective-permute-start | bytes 221192 | tf_op jit(solution)/shard_map/ppermute | solution.py:250
  8.2 2.4 %pack_qg.1 = (bf16[128,1280]{1,0:T(8,128)(2,1)}, bf16[128,1280]{1,0:T(8,128)(2,1)}, bf16[128,1280]{1,0:T(8,128)(2,1)}, bf16[128,1280]{1,0:T(8,128)(2,1)}) custom-call(bf16[1,128,2560]{2,1,0:T(8,128)(2,1)} %q_ref.1, bf16[1,128,2560]{2,1,0:T(8,128)(2,1)} %g_ref.1, bf16[144,256]{1,0:T(8,128)(2,1)} %get-tuple-element.23.after_ref.l0), custom_call_target="tpu_custom_call" | custom-call | tf_op jit(solution)/shard_map/pack_qg/pallas_call | solution.py:283
  10.6 0.8 collective-permute-done.5.l3
  11.4 0.6 copy-done.8
  12.0 1.8 %bundle.1.near_own = bf16[528,256]{1,0:T(8,128)(2,1)} custom-call(bf16[144,256]{1,0:T(8,128)(2,1)} %get-tuple-element.23.after_ref.l0, bf16[144,256]{1,0:T(8,128)(2,1)} %copy-done.6, bf16[144,256]{1,0:T(8,128)(2,1)} %copy-done.7, bf16[144,256]{1,0:T(8,128)(2,1)} %copy-done.8, bf16[128,1280]{1,0:T(8,128)(2,1)} %get-tuple-element.24.after_ref.g0), custom_call_target="tpu_custom_call" | custom-call | tf_op jit(solution)/shard_map/bundle/pallas_call | solution.py:290
  13.8 7.2 %collective-permute-start.7 = (bf16[528,256]{1,0:T(8,128)(2,1)}, bf16[528,256]{1,0:T(8,128)(2,1)S(1)}, u32[]{:S(2)}, u32[]{:S(2)}) collective-permute-start(bf16[528,256]{1,0:T(8,128)(2,1)} %bundle.1.near_own), channel_id=1, source_target_pairs={{0,8},{1,9},{2,10},{3,11},{4,12},{5,13},{6,14},{7,15},{8,0},{9,1},... | collective-permute-start | bytes 811016 | tf_op jit(solution)/shard_map/ppermute | solution.py:250
  21.0 0.4 collective-permute-start
  21.4 3.6 %collective-permute-start.1 = (bf16[128,1280]{1,0:T(8,128)(2,1)}, bf16[128,1280]{1,0:T(8,128)(2,1)S(1)}, u32[]{:S(2)}, u32[]{:S(2)}) collective-permute-start(bf16[128,1280]{1,0:T(8,128)(2,1)} %get-tuple-element.26), channel_id=1, source_target_pairs={{0,4},{1,5},{2,6},{3,7},{4,0},{5,1},{6,2},{7,3},{8,12},{9,13},{10,... | collective-permute-start | bytes 983048 | tf_op jit(solution)/shard_map/ppermute | solution.py:250
  25.0 0.3 collective-permute-start.2
  25.4 2.1 %collective-permute-done.7.far_own = bf16[528,256]{1,0:T(8,128)(2,1)S(1)} collective-permute-done((bf16[528,256]{1,0:T(8,128)(2,1)}, bf16[528,256]{1,0:T(8,128)(2,1)S(1)}, u32[]{:S(2)}, u32[]{:S(2)}) %collective-permute-start.7) | collective-permute-done | bytes 270368 | tf_op jit(solution)/shard_map/ppermute | solution.py:250
  27.5 5.2 %collective-permute-done.g1 = bf16[128,1280]{1,0:T(8,128)(2,1)S(1)} collective-permute-done((bf16[128,1280]{1,0:T(8,128)(2,1)}, bf16[128,1280]{1,0:T(8,128)(2,1)S(1)}, u32[]{:S(2)}, u32[]{:S(2)}) %collective-permute-start) | collective-permute-done | bytes 327712 | tf_op jit(solution)/shard_map/ppermute | solution.py:250
  32.6 5.2 %collective-permute-done.1.g2 = bf16[128,1280]{1,0:T(8,128)(2,1)S(1)} collective-permute-done((bf16[128,1280]{1,0:T(8,128)(2,1)}, bf16[128,1280]{1,0:T(8,128)(2,1)S(1)}, u32[]{:S(2)}, u32[]{:S(2)}) %collective-permute-start.1) | collective-permute-done | bytes 327712 | tf_op jit(solution)/shard_map/ppermute | solution.py:250
  37.9 0.9 %copy-done.1 = bf16[528,256]{1,0:T(8,128)(2,1)S(1)} copy-done((bf16[528,256]{1,0:T(8,128)(2,1)S(1)}, bf16[528,256]{1,0:T(8,128)(2,1)}, u32[]{:S(2)}) %copy-start.1) | copy-done | bytes 270360
  38.9 5.6 %attention.1 = (bf16[128,640]{1,0:T(8,128)(2,1)S(1)}, bf16[128,640]{1,0:T(8,128)(2,1)S(1)}, bf16[128,640]{1,0:T(8,128)(2,1)S(1)}, bf16[128,640]{1,0:T(8,128)(2,1...) custom-call(bf16[128,1280]{1,0:T(8,128)(2,1)S(1)} %copy-done, ...), custom_call_target="tpu_custom_call" | custom-call | tf_op jit(solution)/shard_map/attention/pallas_call | solution.py:302
  44.5 1.0 %collective-permute-start.12 = (bf16[1040,256]{1,0:T(8,128)(2,1)S(1)}, bf16[1040,256]{1,0:T(8,128)(2,1)S(1)}, u32[]{:S(2)}, u32[]{:S(2)}) collective-permute-start(bf16[1040,256]{1,0:T(8,128)(2,1)S(1)} %get-tuple-element.36), channel_id=1, source_target_pairs={{0,1},{1,0},{2,3},{3,2},{4,5},{5,4},{6,7},{7,6},{8,9},{9,8},{10,11... | collective-permute-start | bytes 1597448 | tf_op jit(solution)/shard_map/ppermute | solution.py:250
  45.5 1.5 %collective-permute-done.12 = bf16[1040,256]{1,0:T(8,128)(2,1)S(1)} collective-permute-done((bf16[1040,256]{1,0:T(8,128)(2,1)S(1)}, bf16[1040,256]{1,0:T(8,128)(2,1)S(1)}, u32[]{:S(2)}, u32[]{:S(2)}) %collective-permute-start.12) | collective-permute-done | bytes 532512 | tf_op jit(solution)/shard_map/ppermute | solution.py:250
  47.0 0.1 add_convert_fusion.1
  47.1 5.3 %collective-permute-start.13 = (bf16[512,256]{1,0:T(8,128)(2,1)S(1)}, bf16[512,256]{1,0:T(8,128)(2,1)S(1)}, u32[]{:S(2)}, u32[]{:S(2)}) collective-permute-start(bf16[512,256]{1,0:T(8,128)(2,1)S(1)} %add_convert_fusion.1), channel_id=1, source_target_pairs={{0,8},{1,9},{2,10},{3,11},{4,12},{5,13},{6,14},{7,15},{8,0},{9,1},... | collective-permute-start | bytes 786440 | tf_op jit(solution)/shard_map/ppermute | solution.py:250
  52.4 1.9 %collective-permute-start.17 = (f32[8,128]{1,0:T(8,128)S(1)}, f32[8,128]{1,0:T(8,128)S(1)}, u32[]{:S(2)}, u32[]{:S(2)}) collective-permute-start(f32[8,128]{1,0:T(8,128)S(1)} %fusion), channel_id=1, source_target_pairs={{0,64},{1,65},{2,66},{3,67},{4,68},{5,69},{6,70},{7,71},{16,80},{1... | collective-permute-start | bytes 12296 | tf_op jit(solution)/shard_map/ppermute | solution.py:346
  54.2 1.7 %collective-permute-done.17 = f32[8,128]{1,0:T(8,128)S(1)} collective-permute-done((f32[8,128]{1,0:T(8,128)S(1)}, f32[8,128]{1,0:T(8,128)S(1)}, u32[]{:S(2)}, u32[]{:S(2)}) %collective-permute-start.17) | collective-permute-done | bytes 4128 | tf_op jit(solution)/shard_map/ppermute | solution.py:346
  56.0 1.5 %collective-permute-start.18 = (f32[8,128]{1,0:T(8,128)S(1)}, f32[8,128]{1,0:T(8,128)S(1)}, u32[]{:S(2)}, u32[]{:S(2)}) collective-permute-start(f32[8,128]{1,0:T(8,128)S(1)} %add.39), channel_id=1, source_target_pairs={{0,192},{1,193},{2,194},{3,195},{4,196},{5,197},{6,198},{7,199},{1... | collective-permute-start | bytes 12296 | tf_op jit(solution)/shard_map/ppermute | solution.py:346
  57.5 3.3 %collective-permute-done.18 = f32[8,128]{1,0:T(8,128)S(1)} collective-permute-done((f32[8,128]{1,0:T(8,128)S(1)}, f32[8,128]{1,0:T(8,128)S(1)}, u32[]{:S(2)}, u32[]{:S(2)}) %collective-permute-start.18) | collective-permute-done | bytes 4128 | tf_op jit(solution)/shard_map/ppermute | solution.py:346
  60.8 1.5 %collective-permute-start.19 = (f32[8,128]{1,0:T(8,128)S(1)}, f32[8,128]{1,0:T(8,128)S(1)}, u32[]{:S(2)}, u32[]{:S(2)}) collective-permute-start(f32[8,128]{1,0:T(8,128)S(1)} %add.40), channel_id=1, source_target_pairs={{0,16},{1,17},{2,18},{3,19},{4,20},{5,21},{6,22},{7,23},{16,0},{17... | collective-permute-start | bytes 12296 | tf_op jit(solution)/shard_map/ppermute | solution.py:346
  62.3 3.1 %collective-permute-done.19 = f32[8,128]{1,0:T(8,128)S(1)} collective-permute-done((f32[8,128]{1,0:T(8,128)S(1)}, f32[8,128]{1,0:T(8,128)S(1)}, u32[]{:S(2)}, u32[]{:S(2)}) %collective-permute-start.19) | collective-permute-done | bytes 4128 | tf_op jit(solution)/shard_map/ppermute | solution.py:346
  65.4 0.6 collective-permute-start.20
  65.9 3.7 %collective-permute-start.9 = (bf16[128,640]{1,0:T(8,128)(2,1)S(1)}, bf16[128,640]{1,0:T(8,128)(2,1)S(1)}, u32[]{:S(2)}, u32[]{:S(2)}) collective-permute-start(bf16[128,640]{1,0:T(8,128)(2,1)S(1)} %get-tuple-element.32), channel_id=1, source_target_pairs={{0,6},{1,7},{2,0},{3,1},{4,2},{5,3},{6,4},{7,5},{8,14},{9,15},{10,... | collective-permute-start | bytes 491528 | tf_op jit(solution)/shard_map/ppermute | solution.py:250
  69.7 0.5 collective-permute-start.10
  70.2 0.3 collective-permute-start.11
  70.5 2.9 %collective-permute-start.21 = (f32[8,128]{1,0:T(8,128)S(1)}, f32[8,128]{1,0:T(8,128)S(1)}, u32[]{:S(2)}, u32[]{:S(2)}) collective-permute-start(f32[8,128]{1,0:T(8,128)S(1)} %add.42), channel_id=1, source_target_pairs={{0,48},{1,49},{2,50},{3,51},{4,52},{5,53},{6,54},{7,55},{16,40},{1... | collective-permute-start | bytes 12296 | tf_op jit(solution)/shard_map/ppermute | solution.py:346
  73.4 0.1 add_convert_fusion
  73.5 0.6 fusion.1
  74.2 1.3 %collective-permute-start.16 = (bf16[128,256]{1,0:T(8,128)(2,1)S(1)}, bf16[128,256]{1,0:T(8,128)(2,1)S(1)}, u32[]{:S(2)}, u32[]{:S(2)}) collective-permute-start(bf16[128,256]{1,0:T(8,128)(2,1)S(1)} %get-tuple-element.42), channel_id=1, source_target_pairs={{0,2},{1,3},{2,4},{3,5},{4,6},{5,7},{6,0},{7,1},{8,10},{9,11},{10,... | collective-permute-start | bytes 196616 | tf_op jit(solution)/shard_map/ppermute | solution.py:250
  75.5 0.7 collective-permute-done.9.c1
  76.1 2.1 %collective-permute-start.15 = (bf16[128,256]{1,0:T(8,128)(2,1)S(1)}, bf16[128,256]{1,0:T(8,128)(2,1)S(1)}, u32[]{:S(2)}, u32[]{:S(2)}) collective-permute-start(bf16[128,256]{1,0:T(8,128)(2,1)S(1)} %get-tuple-element.43), channel_id=1, source_target_pairs={{0,4},{1,5},{2,6},{3,7},{4,0},{5,1},{6,2},{7,3},{8,12},{9,13},{10,... | collective-permute-start | bytes 196616 | tf_op jit(solution)/shard_map/ppermute | solution.py:250
  78.3 1.7 %collective-permute-start.14 = (bf16[128,256]{1,0:T(8,128)(2,1)S(1)}, bf16[128,256]{1,0:T(8,128)(2,1)S(1)}, u32[]{:S(2)}, u32[]{:S(2)}) collective-permute-start(bf16[128,256]{1,0:T(8,128)(2,1)S(1)} %get-tuple-element.44), channel_id=1, source_target_pairs={{0,6},{1,7},{2,0},{3,1},{4,2},{5,3},{6,4},{7,5},{8,14},{9,15},{10,... | collective-permute-start | bytes 196616 | tf_op jit(solution)/shard_map/ppermute | solution.py:250
  79.9 0.9 collective-permute-start.24
  80.8 0.1 collective-permute-done.11.c3
  80.9 2.1 %collective-permute-start.23 = (f32[8,128]{1,0:T(8,128)S(1)}, f32[8,128]{1,0:T(8,128)S(1)}, u32[]{:S(2)}, u32[]{:S(2)}) collective-permute-start(f32[8,128]{1,0:T(8,128)S(1)} %add.43.b0), channel_id=1, source_target_pairs={{0,4},{1,5},{2,6},{3,7},{4,0},{5,1},{6,2},{7,3},{8,12},{9,13},{10,... | collective-permute-start | bytes 12296 | tf_op jit(solution)/shard_map/ppermute | solution.py:250
  83.0 1.9 %collective-permute-done.24.b3 = f32[8,128]{1,0:T(8,128)S(1)} collective-permute-done((f32[8,128]{1,0:T(8,128)S(1)}, f32[8,128]{1,0:T(8,128)S(1)}, u32[]{:S(2)}, u32[]{:S(2)}) %collective-permute-start.24) | collective-permute-done | bytes 4128 | tf_op jit(solution)/shard_map/ppermute | solution.py:250
  84.8 0.7 collective-permute-start.22
  85.5 2.1 %place_q.1 = bf16[1,128,2560]{2,1,0:T(8,128)(2,1)} custom-call(bf16[128,640]{1,0:T(8,128)(2,1)} %copy-done.2, bf16[128,640]{1,0:T(8,128)(2,1)} %copy-done.3, bf16[128,640]{1,0:T(8,128)(2,1)} %copy-done.4, bf16[128,640]{1,0:T(8,128)(2,1)} %copy-done.5), custom_call_target="tpu_custom_call" | custom-call | tf_op jit(solution)/shard_map/place_q/pallas_call | solution.py:339
  87.6 0.8 collective-permute-done.22.b1
  88.5 0.5 copy-done.15
  89.0 0.0 copy-done.9
  89.1 1.7 %place.1 = (bf16[1,128,512]{2,1,0:T(8,128)(2,1)}, bf16[1,128,512]{2,1,0:T(8,128)(2,1)}, f32[2560]{0:T(1024)}) custom-call(bf16[128,256]{1,0:T(8,128)(2,1)} %get-tuple-element.45.c0, bf16[128,256]{1,0:T(8,128)(2,1)} %copy-done.11, bf16[128,256]{1,0:T(8,128)(2,1)} %copy-done.10, bf16[128,256]{1,0:T(8,128)(2,1)} %copy-done.9, f32[8,128]{1,0:T(8,128)} %copy-done.12, ...), custom_call_target="tpu_custom_call" | custom-call | tf_op jit(solution)/shard_map/place/pallas_call | solution.py:348
  (52 shorter events, 0.2 us)
Async XLA Ops:
  2.4 8.3 %collective-permute-start.3 = (bf16[144,256]{1,0:T(8,128)(2,1)}, bf16[144,256]{1,0:T(8,128)(2,1)S(1)}, u32[]{:S(2)}, u32[]{:S(2)}) collective-permute-start(bf16[144,256]{1,0:T(8,128)(2,1)} %get-tuple-element.28), channel_id=1, source_target_pairs={{0,2},{1,3},{2,4},{3,5},{4,6},{5,7},{6,0},{7,1},{8,10},{9,11},{10,... | collective-permute-start | bytes 221192 | tf_op jit(solution)/shard_map/ppermute | solution.py:250
  3.9 6.7 %collective-permute-start.4 = (bf16[144,256]{1,0:T(8,128)(2,1)}, bf16[144,256]{1,0:T(8,128)(2,1)S(1)}, u32[]{:S(2)}, u32[]{:S(2)}) collective-permute-start(bf16[144,256]{1,0:T(8,128)(2,1)} %get-tuple-element.29), channel_id=1, source_target_pairs={{0,4},{1,5},{2,6},{3,7},{4,0},{5,1},{6,2},{7,3},{8,12},{9,13},{10,... | collective-permute-start | bytes 221192 | tf_op jit(solution)/shard_map/ppermute | solution.py:250
  6.8 4.6 %collective-permute-start.5 = (bf16[144,256]{1,0:T(8,128)(2,1)}, bf16[144,256]{1,0:T(8,128)(2,1)S(1)}, u32[]{:S(2)}, u32[]{:S(2)}) collective-permute-start(bf16[144,256]{1,0:T(8,128)(2,1)} %get-tuple-element.30), channel_id=1, source_target_pairs={{0,6},{1,7},{2,0},{3,1},{4,2},{5,3},{6,4},{7,5},{8,14},{9,15},{10,... | collective-permute-start | bytes 221192 | tf_op jit(solution)/shard_map/ppermute | solution.py:250
  10.6 0.8 copy-start.6
  10.6 0.8 copy-start.7
  11.4 0.6 copy-start.8
  12.0 13.0 %copy-start.16 = (bf16[128,1280]{1,0:T(8,128)(2,1)S(1)}, bf16[128,1280]{1,0:T(8,128)(2,1)}, u32[]{:S(2)}) copy-start(bf16[128,1280]{1,0:T(8,128)(2,1)} %get-tuple-element.27) | copy-start | bytes 983044
  12.0 25.9 %copy-start = (bf16[128,1280]{1,0:T(8,128)(2,1)S(1)}, bf16[128,1280]{1,0:T(8,128)(2,1)}, u32[]{:S(2)}) copy-start(bf16[128,1280]{1,0:T(8,128)(2,1)} %get-tuple-element.24.after_ref.g0) | copy-start | bytes 983044
  13.8 13.7 %collective-permute-start.7 = (bf16[528,256]{1,0:T(8,128)(2,1)}, bf16[528,256]{1,0:T(8,128)(2,1)S(1)}, u32[]{:S(2)}, u32[]{:S(2)}) collective-permute-start(bf16[528,256]{1,0:T(8,128)(2,1)} %bundle.1.near_own), channel_id=1, source_target_pairs={{0,8},{1,9},{2,10},{3,11},{4,12},{5,13},{6,14},{7,15},{8,0},{9,1},... | collective-permute-start | bytes 811016 | tf_op jit(solution)/shard_map/ppermute | solution.py:250
  21.0 11.6 %collective-permute-start = (bf16[128,1280]{1,0:T(8,128)(2,1)}, bf16[128,1280]{1,0:T(8,128)(2,1)S(1)}, u32[]{:S(2)}, u32[]{:S(2)}) collective-permute-start(bf16[128,1280]{1,0:T(8,128)(2,1)} %get-tuple-element.25), channel_id=1, source_target_pairs={{0,2},{1,3},{2,4},{3,5},{4,6},{5,7},{6,0},{7,1},{8,10},{9,11},{10,... | collective-permute-start | bytes 983048 | tf_op jit(solution)/shard_map/ppermute | solution.py:250
  21.4 16.4 %collective-permute-start.1 = (bf16[128,1280]{1,0:T(8,128)(2,1)}, bf16[128,1280]{1,0:T(8,128)(2,1)S(1)}, u32[]{:S(2)}, u32[]{:S(2)}) collective-permute-start(bf16[128,1280]{1,0:T(8,128)(2,1)} %get-tuple-element.26), channel_id=1, source_target_pairs={{0,4},{1,5},{2,6},{3,7},{4,0},{5,1},{6,2},{7,3},{8,12},{9,13},{10,... | collective-permute-start | bytes 983048 | tf_op jit(solution)/shard_map/ppermute | solution.py:250
  25.0 12.9 %collective-permute-start.2 = (bf16[128,1280]{1,0:T(8,128)(2,1)S(1)}, bf16[128,1280]{1,0:T(8,128)(2,1)S(1)}, u32[]{:S(2)}, u32[]{:S(2)}) collective-permute-start(bf16[128,1280]{1,0:T(8,128)(2,1)S(1)} %copy-done.16), channel_id=1, source_target_pairs={{0,6},{1,7},{2,0},{3,1},{4,2},{5,3},{6,4},{7,5},{8,14},{9,15},{10,... | collective-permute-start | bytes 983048 | tf_op jit(solution)/shard_map/ppermute | solution.py:250
  25.4 12.5 %collective-permute-start.6 = (bf16[528,256]{1,0:T(8,128)(2,1)}, bf16[528,256]{1,0:T(8,128)(2,1)S(1)}, u32[]{:S(2)}, u32[]{:S(2)}) collective-permute-start(bf16[528,256]{1,0:T(8,128)(2,1)} %bundle.1.near_own), channel_id=1, source_target_pairs={{0,1},{1,0},{2,3},{3,2},{4,5},{5,4},{6,7},{7,6},{8,9},{9,8},{10,11... | collective-permute-start | bytes 811016 | tf_op jit(solution)/shard_map/ppermute | solution.py:250
  27.5 10.4 %collective-permute-start.8 = (bf16[528,256]{1,0:T(8,128)(2,1)S(1)}, bf16[528,256]{1,0:T(8,128)(2,1)S(1)}, u32[]{:S(2)}, u32[]{:S(2)}) collective-permute-start(bf16[528,256]{1,0:T(8,128)(2,1)S(1)} %collective-permute-done.7.far_own), channel_id=1, source_target_pairs={{0,1},{1,0},{2,3},{3,2},{4,5},{5,4},{6,7},{7,6},{8,9},{9,8},{10,11... | collective-permute-start | bytes 811016 | tf_op jit(solution)/shard_map/ppermute | solution.py:250
  37.9 1.0 %copy-start.1 = (bf16[528,256]{1,0:T(8,128)(2,1)S(1)}, bf16[528,256]{1,0:T(8,128)(2,1)}, u32[]{:S(2)}) copy-start(bf16[528,256]{1,0:T(8,128)(2,1)} %bundle.1.near_own) | copy-start | bytes 811012
  44.5 2.6 %copy-start.2 = (bf16[128,640]{1,0:T(8,128)(2,1)}, bf16[128,640]{1,0:T(8,128)(2,1)S(1)}, u32[]{:S(2)}) copy-start(bf16[128,640]{1,0:T(8,128)(2,1)S(1)} %get-tuple-element.31.c0) | copy-start | bytes 491524
  44.5 2.5 %collective-permute-start.12 = (bf16[1040,256]{1,0:T(8,128)(2,1)S(1)}, bf16[1040,256]{1,0:T(8,128)(2,1)S(1)}, u32[]{:S(2)}, u32[]{:S(2)}) collective-permute-start(bf16[1040,256]{1,0:T(8,128)(2,1)S(1)} %get-tuple-element.36), channel_id=1, source_target_pairs={{0,1},{1,0},{2,3},{3,2},{4,5},{5,4},{6,7},{7,6},{8,9},{9,8},{10,11... | collective-permute-start | bytes 1597448 | tf_op jit(solution)/shard_map/ppermute | solution.py:250
  47.1 26.3 %collective-permute-start.13 = (bf16[512,256]{1,0:T(8,128)(2,1)S(1)}, bf16[512,256]{1,0:T(8,128)(2,1)S(1)}, u32[]{:S(2)}, u32[]{:S(2)}) collective-permute-start(bf16[512,256]{1,0:T(8,128)(2,1)S(1)} %add_convert_fusion.1), channel_id=1, source_target_pairs={{0,8},{1,9},{2,10},{3,11},{4,12},{5,13},{6,14},{7,15},{8,0},{9,1},... | collective-permute-start | bytes 786440 | tf_op jit(solution)/shard_map/ppermute | solution.py:250
  52.4 3.6 %collective-permute-start.17 = (f32[8,128]{1,0:T(8,128)S(1)}, f32[8,128]{1,0:T(8,128)S(1)}, u32[]{:S(2)}, u32[]{:S(2)}) collective-permute-start(f32[8,128]{1,0:T(8,128)S(1)} %fusion), channel_id=1, source_target_pairs={{0,64},{1,65},{2,66},{3,67},{4,68},{5,69},{6,70},{7,71},{16,80},{1... | collective-permute-start | bytes 12296 | tf_op jit(solution)/shard_map/ppermute | solution.py:346
  56.0 4.8 %collective-permute-start.18 = (f32[8,128]{1,0:T(8,128)S(1)}, f32[8,128]{1,0:T(8,128)S(1)}, u32[]{:S(2)}, u32[]{:S(2)}) collective-permute-start(f32[8,128]{1,0:T(8,128)S(1)} %add.39), channel_id=1, source_target_pairs={{0,192},{1,193},{2,194},{3,195},{4,196},{5,197},{6,198},{7,199},{1... | collective-permute-start | bytes 12296 | tf_op jit(solution)/shard_map/ppermute | solution.py:346
  60.8 4.6 %collective-permute-start.19 = (f32[8,128]{1,0:T(8,128)S(1)}, f32[8,128]{1,0:T(8,128)S(1)}, u32[]{:S(2)}, u32[]{:S(2)}) collective-permute-start(f32[8,128]{1,0:T(8,128)S(1)} %add.40), channel_id=1, source_target_pairs={{0,16},{1,17},{2,18},{3,19},{4,20},{5,21},{6,22},{7,23},{16,0},{17... | collective-permute-start | bytes 12296 | tf_op jit(solution)/shard_map/ppermute | solution.py:346
  65.4 5.1 %collective-permute-start.20 = (f32[8,128]{1,0:T(8,128)S(1)}, f32[8,128]{1,0:T(8,128)S(1)}, u32[]{:S(2)}, u32[]{:S(2)}) collective-permute-start(f32[8,128]{1,0:T(8,128)S(1)} %add.41), channel_id=1, source_target_pairs={{0,56},{1,57},{2,58},{3,59},{4,60},{5,61},{6,62},{7,63},{16,32},{1... | collective-permute-start | bytes 12296 | tf_op jit(solution)/shard_map/ppermute | solution.py:346
  65.9 10.2 %collective-permute-start.9 = (bf16[128,640]{1,0:T(8,128)(2,1)S(1)}, bf16[128,640]{1,0:T(8,128)(2,1)S(1)}, u32[]{:S(2)}, u32[]{:S(2)}) collective-permute-start(bf16[128,640]{1,0:T(8,128)(2,1)S(1)} %get-tuple-element.32), channel_id=1, source_target_pairs={{0,6},{1,7},{2,0},{3,1},{4,2},{5,3},{6,4},{7,5},{8,14},{9,15},{10,... | collective-permute-start | bytes 491528 | tf_op jit(solution)/shard_map/ppermute | solution.py:250
  69.7 10.3 %collective-permute-start.10 = (bf16[128,640]{1,0:T(8,128)(2,1)S(1)}, bf16[128,640]{1,0:T(8,128)(2,1)S(1)}, u32[]{:S(2)}, u32[]{:S(2)}) collective-permute-start(bf16[128,640]{1,0:T(8,128)(2,1)S(1)} %get-tuple-element.33), channel_id=1, source_target_pairs={{0,4},{1,5},{2,6},{3,7},{4,0},{5,1},{6,2},{7,3},{8,12},{9,13},{10,... | collective-permute-start | bytes 491528 | tf_op jit(solution)/shard_map/ppermute | solution.py:250
  70.2 10.7 %collective-permute-start.11 = (bf16[128,640]{1,0:T(8,128)(2,1)S(1)}, bf16[128,640]{1,0:T(8,128)(2,1)S(1)}, u32[]{:S(2)}, u32[]{:S(2)}) collective-permute-start(bf16[128,640]{1,0:T(8,128)(2,1)S(1)} %get-tuple-element.34), channel_id=1, source_target_pairs={{0,2},{1,3},{2,4},{3,5},{4,6},{5,7},{6,0},{7,1},{8,10},{9,11},{10,... | collective-permute-start | bytes 491528 | tf_op jit(solution)/shard_map/ppermute | solution.py:250
  70.5 7.7 %collective-permute-start.21 = (f32[8,128]{1,0:T(8,128)S(1)}, f32[8,128]{1,0:T(8,128)S(1)}, u32[]{:S(2)}, u32[]{:S(2)}) collective-permute-start(f32[8,128]{1,0:T(8,128)S(1)} %add.42), channel_id=1, source_target_pairs={{0,48},{1,49},{2,50},{3,51},{4,52},{5,53},{6,54},{7,55},{16,40},{1... | collective-permute-start | bytes 12296 | tf_op jit(solution)/shard_map/ppermute | solution.py:346
  74.2 14.3 %collective-permute-start.16 = (bf16[128,256]{1,0:T(8,128)(2,1)S(1)}, bf16[128,256]{1,0:T(8,128)(2,1)S(1)}, u32[]{:S(2)}, u32[]{:S(2)}) collective-permute-start(bf16[128,256]{1,0:T(8,128)(2,1)S(1)} %get-tuple-element.42), channel_id=1, source_target_pairs={{0,2},{1,3},{2,4},{3,5},{4,6},{5,7},{6,0},{7,1},{8,10},{9,11},{10,... | collective-permute-start | bytes 196616 | tf_op jit(solution)/shard_map/ppermute | solution.py:250
  76.1 9.4 %copy-start.3 = (bf16[128,640]{1,0:T(8,128)(2,1)}, bf16[128,640]{1,0:T(8,128)(2,1)S(1)}, u32[]{:S(2)}) copy-start(bf16[128,640]{1,0:T(8,128)(2,1)S(1)} %collective-permute-done.9.c1) | copy-start | bytes 491524
  76.1 12.3 %collective-permute-start.15 = (bf16[128,256]{1,0:T(8,128)(2,1)S(1)}, bf16[128,256]{1,0:T(8,128)(2,1)S(1)}, u32[]{:S(2)}, u32[]{:S(2)}) collective-permute-start(bf16[128,256]{1,0:T(8,128)(2,1)S(1)} %get-tuple-element.43), channel_id=1, source_target_pairs={{0,4},{1,5},{2,6},{3,7},{4,0},{5,1},{6,2},{7,3},{8,12},{9,13},{10,... | collective-permute-start | bytes 196616 | tf_op jit(solution)/shard_map/ppermute | solution.py:250
  78.3 10.2 %collective-permute-start.14 = (bf16[128,256]{1,0:T(8,128)(2,1)S(1)}, bf16[128,256]{1,0:T(8,128)(2,1)S(1)}, u32[]{:S(2)}, u32[]{:S(2)}) collective-permute-start(bf16[128,256]{1,0:T(8,128)(2,1)S(1)} %get-tuple-element.44), channel_id=1, source_target_pairs={{0,6},{1,7},{2,0},{3,1},{4,2},{5,3},{6,4},{7,5},{8,14},{9,15},{10,... | collective-permute-start | bytes 196616 | tf_op jit(solution)/shard_map/ppermute | solution.py:250
  79.9 7.7 %copy-start.12 = (f32[8,128]{1,0:T(8,128)}, f32[8,128]{1,0:T(8,128)S(1)}, u32[]{:S(2)}) copy-start(f32[8,128]{1,0:T(8,128)S(1)} %add.43.b0) | copy-start | bytes 12292
  79.9 5.6 %copy-start.4 = (bf16[128,640]{1,0:T(8,128)(2,1)}, bf16[128,640]{1,0:T(8,128)(2,1)S(1)}, u32[]{:S(2)}) copy-start(bf16[128,640]{1,0:T(8,128)(2,1)S(1)} %collective-permute-done.10.c2) | copy-start | bytes 491524
  79.9 4.9 %collective-permute-start.24 = (f32[8,128]{1,0:T(8,128)S(1)}, f32[8,128]{1,0:T(8,128)S(1)}, u32[]{:S(2)}, u32[]{:S(2)}) collective-permute-start(f32[8,128]{1,0:T(8,128)S(1)} %add.43.b0), channel_id=1, source_target_pairs={{0,2},{1,3},{2,4},{3,5},{4,6},{5,7},{6,0},{7,1},{8,10},{9,11},{10,... | collective-permute-start | bytes 12296 | tf_op jit(solution)/shard_map/ppermute | solution.py:250
  80.9 4.6 %copy-start.5 = (bf16[128,640]{1,0:T(8,128)(2,1)}, bf16[128,640]{1,0:T(8,128)(2,1)S(1)}, u32[]{:S(2)}) copy-start(bf16[128,640]{1,0:T(8,128)(2,1)S(1)} %collective-permute-done.11.c3) | copy-start | bytes 491524
  80.9 6.7 %collective-permute-start.23 = (f32[8,128]{1,0:T(8,128)S(1)}, f32[8,128]{1,0:T(8,128)S(1)}, u32[]{:S(2)}, u32[]{:S(2)}) collective-permute-start(f32[8,128]{1,0:T(8,128)S(1)} %add.43.b0), channel_id=1, source_target_pairs={{0,4},{1,5},{2,6},{3,7},{4,0},{5,1},{6,2},{7,3},{8,12},{9,13},{10,... | collective-permute-start | bytes 12296 | tf_op jit(solution)/shard_map/ppermute | solution.py:250
  84.8 2.8 %copy-start.13 = (f32[8,128]{1,0:T(8,128)}, f32[8,128]{1,0:T(8,128)S(1)}, u32[]{:S(2)}) copy-start(f32[8,128]{1,0:T(8,128)S(1)} %collective-permute-done.24.b3) | copy-start | bytes 12292
  84.8 3.6 %collective-permute-start.22 = (f32[8,128]{1,0:T(8,128)S(1)}, f32[8,128]{1,0:T(8,128)S(1)}, u32[]{:S(2)}, u32[]{:S(2)}) collective-permute-start(f32[8,128]{1,0:T(8,128)S(1)} %add.43.b0), channel_id=1, source_target_pairs={{0,6},{1,7},{2,0},{3,1},{4,2},{5,3},{6,4},{7,5},{8,14},{9,15},{10,... | collective-permute-start | bytes 12296 | tf_op jit(solution)/shard_map/ppermute | solution.py:250
  87.6 0.9 copy-start.14
  88.4 0.6 copy-start.15
  88.5 0.6 copy-start.9
  88.5 0.6 copy-start.10
  88.5 0.6 copy-start.11
